TPU v7x, 32 devices: a whole 2x2x4 slice. The times are simulated.
32 devices in a mesh: groups: 2 (over y), expert: 16 (over z, x, core), dp: 1.
Axes of the slice: x: 2, y: 2, z: 4, core: 2. Of those that a mesh axis runs over, the one named last changes fastest.
Arguments:
- output_cotangent: bfloat16 [1024, 2048], P(('groups', 'expert', 'dp')), parts along dimension 0, may hold values from -6 to 6
- route: int32 [1024, 8], P(('groups', 'expert', 'dp')), parts along dimension 0, may hold values from 0 to 15, all different within a row; in each aligned block of 32 rows (0 to 31, 32 to 63, ...) at most 24 rows name the same one
- routing_weights: bfloat16 [1024, 8], P(('groups', 'expert', 'dp')), parts along dimension 0, may hold values from 0.049804688 to 1
- hidden: bfloat16 [32, 1, 16, 24, 768], P(('groups', 'expert'), 'dp'), parts along dimension 0, may hold values from -6 to 6
- down_weight: bfloat16 [16, 768, 2048], P('expert', 'dp'), may hold values from -0.21875 to 0.21875
- first_adapter_factors: bfloat16 [16, 768, 32], P('expert'), may hold values from -0.21875 to 0.21875
- second_adapter_factors: bfloat16 [16, 32, 2048], P('expert'), may hold values from -1 to 1
Outputs:
- hidden_cotangent: bfloat16 [32, 1, 16, 24, 768], P(('groups', 'expert'), 'dp'), parts along dimension 0
- first_factor_gradient: float32 [32, 768, 32], P(('groups', 'expert')), parts along dimension 0
- second_factor_gradient: float32 [32, 32, 2048], P(('groups', 'expert')), parts along dimension 0
- routing_weight_gradient: float32 [1024, 8], P(('groups', 'expert', 'dp')), parts along dimension 0
There are 2 independent parts, one for each index of `groups`. A program takes and returns all parts, laid end to end along the dimension named above; an argument that names none is the same for every part. Nothing has to cross between parts.
Inputs may be any that keep to these rules, and one draw needn't show every extreme that they name: `route`: each row names 8 different experts. In the 32 rows of one device no expert is named by more than 24 rows, a bound that some block reaches of them.
All inputs are finite; a program needn't handle non-finite values.
Results may differ from a plain program's by a relative error of at most 0.0056.
Values may be sent and summed in bfloat16 or wider, within the bound.
No kernel may reach another device: no remote copies, remote signals or barrier semaphores. Data moves between devices by JAX's collectives and lax.ppermute only.
A program may use at most 64 MiB of HBM per device.

v0:
```python
import jax
import jax.numpy as jnp
from jax import lax
from jax.sharding import PartitionSpec as P

adapter_scale = 2.0


def slot_positions(route, expert_total):
    expert_ids = lax.broadcasted_iota(jnp.int32, (1, 1, expert_total), 2)
    expert_hits = jnp.sum((route[:, :, None] == expert_ids).astype(jnp.int32), axis=1)
    earlier = jnp.cumsum(expert_hits, axis=0) - expert_hits
    return jnp.take_along_axis(earlier, route, axis=1)


def local(
    output_cotangent,
    route,
    routing_weights,
    hidden,
    down_weight,
    first_adapter_factors,
    second_adapter_factors,
):
    resident, pair_one, sources, capacity, hidden_width = hidden.shape
    expert_count = lax.axis_size("expert")
    expert_total = resident * expert_count
    model_width = output_cotangent.shape[1]
    position = slot_positions(route, expert_total)
    target = route * capacity + position
    slot_cells = lax.broadcasted_iota(jnp.int32, (expert_total * capacity, 1, 1), 0)
    matches = slot_cells == target[None, :, :]
    picker = jnp.any(matches, axis=2).astype(jnp.bfloat16)
    send_rows = jnp.dot(picker, output_cotangent, preferred_element_type=jnp.float32).astype(
        jnp.bfloat16
    )
    send_rows = send_rows.reshape(expert_total, capacity, model_width)
    send_weight = jnp.sum(
        jnp.where(matches, routing_weights[None, :, :].astype(jnp.float32), 0.0), axis=(1, 2)
    )
    send_weight = send_weight.astype(jnp.bfloat16).reshape(expert_total, capacity)
    recv_rows, recv_weight = (
        lax.all_to_all(send_rows, "expert", split_axis=0, concat_axis=0, tiled=True),
        lax.all_to_all(send_weight, "expert", split_axis=0, concat_axis=0, tiled=True),
    )
    grad_rows = recv_rows.reshape(sources, resident, capacity, model_width)
    scales = recv_weight.reshape(sources, resident, capacity)
    hidden_inputs = hidden.reshape(resident, sources, capacity, hidden_width)
    reduced_rank_product = jnp.einsum(
        "bwlv,bvs->bwls", hidden_inputs, first_adapter_factors, preferred_element_type=jnp.float32
    ).astype(jnp.bfloat16)
    adapter_result = jnp.einsum(
        "nvli,nit->vnlt",
        reduced_rank_product,
        second_adapter_factors,
        preferred_element_type=jnp.float32,
    )
    fixed_output = jnp.einsum(
        "ejcf,efd->jecd",
        hidden_inputs,
        lax.all_gather(down_weight, "dp", axis=1, tiled=True),
        preferred_element_type=jnp.float32,
    )
    output_values = fixed_output + adapter_scale * adapter_result
    slot_grad = jnp.sum(grad_rows.astype(jnp.float32) * output_values, axis=3)
    scaled_result = (scales[..., None].astype(jnp.float32) * grad_rows.astype(jnp.float32)).astype(
        jnp.bfloat16
    )
    projected_down = jnp.einsum(
        "mzxl,zil->mzxi", scaled_result, second_adapter_factors, preferred_element_type=jnp.float32
    ).astype(jnp.bfloat16)
    fixed_backward = jnp.einsum(
        "jecd,efd->ejcf",
        scaled_result,
        lax.all_gather(down_weight, "dp", axis=1, tiled=True),
        preferred_element_type=jnp.float32,
    )
    activation_cotangent = fixed_backward + adapter_scale * jnp.einsum(
        "mwsa,wqa->wmsq", projected_down, first_adapter_factors, preferred_element_type=jnp.float32
    )
    hidden_cotangent = activation_cotangent.astype(jnp.bfloat16).reshape(hidden.shape)
    first_share = adapter_scale * jnp.einsum(
        "ejcf,jecr->efr", hidden_inputs, projected_down, preferred_element_type=jnp.float32
    )
    second_share = adapter_scale * jnp.einsum(
        "ejcr,jecd->erd", reduced_rank_product, scaled_result, preferred_element_type=jnp.float32
    )
    first_factor_gradient, second_factor_gradient = lax.psum((first_share, second_share), "dp")
    returned_grads = lax.all_to_all(slot_grad, "expert", split_axis=0, concat_axis=0, tiled=True)
    returned_flat = returned_grads.reshape(expert_total * capacity)
    routing_weight_gradient = jnp.sum(jnp.where(matches, returned_flat[:, None, None], 0.0), axis=0)
    return (
        hidden_cotangent,
        first_factor_gradient,
        second_factor_gradient,
        routing_weight_gradient,
    )


def solution(mesh):
    in_specs = (
        P(("groups", "expert", "dp"), None),
        P(("groups", "expert", "dp"), None),
        P(("groups", "expert", "dp"), None),
        P(("groups", "expert"), "dp", None, None, None),
        P("expert", "dp", None),
        P("expert", None, None),
        P("expert", None, None),
    )
    out_specs = (
        P(("groups", "expert"), "dp", None, None, None),
        P(("groups", "expert"), None, None),
        P(("groups", "expert"), None, None),
        P(("groups", "expert", "dp"), None),
    )
    return jax.shard_map(local, mesh=mesh, in_specs=in_specs, out_specs=out_specs, check_vma=False)
```

profile of v0, /device:TPU:0, one launch (start us, length us, event | category | flops | bytes accessed | tf_op | source)
XLA Modules:
  0.0 88.0 jit_solution(18030818407046685234)
XLA Ops:
  0.6 0.0 copy-start
  0.6 0.9 convert_reduce_fusion
  1.5 0.8 bitcast_or_fusion
  2.3 0.1 copy.42
  2.4 0.1 reduce_window_sum.11
  2.4 0.1 copy.44
  2.5 0.1 reshape.120
  2.6 0.0 copy-start.4
  2.6 0.0 copy-start.3
  2.6 1.9 %gather_fusion = s32[256]{0:T(256)S(1)} fusion(s32[32,16]{1,0:T(8,128)S(1)} %sub.3, s32[256]{0:T(256)S(1)} %reshape.120), kind=kCustom, calls=%fused_computation | custom fusion | bytes 4096 | tf_op jit(solution)/shard_map/jit(take_along_axis)/gather | solution.py:13
  4.6 0.0 copy-start.1
  4.6 0.1 reshape.123
  4.7 0.1 copy.45
  4.7 0.0 copy-done.4
  4.7 0.1 copy.46
  4.8 0.2 fusion.24
  5.0 0.0 copy-done.3
  5.0 1.8 %convolution_convert_fusion = bf16[384,2048]{1,0:T(8,128)(2,1)} fusion(pred[384,32]{0,1:T(8,128)(4,1)S(1)} %fusion.24, bf16[32,2048]{1,0:T(8,128)(2,1)S(1)} %copy-done.3), kind=kOutput, calls=%fused_computation.11 | convolution fusion | flops 51118080 | bytes 1716224 | tf_op jit(solution)/shard_map/dot_general | solution.py:34
  6.8 7.4 %all-to-all-start.1 = ((bf16[16,24,2048]{2,1,0:T(8,128)(2,1)}), bf16[16,24,2048]{2,1,0:T(8,128)(2,1)}, u32[]{:S(2)}, u32[]{:S(2)}) async-start(bf16[16,24,2048]{2,1,0:T(8,128)(2,1)} %bitcast.72), calls=%async_computation.1 | async-start | bytes 3145728 | tf_op jit(solution)/shard_map/all_to_all | solution.py:43
  14.3 0.0 copy-done.1
  14.3 1.4 %convolution_convert_fusion.1 = bf16[16,24,32]{2,1,0:T(8,128)(2,1)S(1)} fusion(bf16[1,1,16,24,768]{4,3,2,1,0:T(8,128)(2,1)} %param.10, bf16[1,768,32]{1,2,0:T(8,128)(2,1)S(1)} %copy-done.1), kind=kOutput, calls=%fused_computation.21 | convolution fusion | flops 18886656 | bytes 663552 | tf_op jit(solution)/shard_map/bwlv,bvs->bwls/dot_general | solution.py:49
  15.6 0.0 copy-done
  15.6 0.0 copy-start.2
  15.6 4.2 %fusion.3 = f32[2048,16,24]{0,2,1:T(8,128)} fusion(bf16[1,768,2048]{2,1,0:T(8,128)(2,1)S(1)} %copy-done, bf16[1,1,16,24,768]{4,3,2,1,0:T(8,128)(2,1)} %param.10), kind=kOutput, calls=%fused_computation.7 | convolution fusion | flops 1207959552 | bytes 6881280 | tf_op jit(solution)/shard_map/ejcf,efd->jecd/dot_general | solution.py:58
  19.8 0.0 copy-start.5
  19.8 26.5 %all-to-all-done.1 = bf16[16,24,2048]{2,1,0:T(8,128)(2,1)} async-done(((bf16[16,24,2048]{2,1,0:T(8,128)(2,1)}), bf16[16,24,2048]{2,1,0:T(8,128)(2,1)}, u32[]{:S(2)}, u32[]{:S(2)}) %all-to-all-start.1) | async-done | bytes 1572896 | tf_op jit(solution)/shard_map/all_to_all | solution.py:43
  46.3 0.0 copy-done.2
  46.3 3.7 %fusion.2 = f32[16,24]{1,0:T(8,128)} fusion(bf16[16,24,2048]{2,1,0:T(8,128)(2,1)} %all-to-all-done.1, f32[2048,16,24]{0,2,1:T(8,128)} %fusion.3, bf16[16,24,32]{2,1,0:T(8,128)(2,1)S(1)} %convolution_convert_fusion.1, bf16[1,32,2048]{2,1,0:T(8,128)(2,1)S(1)} %copy-done.2), kind=kOutput, calls=%fused_computation.5 | convolution fusion | flops 54263424 | bytes 4875776 | tf_op jit(solution)/shard_map/nvli,nit->vnlt/dot_general | solution.py:52
  50.0 9.1 %all-to-all-start.2 = ((f32[16,1,24]{2,1,0:T(1,128)}), f32[16,1,24]{2,1,0:T(1,128)S(1)}, u32[]{:S(2)}, u32[]{:S(2)}) async-start(f32[16,1,24]{2,1,0:T(1,128)} %bitcast.20), calls=%async_computation.2 | async-start | bytes 16384 | tf_op jit(solution)/shard_map/all_to_all | solution.py:89
  59.1 0.0 copy-done.5
  59.1 0.1 copy.47
  59.2 6.2 %all-to-all-done.2 = f32[16,1,24]{2,1,0:T(1,128)S(1)} async-done(((f32[16,1,24]{2,1,0:T(1,128)}), f32[16,1,24]{2,1,0:T(1,128)S(1)}, u32[]{:S(2)}, u32[]{:S(2)}) %all-to-all-start.2) | async-done | bytes 1568 | tf_op jit(solution)/shard_map/all_to_all | solution.py:89
  65.4 0.5 broadcast.43
  65.9 0.7 reduce.4
  66.6 0.1 broadcast_in_dim.34
  66.7 0.2 select_reduce_fusion
  66.9 0.7 convert_element_type.75
  67.6 3.5 %all-to-all-start = ((bf16[16,1,24]{2,1,0:T(2,128)(2,1)}), bf16[16,1,24]{2,1,0:T(2,128)(2,1)S(1)}, u32[]{:S(2)}, u32[]{:S(2)}) async-start(bf16[16,1,24]{2,1,0:T(2,128)(2,1)} %convert_element_type.75), calls=%async_computation | async-start | bytes 16384 | tf_op jit(solution)/shard_map/all_to_all | solution.py:44
  71.1 0.7 copy.49
  71.7 5.6 %all-to-all-done = bf16[16,1,24]{2,1,0:T(2,128)(2,1)S(1)} async-done(((bf16[16,1,24]{2,1,0:T(2,128)(2,1)}), bf16[16,1,24]{2,1,0:T(2,128)(2,1)S(1)}, u32[]{:S(2)}, u32[]{:S(2)}) %all-to-all-start) | async-done | bytes 800 | tf_op jit(solution)/shard_map/all_to_all | solution.py:44
  77.4 2.0 %fusion.16 = bf16[16,24,32]{2,1,0:T(8,128)(2,1)S(1)} fusion(bf16[16,24,2048]{2,1,0:T(8,128)(2,1)} %all-to-all-done.1, f32[16,24]{1,0:T(8,128)S(1)} %bitcast.73, bf16[1,32,2048]{2,1,0:T(8,128)(2,1)S(1)} %copy-done.2), kind=kOutput, calls=%fused_computation.20 | convolution fusion | flops 52703232 | bytes 1730048 | tf_op jit(solution)/shard_map/mzxl,zil->mzxi/dot_general | solution.py:69
  79.4 1.9 %fusion.20 = f32[1,768,32]{1,2,0:T(8,128)} fusion(bf16[16,24,32]{2,1,0:T(8,128)(2,1)S(1)} %fusion.16, bf16[1,1,16,24,768]{4,3,2,1,0:T(8,128)(2,1)} %param.10), kind=kOutput, calls=%fused_computation.24 | convolution fusion | flops 18898944 | bytes 712704 | tf_op jit(solution)/shard_map/ejcf,jecr->efr/dot_general | solution.py:82
  81.4 2.9 %fusion.5 = f32[16,24,768]{2,1,0:T(8,128)S(1)} fusion(bf16[1,768,2048]{2,1,0:T(8,128)(2,1)S(1)} %copy-done, bf16[16,24,2048]{2,1,0:T(8,128)(2,1)} %all-to-all-done.1, f32[16,24]{1,0:T(8,128)S(1)} %bitcast.74), kind=kOutput, calls=%fused_computation.9 | convolution fusion | flops 1210318848 | bytes 5899776 | tf_op jit(solution)/shard_map/jecd,efd->ejcf/dot_general | solution.py:72
  84.2 1.1 %fusion.11 = bf16[1,1,16,24,768]{4,3,2,1,0:T(8,128)(2,1)} fusion(f32[16,24,768]{2,1,0:T(8,128)S(1)} %fusion.5, bf16[16,24,32]{2,1,0:T(8,128)(2,1)S(1)} %fusion.16, bf16[1,768,32]{1,2,0:T(8,128)(2,1)S(1)} %copy-done.1), kind=kOutput, calls=%fused_computation.18 | convolution fusion | flops 19759104 | bytes 1843200 | tf_op jit(solution)/shard_map/mwsa,wqa->wmsq/dot_general | solution.py:78
  85.3 2.6 %fusion.8 = f32[1,32,2048]{2,1,0:T(8,128)} fusion(bf16[16,24,32]{2,1,0:T(8,128)(2,1)S(1)} %convolution_convert_fusion.1, bf16[16,24,2048]{2,1,0:T(8,128)(2,1)} %all-to-all-done.1, f32[16,24]{1,0:T(8,128)S(1)} %bitcast.75), kind=kOutput, calls=%fused_computation.14 | convolution fusion | flops 52756480 | bytes 1861120 | tf_op jit(solution)/shard_map/ejcr,jecd->erd/dot_general | solution.py:85
  (3 shorter events, 0.0 us)
Async XLA Ops:
  0.6 15.0 %copy-start = (bf16[1,768,2048]{2,1,0:T(8,128)(2,1)S(1)}, bf16[1,768,2048]{2,1,0:T(8,128)(2,1)}, u32[]{:S(2)}) copy-start(bf16[1,768,2048]{2,1,0:T(8,128)(2,1)} %param.11) | copy-start | bytes 9437188
  2.6 2.1 %copy-start.4 = (s32[32,8]{0,1:T(8,128)S(1)}, s32[32,8]{0,1:T(8,128)}, u32[]{:S(2)}) copy-start(s32[32,8]{0,1:T(8,128)} %param.8) | copy-start | bytes 3076
  2.6 2.4 %copy-start.3 = (bf16[32,2048]{1,0:T(8,128)(2,1)S(1)}, bf16[32,2048]{1,0:T(8,128)(2,1)}, u32[]{:S(2)}) copy-start(bf16[32,2048]{1,0:T(8,128)(2,1)} %param.7) | copy-start | bytes 393220
  4.6 9.7 %copy-start.1 = (bf16[1,768,32]{1,2,0:T(8,128)(2,1)S(1)}, bf16[1,768,32]{1,2,0:T(8,128)(2,1)}, u32[]{:S(2)}) copy-start(bf16[1,768,32]{1,2,0:T(8,128)(2,1)} %param.12) | copy-start | bytes 147460
  6.8 39.4 %all-to-all-start.1 = ((bf16[16,24,2048]{2,1,0:T(8,128)(2,1)}), bf16[16,24,2048]{2,1,0:T(8,128)(2,1)}, u32[]{:S(2)}, u32[]{:S(2)}) async-start(bf16[16,24,2048]{2,1,0:T(8,128)(2,1)} %bitcast.72), calls=%async_computation.1 | async-start | bytes 3145728 | tf_op jit(solution)/shard_map/all_to_all | solution.py:43
  15.6 30.7 %copy-start.2 = (bf16[1,32,2048]{2,1,0:T(8,128)(2,1)S(1)}, bf16[1,32,2048]{2,1,0:T(8,128)(2,1)}, u32[]{:S(2)}) copy-start(bf16[1,32,2048]{2,1,0:T(8,128)(2,1)} %param.13) | copy-start | bytes 393220
  19.8 39.3 %copy-start.5 = (bf16[32,8]{0,1:T(8,128)(2,1)S(1)}, bf16[32,8]{0,1:T(8,128)(2,1)}, u32[]{:S(2)}) copy-start(bf16[32,8]{0,1:T(8,128)(2,1)} %param.9) | copy-start | bytes 1540
  50.0 15.4 %all-to-all-start.2 = ((f32[16,1,24]{2,1,0:T(1,128)}), f32[16,1,24]{2,1,0:T(1,128)S(1)}, u32[]{:S(2)}, u32[]{:S(2)}) async-start(f32[16,1,24]{2,1,0:T(1,128)} %bitcast.20), calls=%async_computation.2 | async-start | bytes 16384 | tf_op jit(solution)/shard_map/all_to_all | solution.py:89
  67.6 9.8 %all-to-all-start = ((bf16[16,1,24]{2,1,0:T(2,128)(2,1)}), bf16[16,1,24]{2,1,0:T(2,128)(2,1)S(1)}, u32[]{:S(2)}, u32[]{:S(2)}) async-start(bf16[16,1,24]{2,1,0:T(2,128)(2,1)} %convert_element_type.75), calls=%async_computation | async-start | bytes 16384 | tf_op jit(solution)/shard_map/all_to_all | solution.py:44
where the time goes:
time: 88.5 us; the launch traced here: 88 us
  waiting for transfers between devices  38.3 us (43%)
  matrix products  21.6 us (24%)
  starting transfers between devices  20 us (23%)
  local copies, waits for them, and re-layouts  4.49 us (5%)
  other arithmetic  2.79 us (3%)
    all_to_all x1, waiting for transfers between devices, local(): lax.all_to_all(send_rows, 'expert', split_axis=0, concat_axis=0, tiled=True)  26.5 us
    all_to_all x1, starting transfers between devices, local(): lax.all_to_all(slot_grad, 'expert', split_axis=0, concat_axis=0, tiled=True)  9.11 us
    all_to_all x1, starting transfers between devices, local(): lax.all_to_all(send_rows, 'expert', split_axis=0, concat_axis=0, tiled=True)  7.4 us
    all_to_all x1, waiting for transfers between devices, local(): lax.all_to_all(slot_grad, 'expert', split_axis=0, concat_axis=0, tiled=True)  6.24 us
    all_to_all x1, waiting for transfers between devices, local(): lax.all_to_all(send_weight, 'expert', split_axis=0, concat_axis=0, tiled=...  5.63 us
    dot_general x1, matrix products, local(): jnp.einsum('ejcf,efd->jecd', hidden_inputs, lax.all_gather(down_weight, '...  4.17 us
    dot_general x1, matrix products, local(): jnp.einsum('nvli,nit->vnlt', reduced_rank_product, second_adapter_factors...  3.68 us
    all_to_all x1, starting transfers between devices, local(): lax.all_to_all(send_weight, 'expert', split_axis=0, concat_axis=0, tiled=...  3.47 us
  transfers between devices with their start and end apart: 3, of which 3 were waited for; matrix products, arithmetic and copies ran while one was open for 7% of the time, Pallas kernels for 0%

commit v1 on v0

--- a/solution.py
+++ b/solution.py
@@ -1,9 +1,15 @@
+import functools
+
 import jax
 import jax.numpy as jnp
 from jax import lax
+from jax.experimental import pallas as pl
+from jax.experimental.pallas import tpu as pltpu
 from jax.sharding import PartitionSpec as P
 
 adapter_scale = 2.0
+lanes = 128
+mebibyte = 1 << 20
 
 
 def slot_positions(route, expert_total):
@@ -13,7 +19,7 @@
     return jnp.take_along_axis(earlier, route, axis=1)
 
 
-def local(
+def dispatched(
     output_cotangent,
     route,
     routing_weights,
@@ -97,6 +103,225 @@
     )
 
 
+def forward_kernel(hidden_ref, down_ref, first_ref, second_ref, low_ref, out_ref):
+    hidden = hidden_ref[...]
+    low = lax.dot_general(
+        hidden, first_ref[...], (((1,), (1,)), ((), ())), preferred_element_type=jnp.float32
+    ).astype(jnp.bfloat16)
+    low_ref[...] = low
+    width = out_ref.shape[1]
+    step = min(width, 512)
+    for start in range(0, width, step):
+        cols = slice(start, start + step)
+        out_ref[:, cols] = jnp.dot(
+            hidden, down_ref[:, cols], preferred_element_type=jnp.float32
+        ) + adapter_scale * jnp.dot(low, second_ref[:, cols], preferred_element_type=jnp.float32)
+
+
+def combine_kernel(count, tokens, capacity, me_ref, *refs):
+    blocks, (out_ref, scaled_ref, pair_ref, rows_ref, sems) = refs[:count], refs[count:]
+    width = out_ref.shape[1]
+    slots = count * capacity
+    copies = [
+        pltpu.make_async_copy(
+            blocks[s], rows_ref.at[pl.ds(tokens * s, tokens), :], sems.at[s]
+        )
+        for s in range(count)
+    ]
+    for copy in copies:
+        copy.start()
+    for copy in copies:
+        copy.wait()
+    me = me_ref[0]
+    hits, weights = [], []
+    for s in range(count):
+        meta = rows_ref[tokens * s : tokens * s + 16, width : width + lanes].astype(jnp.float32)
+        match = meta[0:8] == me.astype(jnp.float32)
+        hits.append(jnp.sum(jnp.where(match, 1.0, 0.0), axis=0, keepdims=True))
+        weights.append(jnp.sum(jnp.where(match, meta[8:16], 0.0), axis=0, keepdims=True))
+    hit = jnp.concatenate(hits, axis=0)
+    weight = jnp.concatenate(weights, axis=0)
+    before = (
+        lax.broadcasted_iota(jnp.int32, (lanes, lanes), 0)
+        < lax.broadcasted_iota(jnp.int32, (lanes, lanes), 1)
+    )
+    earlier = jnp.dot(
+        hit.astype(jnp.bfloat16),
+        jnp.where(before, 1.0, 0.0).astype(jnp.bfloat16),
+        preferred_element_type=jnp.float32,
+    )
+    source = jnp.bitwise_xor(lax.broadcasted_iota(jnp.int32, (count, lanes), 0), me)
+    target = jnp.where(hit > 0.0, (source * capacity).astype(jnp.float32) + earlier, -1.0)
+    per = lanes // tokens
+    lane = lax.broadcasted_iota(jnp.int32, (1, lanes), 1)
+    slot = lax.broadcasted_iota(jnp.int32, (slots, lanes), 0).astype(jnp.float32)
+
+    def merged(rows, q):
+        row = rows[per * q : per * q + 1]
+        for r in range(1, per):
+            shifted = pltpu.roll(rows[per * q + r : per * q + r + 1], tokens * r, 1)
+            row = jnp.where(lane >= tokens * r, shifted, row)
+        return row
+
+    picks, column = [], jnp.zeros((slots, 1), jnp.float32)
+    for q in range(count // per):
+        pick = jnp.where(slot == merged(target, q), 1.0, 0.0)
+        column = column + jnp.sum(pick * merged(weight, q), axis=1, keepdims=True)
+        picks.append(pick)
+    picker = jnp.concatenate([pick.astype(jnp.bfloat16) for pick in picks], axis=1)
+    grads = jnp.zeros((slots, 1), jnp.float32)
+    step = min(width, 512)
+    for start in range(0, width, step):
+        cols = slice(start, start + step)
+        rows = jnp.dot(picker, rows_ref[:, cols], preferred_element_type=jnp.float32)
+        grads = grads + jnp.sum(rows * out_ref[:, cols], axis=1, keepdims=True)
+        scaled_ref[:, cols] = (rows * column).astype(jnp.bfloat16)
+    for q in range(count // per):
+        row = jnp.sum(picks[q] * grads, axis=0, keepdims=True)
+        for r in range(per):
+            s = per * q + r
+            pair_ref[s : s + 1, :] = row if r == 0 else pltpu.roll(row, lanes - tokens * r, 1)
+
+
+def backward_kernel(
+    scaled_ref, hidden_ref, low_ref, down_ref, first_ref, second_ref, cot_ref, dfirst_ref, dsecond_ref
+):
+    scaled = scaled_ref[...]
+    over_last = (((1,), (1,)), ((), ()))
+    over_first = (((0,), (0,)), ((), ()))
+    lowered = lax.dot_general(
+        scaled, second_ref[...], over_last, preferred_element_type=jnp.float32
+    ).astype(jnp.bfloat16)
+    fixed = lax.dot_general(scaled, down_ref[...], over_last, preferred_element_type=jnp.float32)
+    adapter = jnp.dot(lowered, first_ref[...], preferred_element_type=jnp.float32)
+    cot_ref[...] = (fixed + adapter_scale * adapter).astype(jnp.bfloat16)
+    dfirst_ref[...] = adapter_scale * lax.dot_general(
+        lowered, hidden_ref[...], over_first, preferred_element_type=jnp.float32
+    )
+    dsecond_ref[...] = adapter_scale * lax.dot_general(
+        low_ref[...], scaled, over_first, preferred_element_type=jnp.float32
+    )
+
+
+vmem = pl.BlockSpec(memory_space=pltpu.VMEM)
+anywhere = pl.BlockSpec(memory_space=pl.ANY)
+
+
+def gathered(
+    output_cotangent,
+    route,
+    routing_weights,
+    hidden,
+    down_weight,
+    first_adapter_factors,
+    second_adapter_factors,
+):
+    _, _, sources, capacity, hidden_width = hidden.shape
+    tokens, width = output_cotangent.shape
+    rank = first_adapter_factors.shape[2]
+    count = lax.axis_size("expert")
+    slots = sources * capacity
+    me = lax.axis_index("expert").astype(jnp.int32)
+
+    def swap(array, distance):
+        return lax.ppermute(array, "expert", [(i, i ^ distance) for i in range(count)])
+
+    route_rows = route.T
+    meta = jnp.concatenate([route_rows.astype(jnp.bfloat16), routing_weights.T], axis=0)
+    meta = jnp.pad(
+        meta, ((0, tokens - meta.shape[0]), (0, lanes - tokens)), constant_values=-1.0
+    )
+    payload = jnp.concatenate([output_cotangent, meta], axis=1)
+
+    hidden_rows = hidden.reshape(slots, hidden_width)
+    down = down_weight[0]
+    first = first_adapter_factors[0].T
+    second = second_adapter_factors[0]
+    low, out = pl.pallas_call(
+        forward_kernel,
+        out_shape=(
+            jax.ShapeDtypeStruct((slots, rank), jnp.bfloat16),
+            jax.ShapeDtypeStruct((slots, width), jnp.float32),
+        ),
+        in_specs=[vmem] * 4,
+        out_specs=(vmem, vmem),
+        compiler_params=pltpu.CompilerParams(vmem_limit_bytes=32 * mebibyte),
+        name="forward",
+    )(hidden_rows, down, first, second)
+
+    blocks = {0: payload}
+    far = [d for d in range(4, count, 4)]
+    for d in far:
+        blocks[d] = swap(payload, d)
+    for d in [0] + far:
+        blocks[d + 2] = swap(blocks[d], 2)
+    for d in [0] + far:
+        blocks[d + 1] = swap(blocks[d], 1)
+        blocks[d + 3] = swap(blocks[d + 2], 1)
+
+    scaled, pair = pl.pallas_call(
+        functools.partial(combine_kernel, count, tokens, capacity),
+        out_shape=(
+            jax.ShapeDtypeStruct((slots, width), jnp.bfloat16),
+            jax.ShapeDtypeStruct((count, lanes), jnp.float32),
+        ),
+        in_specs=[pl.BlockSpec(memory_space=pltpu.SMEM)] + [anywhere] * count + [vmem],
+        out_specs=(vmem, vmem),
+        scratch_shapes=[
+            pltpu.VMEM((count * tokens, width + lanes), jnp.bfloat16),
+            pltpu.SemaphoreType.DMA((count,)),
+        ],
+        compiler_params=pltpu.CompilerParams(vmem_limit_bytes=32 * mebibyte),
+        name="combine",
+    )(me.reshape(1), *[blocks[s] for s in range(count)], out)
+
+    cotangent, dfirst, dsecond = pl.pallas_call(
+        backward_kernel,
+        out_shape=(
+            jax.ShapeDtypeStruct((slots, hidden_width), jnp.bfloat16),
+            jax.ShapeDtypeStruct((rank, hidden_width), jnp.float32),
+            jax.ShapeDtypeStruct((rank, width), jnp.float32),
+        ),
+        in_specs=[vmem] * 6,
+        out_specs=(vmem,) * 3,
+        compiler_params=pltpu.CompilerParams(vmem_limit_bytes=32 * mebibyte),
+        name="backward",
+    )(scaled, hidden_rows, low, down, first, second)
+
+    distance = lax.broadcasted_iota(jnp.int32, pair.shape, 0)
+    bit = 1
+    while bit < count:
+        pair = jnp.where(jnp.bitwise_and(distance, bit) > 0, swap(pair, bit), pair)
+        bit *= 2
+    wanted = jnp.bitwise_xor(route_rows, me)[None]
+    hop = lax.broadcasted_iota(jnp.int32, (count, 1, 1), 0)
+    gradient = jnp.sum(jnp.where(wanted == hop, pair[:, None, :tokens], 0.0), axis=0).T
+    return (
+        cotangent.reshape(hidden.shape),
+        dfirst.T[None],
+        dsecond[None],
+        gradient,
+    )
+
+
+def local(output_cotangent, route, routing_weights, hidden, *parameters):
+    resident, pairs, sources, capacity, _ = hidden.shape
+    count = lax.axis_size("expert")
+    tokens, top = route.shape
+    gather = (
+        pairs * lax.axis_size("dp") == 1
+        and resident == 1
+        and count & (count - 1) == 0
+        and 4 <= count <= 256
+        and lanes % tokens == 0
+        and count % (lanes // tokens) == 0
+        and top == 8
+        and 16 <= tokens <= 2 * capacity
+    )
+    form = gathered if gather else dispatched
+    return form(output_cotangent, route, routing_weights, hidden, *parameters)
+
+
 def solution(mesh):
     in_specs = (
         P(("groups", "expert", "dp"), None),

time: 88.5 us -> 57.1 us (0.65)
  matrix products: 21.6 us -> 0 us
  waiting for transfers between devices: 38.3 us -> 18.5 us
  Pallas kernels: 0 us -> 10.8 us
  starting transfers between devices: 20 us -> 18.7 us
    all_to_all x3 -> x0, waiting for transfers between devices: 38.3 us -> none  [the longest x1 26.5 us: local(): lax.all_to_all(send_rows, 'expert', split_axis=0, concat_axis=0, tiled=True)]
    dot_general x9 -> x0, matrix products: 21.6 us -> none  [the longest x1 4.17 us: local(): jnp.einsum('ejcf,efd->jecd', hidden_inputs, lax.all_gather(down_weight, '...]
    all_to_all x3 -> x0, starting transfers between devices: 20 us -> none  [the longest x1 9.11 us: local(): lax.all_to_all(slot_grad, 'expert', split_axis=0, concat_axis=0, tiled=True)]
    ppermute x0 -> x19, starting transfers between devices: none -> 18.7 us  [swap(): lax.ppermute(array, 'expert', [(i, i ^ distance) for i in range(count)])]
    ppermute x0 -> x19, waiting for transfers between devices: none -> 18.5 us  [swap(): lax.ppermute(array, 'expert', [(i, i ^ distance) for i in range(count)])]
    pallas_call x0 -> x3, Pallas kernels: none -> 10.8 us  [the longest x1 4.72 us: gathered(): pl.pallas_call(functools.partial(combine_kernel, count, tokens, capacity)...]
    unnamed x13 -> x14, local copies, waits for them, and re-layouts: 0.7 us -> 4.67 us
    gather x5 -> x0, local copies, waits for them, and re-layouts: 2.26 us -> none  [slot_positions(): return jnp.take_along_axis(earlier, route, axis=1)]
  transfers between devices with their start and end apart: 3 -> 19, of which waited for: 3 -> 7; matrix products, arithmetic and copies ran while one was open for 7% -> 0% of each run, Pallas kernels for 0% -> 11%
where the time goes in v1:
time: 57.1 us; the launch traced here: 56.7 us
  starting transfers between devices  18.7 us (33%)
  waiting for transfers between devices  18.5 us (32%)
  Pallas kernels  10.8 us (19%)
  local copies, waits for them, and re-layouts  4.67 us (8%)
  other arithmetic  3.3 us (6%)
  between operations  0.76 us (1%)
    ppermute x19, starting transfers between devices, swap(): lax.ppermute(array, 'expert', [(i, i ^ distance) for i in range(count)])  18.7 us
    ppermute x19, waiting for transfers between devices, swap(): lax.ppermute(array, 'expert', [(i, i ^ distance) for i in range(count)])  18.5 us
    pallas_call x1, Pallas kernels, gathered(): pl.pallas_call(functools.partial(combine_kernel, count, tokens, capacity)...  4.72 us
    unnamed x14, local copies, waits for them, and re-layouts  4.67 us
    pallas_call x1, Pallas kernels, gathered(): pl.pallas_call(backward_kernel, out_shape=(jax.ShapeDtypeStruct((slots, h...  3.8 us
    pallas_call x1, Pallas kernels, gathered(): pl.pallas_call(forward_kernel, out_shape=(jax.ShapeDtypeStruct((slots, ra...  2.28 us
  transfers between devices with their start and end apart: 19, of which 7 were waited for; matrix products, arithmetic and copies ran while one was open for 0% of the time, Pallas kernels for 11%

profile of v1, /device:TPU:0, one launch (start us, length us, event | category | flops | bytes accessed | tf_op | source)
XLA Modules:
  0.0 56.7 jit_solution(346935880162411473)
XLA Ops:
  0.6 0.8 %xor_bitcast_fusion = (s32[8,32]{1,0:T(8,128)S(1)}, bf16[8,32]{1,0:T(8,128)(2,1)S(1)}) fusion(s32[32,8]{0,1:T(8,128)} %param.8, s32[]{:T(128)} %axis_index.12), kind=kLoop, calls=%fused_computation.12 | loop fusion | flops 512 | bytes 2564 | tf_op jit(solution)/shard_map/xor | solution.py:296
  1.4 0.7 %fusion.5 = bf16[32,128]{1,0:T(8,128)(2,1)S(1)} fusion(bf16[8,32]{1,0:T(8,128)(2,1)} %bitcast.27, bf16[8,32]{1,0:T(8,128)(2,1)S(1)} %get-tuple-element.19), kind=kLoop, calls=%fused_computation.10 | loop fusion | flops 45056 | bytes 9216 | tf_op jit(solution)/shard_map/concatenate | solution.py:230
  2.1 0.9 %pad_maximum_fusion.refs_0_ = bf16[32,2176]{1,0:T(8,128)(2,1)S(1)} fusion(bf16[32,128]{1,0:T(8,128)(2,1)S(1)} %fusion.5, bf16[32,2048]{1,0:T(8,128)(2,1)} %param.7), kind=kLoop, calls=%fused_computation | loop fusion | flops 278528 | bytes 278528 | tf_op jit(solution)/shard_map/concatenate | solution.py:234
  3.0 4.1 %collective-permute-start.7 = (bf16[32,2176]{1,0:T(8,128)(2,1)S(1)}, bf16[32,2176]{1,0:T(8,128)(2,1)S(1)}, u32[]{:S(2)}, u32[]{:S(2)}) collective-permute-start(bf16[32,2176]{1,0:T(8,128)(2,1)S(1)} %pad_maximum_fusion.refs_0_), channel_id=1, source_target_pairs={{0,8},{1,9},{2,10},{3,11},{4,12},{5,13},{6,14},{7,15},{8,0},{9,1},... | collective-permute-start | bytes 417800 | tf_op jit(solution)/shard_map/ppermute | solution.py:227
  7.1 1.3 %collective-permute-start.11 = (bf16[32,2176]{1,0:T(8,128)(2,1)S(1)}, bf16[32,2176]{1,0:T(8,128)(2,1)S(1)}, u32[]{:S(2)}, u32[]{:S(2)}) collective-permute-start(bf16[32,2176]{1,0:T(8,128)(2,1)S(1)} %pad_maximum_fusion.refs_0_), channel_id=1, source_target_pairs={{0,12},{1,13},{2,14},{3,15},{4,8},{5,9},{6,10},{7,11},{8,4},{9,5},... | collective-permute-start | bytes 417800 | tf_op jit(solution)/shard_map/ppermute | solution.py:227
  8.5 0.2 collective-permute-start.3
  8.7 1.5 %collective-permute-start.1 = (bf16[32,2176]{1,0:T(8,128)(2,1)S(1)}, bf16[32,2176]{1,0:T(8,128)(2,1)S(1)}, u32[]{:S(2)}, u32[]{:S(2)}) collective-permute-start(bf16[32,2176]{1,0:T(8,128)(2,1)S(1)} %pad_maximum_fusion.refs_0_), channel_id=1, source_target_pairs={{0,2},{1,3},{2,0},{3,1},{4,6},{5,7},{6,4},{7,5},{8,10},{9,11},{10,... | collective-permute-start | bytes 417800 | tf_op jit(solution)/shard_map/ppermute | solution.py:227
  10.2 0.0 collective-permute-start
  10.2 7.4 %collective-permute-done.7.refs_8_ = bf16[32,2176]{1,0:T(8,128)(2,1)S(1)} collective-permute-done((bf16[32,2176]{1,0:T(8,128)(2,1)S(1)}, bf16[32,2176]{1,0:T(8,128)(2,1)S(1)}, u32[]{:S(2)}, u32[]{:S(2)}) %collective-permute-start.7) | collective-permute-done | bytes 139296 | tf_op jit(solution)/shard_map/ppermute | solution.py:227
  17.6 1.8 %collective-permute-start.9 = (bf16[32,2176]{1,0:T(8,128)(2,1)S(1)}, bf16[32,2176]{1,0:T(8,128)(2,1)S(1)}, u32[]{:S(2)}, u32[]{:S(2)}) collective-permute-start(bf16[32,2176]{1,0:T(8,128)(2,1)S(1)} %collective-permute-done.7.refs_8_), channel_id=1, source_target_pairs={{0,2},{1,3},{2,0},{3,1},{4,6},{5,7},{6,4},{7,5},{8,10},{9,11},{10,... | collective-permute-start | bytes 417800 | tf_op jit(solution)/shard_map/ppermute | solution.py:227
  19.5 0.0 collective-permute-done.11.refs_12_
  19.5 0.2 collective-permute-start.13
  19.7 0.0 collective-permute-done.3.refs_4_
  19.7 1.8 %collective-permute-start.5 = (bf16[32,2176]{1,0:T(8,128)(2,1)S(1)}, bf16[32,2176]{1,0:T(8,128)(2,1)S(1)}, u32[]{:S(2)}, u32[]{:S(2)}) collective-permute-start(bf16[32,2176]{1,0:T(8,128)(2,1)S(1)} %collective-permute-done.3.refs_4_), channel_id=1, source_target_pairs={{0,2},{1,3},{2,0},{3,1},{4,6},{5,7},{6,4},{7,5},{8,10},{9,11},{10,... | collective-permute-start | bytes 417800 | tf_op jit(solution)/shard_map/ppermute | solution.py:227
  21.5 0.0 collective-permute-done.1.refs_2_
  21.5 0.0 collective-permute-start.12
  21.5 0.0 collective-permute-done.refs_1_
  21.5 0.5 collective-permute-start.4
  22.0 2.2 %collective-permute-done.9.refs_10_ = bf16[32,2176]{1,0:T(8,128)(2,1)S(1)} collective-permute-done((bf16[32,2176]{1,0:T(8,128)(2,1)S(1)}, bf16[32,2176]{1,0:T(8,128)(2,1)S(1)}, u32[]{:S(2)}, u32[]{:S(2)}) %collective-permute-start.9) | collective-permute-done | bytes 139296 | tf_op jit(solution)/shard_map/ppermute | solution.py:227
  24.2 0.0 collective-permute-start.8
  24.2 1.9 %collective-permute-done.13.refs_14_ = bf16[32,2176]{1,0:T(8,128)(2,1)S(1)} collective-permute-done((bf16[32,2176]{1,0:T(8,128)(2,1)S(1)}, bf16[32,2176]{1,0:T(8,128)(2,1)S(1)}, u32[]{:S(2)}, u32[]{:S(2)}) %collective-permute-start.13) | collective-permute-done | bytes 139296 | tf_op jit(solution)/shard_map/ppermute | solution.py:227
  26.1 0.0 collective-permute-start.2
  26.1 1.5 %collective-permute-done.5.refs_6_ = bf16[32,2176]{1,0:T(8,128)(2,1)S(1)} collective-permute-done((bf16[32,2176]{1,0:T(8,128)(2,1)S(1)}, bf16[32,2176]{1,0:T(8,128)(2,1)S(1)}, u32[]{:S(2)}, u32[]{:S(2)}) %collective-permute-start.5) | collective-permute-done | bytes 139296 | tf_op jit(solution)/shard_map/ppermute | solution.py:227
  27.6 0.0 collective-permute-start.10
  27.6 0.0 collective-permute-done.12.refs_13_
  27.6 0.5 collective-permute-start.14
  28.1 0.0 collective-permute-done.4.refs_5_
  28.1 0.1 collective-permute-start.6
  28.2 0.0 copy-start
  28.2 1.9 %copy-done = bf16[1,768,2048]{2,1,0:T(8,128)(2,1)S(1)} copy-done((bf16[1,768,2048]{2,1,0:T(8,128)(2,1)S(1)}, bf16[1,768,2048]{2,1,0:T(8,128)(2,1)}, u32[]{:S(2)}) %copy-start) | copy-done | bytes 3145752
  30.1 0.0 copy-start.2
  30.1 1.1 %copy-done.2 = bf16[1,1,16,24,768]{4,3,2,1,0:T(8,128)(2,1)S(1)} copy-done((bf16[1,1,16,24,768]{4,3,2,1,0:T(8,128)(2,1)S(1)}, bf16[1,1,16,24,768]{4,3,2,1,0:T(8,128)(2,1)}, u32[]{:S(2)}) %copy-start.2) | copy-done | bytes 589848
  31.2 0.0 copy-start.3
  31.2 0.9 %copy-done.3 = bf16[1,32,2048]{2,1,0:T(8,128)(2,1)S(1)} copy-done((bf16[1,32,2048]{2,1,0:T(8,128)(2,1)S(1)}, bf16[1,32,2048]{2,1,0:T(8,128)(2,1)}, u32[]{:S(2)}) %copy-start.3) | copy-done | bytes 131096
  32.1 0.0 copy-start.5
  32.1 0.8 %copy-done.5 = bf16[1,768,32]{1,2,0:T(8,128)(2,1)S(1)} copy-done((bf16[1,768,32]{1,2,0:T(8,128)(2,1)S(1)}, bf16[1,768,32]{1,2,0:T(8,128)(2,1)}, u32[]{:S(2)}) %copy-start.5) | copy-done | bytes 49176
  32.9 2.3 %forward.1 = (bf16[384,32]{1,0:T(8,128)(2,1)S(1)}, f32[384,2048]{1,0:T(8,128)S(1)}) custom-call(bf16[384,768]{1,0:T(8,128)(2,1)S(1)} %bitcast.20, bf16[768,2048]{1,0:T(8,128)(2,1)S(1)} %bitcast.18, bf16[32,768]{1,0:T(8,128)(2,1)S(1)} %bitcast.24, bf16[32,2048]{1,0:T(8,128)(2,1)S(1)} %bitcast.22), custom_call_target="tpu_custom_call" | custom-call | tf_op jit(solution)/shard_map/forward/pallas_call | solution.py:240
  35.2 0.0 copy-start.1
  35.2 0.0 copy-start.4
  35.2 0.0 copy-start.6
  35.2 0.0 collective-permute-done.8.refs_9_
  35.2 0.0 collective-permute-done.2.refs_3_
  35.2 0.0 collective-permute-done.10.refs_11_
  35.2 0.0 collective-permute-done.14.refs_15_
  35.2 0.0 collective-permute-done.6.refs_7_
  35.2 4.7 %combine.1 = (bf16[384,2048]{1,0:T(8,128)(2,1)S(1)}, f32[16,128]{1,0:T(8,128)S(1)}) custom-call(s32[1]{0:T(128)} %bitcast.me_ref, bf16[32,2176]{1,0:T(8,128)(2,1)S(1)} %pad_maximum_fusion.refs_0_, bf16[32,2176]{1,0:T(8,128)(2,1)S(1)} %collective-permute-done.refs_1_, bf16[32,2176]{1,0:T(8,128)(2,1)S(1)} %collective-permute-done.1.refs_2_, ...), custom_call_target="tpu_custom_call" | custom-call | tf_op jit(solution)/shard_map/combine/pallas_call | solution.py:262
  40.0 0.5 collective-permute-start.15
  40.5 0.8 %collective-permute-done.15 = f32[16,128]{1,0:T(8,128)S(1)} collective-permute-done((f32[16,128]{1,0:T(8,128)S(1)}, f32[16,128]{1,0:T(8,128)S(1)}, u32[]{:S(2)}, u32[]{:S(2)}) %collective-permute-start.15) | collective-permute-done | bytes 8224 | tf_op jit(solution)/shard_map/ppermute | solution.py:227
  41.3 0.1 broadcast_select_fusion
  41.4 1.2 %collective-permute-start.16 = (f32[16,128]{1,0:T(8,128)S(1)}, f32[16,128]{1,0:T(8,128)S(1)}, u32[]{:S(2)}, u32[]{:S(2)}) collective-permute-start(f32[16,128]{1,0:T(8,128)S(1)} %broadcast_select_fusion), channel_id=1, source_target_pairs={{0,2},{1,3},{2,0},{3,1},{4,6},{5,7},{6,4},{7,5},{8,10},{9,11},{10,... | collective-permute-start | bytes 24584 | tf_op jit(solution)/shard_map/ppermute | solution.py:227
  42.6 2.4 %collective-permute-done.16 = f32[16,128]{1,0:T(8,128)S(1)} collective-permute-done((f32[16,128]{1,0:T(8,128)S(1)}, f32[16,128]{1,0:T(8,128)S(1)}, u32[]{:S(2)}, u32[]{:S(2)}) %collective-permute-start.16) | collective-permute-done | bytes 8224 | tf_op jit(solution)/shard_map/ppermute | solution.py:227
  45.0 0.1 broadcast_select_fusion.1
  45.1 1.5 %collective-permute-start.17 = (f32[16,128]{1,0:T(8,128)S(1)}, f32[16,128]{1,0:T(8,128)S(1)}, u32[]{:S(2)}, u32[]{:S(2)}) collective-permute-start(f32[16,128]{1,0:T(8,128)S(1)} %broadcast_select_fusion.1), channel_id=1, source_target_pairs={{0,4},{1,5},{2,6},{3,7},{4,0},{5,1},{6,2},{7,3},{8,12},{9,13},{10,... | collective-permute-start | bytes 24584 | tf_op jit(solution)/shard_map/ppermute | solution.py:227
  46.6 2.2 %collective-permute-done.17 = f32[16,128]{1,0:T(8,128)S(1)} collective-permute-done((f32[16,128]{1,0:T(8,128)S(1)}, f32[16,128]{1,0:T(8,128)S(1)}, u32[]{:S(2)}, u32[]{:S(2)}) %collective-permute-start.17) | collective-permute-done | bytes 8224 | tf_op jit(solution)/shard_map/ppermute | solution.py:227
  48.8 0.1 broadcast_select_fusion.2
  48.8 3.4 %collective-permute-start.18 = (f32[16,128]{1,0:T(8,128)S(1)}, f32[16,128]{1,0:T(8,128)S(1)}, u32[]{:S(2)}, u32[]{:S(2)}) collective-permute-start(f32[16,128]{1,0:T(8,128)S(1)} %broadcast_select_fusion.2), channel_id=1, source_target_pairs={{0,8},{1,9},{2,10},{3,11},{4,12},{5,13},{6,14},{7,15},{8,0},{9,1},... | collective-permute-start | bytes 24584 | tf_op jit(solution)/shard_map/ppermute | solution.py:227
  52.2 0.0 copy-done.1
  52.2 0.0 copy-done.4
  52.2 0.0 copy-done.6
  52.2 3.8 %backward.1 = (bf16[384,768]{1,0:T(8,128)(2,1)}, f32[32,768]{1,0:T(8,128)}, f32[32,2048]{1,0:T(8,128)}) custom-call(bf16[384,2048]{1,0:T(8,128)(2,1)S(1)} %get-tuple-element.12.scaled_ref, bf16[384,768]{1,0:T(8,128)(2,1)S(1)} %bitcast.21, bf16[384,32]{1,0:T(8,128)(2,1)S(1)} %get-tuple-element.13.low_ref, bf16[768,2048]{1,0:T(8,128)(2,1)S(1)} %bitcast.19, ...), custom_call_target="tpu_custom_call" | custom-call | tf_op jit(solution)/shard_map/backward/pallas_call | solution.py:278
  56.0 0.0 collective-permute-done.18
  56.0 0.1 slice_select_fusion
  56.1 0.6 %select_reduce_fusion = f32[8,32]{1,0:T(8,128)} fusion(f32[16,32]{1,0:T(8,128)S(1)} %slice_select_fusion, s32[8,32]{1,0:T(8,128)S(1)} %get-tuple-element.18), kind=kLoop, calls=%fused_computation.1 | loop fusion | flops 12032 | bytes 4096 | tf_op jit(solution)/shard_map/reduce_sum | solution.py:298
  (4 shorter events, 0.0 us)
Async XLA Ops:
  3.0 14.6 %collective-permute-start.7 = (bf16[32,2176]{1,0:T(8,128)(2,1)S(1)}, bf16[32,2176]{1,0:T(8,128)(2,1)S(1)}, u32[]{:S(2)}, u32[]{:S(2)}) collective-permute-start(bf16[32,2176]{1,0:T(8,128)(2,1)S(1)} %pad_maximum_fusion.refs_0_), channel_id=1, source_target_pairs={{0,8},{1,9},{2,10},{3,11},{4,12},{5,13},{6,14},{7,15},{8,0},{9,1},... | collective-permute-start | bytes 417800 | tf_op jit(solution)/shard_map/ppermute | solution.py:227
  7.1 12.4 %collective-permute-start.11 = (bf16[32,2176]{1,0:T(8,128)(2,1)S(1)}, bf16[32,2176]{1,0:T(8,128)(2,1)S(1)}, u32[]{:S(2)}, u32[]{:S(2)}) collective-permute-start(bf16[32,2176]{1,0:T(8,128)(2,1)S(1)} %pad_maximum_fusion.refs_0_), channel_id=1, source_target_pairs={{0,12},{1,13},{2,14},{3,15},{4,8},{5,9},{6,10},{7,11},{8,4},{9,5},... | collective-permute-start | bytes 417800 | tf_op jit(solution)/shard_map/ppermute | solution.py:227
  8.5 11.2 %collective-permute-start.3 = (bf16[32,2176]{1,0:T(8,128)(2,1)S(1)}, bf16[32,2176]{1,0:T(8,128)(2,1)S(1)}, u32[]{:S(2)}, u32[]{:S(2)}) collective-permute-start(bf16[32,2176]{1,0:T(8,128)(2,1)S(1)} %pad_maximum_fusion.refs_0_), channel_id=1, source_target_pairs={{0,4},{1,5},{2,6},{3,7},{4,0},{5,1},{6,2},{7,3},{8,12},{9,13},{10,... | collective-permute-start | bytes 417800 | tf_op jit(solution)/shard_map/ppermute | solution.py:227
  8.7 12.8 %collective-permute-start.1 = (bf16[32,2176]{1,0:T(8,128)(2,1)S(1)}, bf16[32,2176]{1,0:T(8,128)(2,1)S(1)}, u32[]{:S(2)}, u32[]{:S(2)}) collective-permute-start(bf16[32,2176]{1,0:T(8,128)(2,1)S(1)} %pad_maximum_fusion.refs_0_), channel_id=1, source_target_pairs={{0,2},{1,3},{2,0},{3,1},{4,6},{5,7},{6,4},{7,5},{8,10},{9,11},{10,... | collective-permute-start | bytes 417800 | tf_op jit(solution)/shard_map/ppermute | solution.py:227
  10.2 11.3 %collective-permute-start = (bf16[32,2176]{1,0:T(8,128)(2,1)S(1)}, bf16[32,2176]{1,0:T(8,128)(2,1)S(1)}, u32[]{:S(2)}, u32[]{:S(2)}) collective-permute-start(bf16[32,2176]{1,0:T(8,128)(2,1)S(1)} %pad_maximum_fusion.refs_0_), channel_id=1, source_target_pairs={{0,1},{1,0},{2,3},{3,2},{4,5},{5,4},{6,7},{7,6},{8,9},{9,8},{10,11... | collective-permute-start | bytes 417800 | tf_op jit(solution)/shard_map/ppermute | solution.py:227
  17.6 6.6 %collective-permute-start.9 = (bf16[32,2176]{1,0:T(8,128)(2,1)S(1)}, bf16[32,2176]{1,0:T(8,128)(2,1)S(1)}, u32[]{:S(2)}, u32[]{:S(2)}) collective-permute-start(bf16[32,2176]{1,0:T(8,128)(2,1)S(1)} %collective-permute-done.7.refs_8_), channel_id=1, source_target_pairs={{0,2},{1,3},{2,0},{3,1},{4,6},{5,7},{6,4},{7,5},{8,10},{9,11},{10,... | collective-permute-start | bytes 417800 | tf_op jit(solution)/shard_map/ppermute | solution.py:227
  19.5 6.7 %collective-permute-start.13 = (bf16[32,2176]{1,0:T(8,128)(2,1)S(1)}, bf16[32,2176]{1,0:T(8,128)(2,1)S(1)}, u32[]{:S(2)}, u32[]{:S(2)}) collective-permute-start(bf16[32,2176]{1,0:T(8,128)(2,1)S(1)} %collective-permute-done.11.refs_12_), channel_id=1, source_target_pairs={{0,2},{1,3},{2,0},{3,1},{4,6},{5,7},{6,4},{7,5},{8,10},{9,11},{10,... | collective-permute-start | bytes 417800 | tf_op jit(solution)/shard_map/ppermute | solution.py:227
  19.7 8.0 %collective-permute-start.5 = (bf16[32,2176]{1,0:T(8,128)(2,1)S(1)}, bf16[32,2176]{1,0:T(8,128)(2,1)S(1)}, u32[]{:S(2)}, u32[]{:S(2)}) collective-permute-start(bf16[32,2176]{1,0:T(8,128)(2,1)S(1)} %collective-permute-done.3.refs_4_), channel_id=1, source_target_pairs={{0,2},{1,3},{2,0},{3,1},{4,6},{5,7},{6,4},{7,5},{8,10},{9,11},{10,... | collective-permute-start | bytes 417800 | tf_op jit(solution)/shard_map/ppermute | solution.py:227
  21.5 6.1 %collective-permute-start.12 = (bf16[32,2176]{1,0:T(8,128)(2,1)S(1)}, bf16[32,2176]{1,0:T(8,128)(2,1)S(1)}, u32[]{:S(2)}, u32[]{:S(2)}) collective-permute-start(bf16[32,2176]{1,0:T(8,128)(2,1)S(1)} %collective-permute-done.11.refs_12_), channel_id=1, source_target_pairs={{0,1},{1,0},{2,3},{3,2},{4,5},{5,4},{6,7},{7,6},{8,9},{9,8},{10,11... | collective-permute-start | bytes 417800 | tf_op jit(solution)/shard_map/ppermute | solution.py:227
  21.5 6.6 %collective-permute-start.4 = (bf16[32,2176]{1,0:T(8,128)(2,1)S(1)}, bf16[32,2176]{1,0:T(8,128)(2,1)S(1)}, u32[]{:S(2)}, u32[]{:S(2)}) collective-permute-start(bf16[32,2176]{1,0:T(8,128)(2,1)S(1)} %collective-permute-done.3.refs_4_), channel_id=1, source_target_pairs={{0,1},{1,0},{2,3},{3,2},{4,5},{5,4},{6,7},{7,6},{8,9},{9,8},{10,11... | collective-permute-start | bytes 417800 | tf_op jit(solution)/shard_map/ppermute | solution.py:227
  24.2 11.0 %collective-permute-start.8 = (bf16[32,2176]{1,0:T(8,128)(2,1)S(1)}, bf16[32,2176]{1,0:T(8,128)(2,1)S(1)}, u32[]{:S(2)}, u32[]{:S(2)}) collective-permute-start(bf16[32,2176]{1,0:T(8,128)(2,1)S(1)} %collective-permute-done.7.refs_8_), channel_id=1, source_target_pairs={{0,1},{1,0},{2,3},{3,2},{4,5},{5,4},{6,7},{7,6},{8,9},{9,8},{10,11... | collective-permute-start | bytes 417800 | tf_op jit(solution)/shard_map/ppermute | solution.py:227
  26.1 9.1 %collective-permute-start.2 = (bf16[32,2176]{1,0:T(8,128)(2,1)S(1)}, bf16[32,2176]{1,0:T(8,128)(2,1)S(1)}, u32[]{:S(2)}, u32[]{:S(2)}) collective-permute-start(bf16[32,2176]{1,0:T(8,128)(2,1)S(1)} %collective-permute-done.1.refs_2_), channel_id=1, source_target_pairs={{0,1},{1,0},{2,3},{3,2},{4,5},{5,4},{6,7},{7,6},{8,9},{9,8},{10,11... | collective-permute-start | bytes 417800 | tf_op jit(solution)/shard_map/ppermute | solution.py:227
  27.6 7.6 %collective-permute-start.10 = (bf16[32,2176]{1,0:T(8,128)(2,1)S(1)}, bf16[32,2176]{1,0:T(8,128)(2,1)S(1)}, u32[]{:S(2)}, u32[]{:S(2)}) collective-permute-start(bf16[32,2176]{1,0:T(8,128)(2,1)S(1)} %collective-permute-done.9.refs_10_), channel_id=1, source_target_pairs={{0,1},{1,0},{2,3},{3,2},{4,5},{5,4},{6,7},{7,6},{8,9},{9,8},{10,11... | collective-permute-start | bytes 417800 | tf_op jit(solution)/shard_map/ppermute | solution.py:227
  27.6 7.6 %collective-permute-start.14 = (bf16[32,2176]{1,0:T(8,128)(2,1)S(1)}, bf16[32,2176]{1,0:T(8,128)(2,1)S(1)}, u32[]{:S(2)}, u32[]{:S(2)}) collective-permute-start(bf16[32,2176]{1,0:T(8,128)(2,1)S(1)} %collective-permute-done.13.refs_14_), channel_id=1, source_target_pairs={{0,1},{1,0},{2,3},{3,2},{4,5},{5,4},{6,7},{7,6},{8,9},{9,8},{10,11... | collective-permute-start | bytes 417800 | tf_op jit(solution)/shard_map/ppermute | solution.py:227
  28.1 7.1 %collective-permute-start.6 = (bf16[32,2176]{1,0:T(8,128)(2,1)S(1)}, bf16[32,2176]{1,0:T(8,128)(2,1)S(1)}, u32[]{:S(2)}, u32[]{:S(2)}) collective-permute-start(bf16[32,2176]{1,0:T(8,128)(2,1)S(1)} %collective-permute-done.5.refs_6_), channel_id=1, source_target_pairs={{0,1},{1,0},{2,3},{3,2},{4,5},{5,4},{6,7},{7,6},{8,9},{9,8},{10,11... | collective-permute-start | bytes 417800 | tf_op jit(solution)/shard_map/ppermute | solution.py:227
  28.2 1.9 %copy-start = (bf16[1,768,2048]{2,1,0:T(8,128)(2,1)S(1)}, bf16[1,768,2048]{2,1,0:T(8,128)(2,1)}, u32[]{:S(2)}) copy-start(bf16[1,768,2048]{2,1,0:T(8,128)(2,1)} %param.11) | copy-start | bytes 9437188
  30.1 1.1 %copy-start.2 = (bf16[1,1,16,24,768]{4,3,2,1,0:T(8,128)(2,1)S(1)}, bf16[1,1,16,24,768]{4,3,2,1,0:T(8,128)(2,1)}, u32[]{:S(2)}) copy-start(bf16[1,1,16,24,768]{4,3,2,1,0:T(8,128)(2,1)} %param.10) | copy-start | bytes 1769476
  31.2 0.9 %copy-start.3 = (bf16[1,32,2048]{2,1,0:T(8,128)(2,1)S(1)}, bf16[1,32,2048]{2,1,0:T(8,128)(2,1)}, u32[]{:S(2)}) copy-start(bf16[1,32,2048]{2,1,0:T(8,128)(2,1)} %param.13) | copy-start | bytes 393220
  32.1 0.8 %copy-start.5 = (bf16[1,768,32]{1,2,0:T(8,128)(2,1)S(1)}, bf16[1,768,32]{1,2,0:T(8,128)(2,1)}, u32[]{:S(2)}) copy-start(bf16[1,768,32]{1,2,0:T(8,128)(2,1)} %param.12) | copy-start | bytes 147460
  35.2 17.1 %copy-start.1 = (bf16[1,768,2048]{2,1,0:T(8,128)(2,1)S(1)}, bf16[1,768,2048]{2,1,0:T(8,128)(2,1)}, u32[]{:S(2)}) copy-start(bf16[1,768,2048]{2,1,0:T(8,128)(2,1)} %param.11) | copy-start | bytes 9437188
  35.2 17.1 %copy-start.4 = (bf16[1,32,2048]{2,1,0:T(8,128)(2,1)S(1)}, bf16[1,32,2048]{2,1,0:T(8,128)(2,1)}, u32[]{:S(2)}) copy-start(bf16[1,32,2048]{2,1,0:T(8,128)(2,1)} %param.13) | copy-start | bytes 393220
  35.2 17.1 %copy-start.6 = (bf16[1,768,32]{1,2,0:T(8,128)(2,1)S(1)}, bf16[1,768,32]{1,2,0:T(8,128)(2,1)}, u32[]{:S(2)}) copy-start(bf16[1,768,32]{1,2,0:T(8,128)(2,1)} %param.12) | copy-start | bytes 147460
  40.0 1.3 %collective-permute-start.15 = (f32[16,128]{1,0:T(8,128)S(1)}, f32[16,128]{1,0:T(8,128)S(1)}, u32[]{:S(2)}, u32[]{:S(2)}) collective-permute-start(f32[16,128]{1,0:T(8,128)S(1)} %get-tuple-element.17), channel_id=1, source_target_pairs={{0,1},{1,0},{2,3},{3,2},{4,5},{5,4},{6,7},{7,6},{8,9},{9,8},{10,11... | collective-permute-start | bytes 24584 | tf_op jit(solution)/shard_map/ppermute | solution.py:227
  41.4 3.7 %collective-permute-start.16 = (f32[16,128]{1,0:T(8,128)S(1)}, f32[16,128]{1,0:T(8,128)S(1)}, u32[]{:S(2)}, u32[]{:S(2)}) collective-permute-start(f32[16,128]{1,0:T(8,128)S(1)} %broadcast_select_fusion), channel_id=1, source_target_pairs={{0,2},{1,3},{2,0},{3,1},{4,6},{5,7},{6,4},{7,5},{8,10},{9,11},{10,... | collective-permute-start | bytes 24584 | tf_op jit(solution)/shard_map/ppermute | solution.py:227
  45.1 3.7 %collective-permute-start.17 = (f32[16,128]{1,0:T(8,128)S(1)}, f32[16,128]{1,0:T(8,128)S(1)}, u32[]{:S(2)}, u32[]{:S(2)}) collective-permute-start(f32[16,128]{1,0:T(8,128)S(1)} %broadcast_select_fusion.1), channel_id=1, source_target_pairs={{0,4},{1,5},{2,6},{3,7},{4,0},{5,1},{6,2},{7,3},{8,12},{9,13},{10,... | collective-permute-start | bytes 24584 | tf_op jit(solution)/shard_map/ppermute | solution.py:227
  48.8 7.2 %collective-permute-start.18 = (f32[16,128]{1,0:T(8,128)S(1)}, f32[16,128]{1,0:T(8,128)S(1)}, u32[]{:S(2)}, u32[]{:S(2)}) collective-permute-start(f32[16,128]{1,0:T(8,128)S(1)} %broadcast_select_fusion.2), channel_id=1, source_target_pairs={{0,8},{1,9},{2,10},{3,11},{4,12},{5,13},{6,14},{7,15},{8,0},{9,1},... | collective-permute-start | bytes 24584 | tf_op jit(solution)/shard_map/ppermute | solution.py:227

commit v2 on v0

--- a/solution.py
+++ b/solution.py
@@ -1,9 +1,17 @@
+import functools
+
 import jax
 import jax.numpy as jnp
 from jax import lax
+from jax.experimental import pallas as pl
+from jax.experimental.pallas import tpu as pltpu
 from jax.sharding import PartitionSpec as P
 
 adapter_scale = 2.0
+lanes = 128
+mebibyte = 1 << 20
+over_last = (((1,), (1,)), ((), ()))
+over_first = (((0,), (0,)), ((), ()))
 
 
 def slot_positions(route, expert_total):
@@ -13,7 +21,7 @@
     return jnp.take_along_axis(earlier, route, axis=1)
 
 
-def local(
+def dispatched(
     output_cotangent,
     route,
     routing_weights,
@@ -97,6 +105,383 @@
     )
 
 
+def start_copies(pairs, sems):
+    copies = [pltpu.make_async_copy(a, b, sems.at[i]) for i, (a, b) in enumerate(pairs)]
+    for copy in copies:
+        copy.start()
+    return copies
+
+
+def pack_kernel(
+    cotangent_hbm, route_hbm, weight_hbm, payload_ref, wanted_ref, route_vmem, weight_vmem, sems
+):
+    tokens, width = cotangent_hbm.shape
+    copies = start_copies(
+        [
+            (route_hbm, route_vmem),
+            (weight_hbm, weight_vmem),
+            (cotangent_hbm, payload_ref.at[:, pl.ds(0, width)]),
+        ],
+        sems,
+    )
+    payload_ref[:, width:] = jnp.full((tokens, lanes), -1.0, jnp.bfloat16)
+    copies[0].wait()
+    copies[1].wait()
+    wanted_ref[...] = jnp.bitwise_xor(route_vmem[...], lax.axis_index("expert"))
+    both = jnp.concatenate(
+        [route_vmem[...].astype(jnp.float32), weight_vmem[...].astype(jnp.float32)], axis=0
+    )
+    payload_ref[:16, width : width + tokens] = both.astype(jnp.bfloat16)
+    copies[2].wait()
+
+
+def pieces(total, size):
+    return [slice(start, start + size) for start in range(0, total, size)]
+
+
+def forward_kernel(
+    hidden_hbm,
+    down_hbm,
+    first_hbm,
+    second_hbm,
+    low_one,
+    low_two,
+    out_one,
+    out_two,
+    hidden,
+    down,
+    first,
+    second,
+    low,
+    out,
+    load_sems,
+    store_sems,
+):
+    slots = out_one.shape[0]
+    half = lax.axis_index("expert") // (lax.axis_size("expert") // 2)
+    cuts = pieces(out_one.shape[1], 512)
+    parts = [pl.ds(0, slots), pl.ds(slots, slots)]
+    bases = [pl.multiple_of(jnp.bitwise_xor(half, part) * slots, slots) for part in (0, 1)]
+    loads = start_copies(
+        [(hidden_hbm.at[pl.ds(base, slots), :], hidden.at[here, :]) for base, here in zip(bases, parts)]
+        + [(first_hbm, first), (second_hbm, second)]
+        + [(down_hbm.at[:, cut], down.at[:, cut]) for cut in cuts],
+        load_sems,
+    )
+    for load in loads[:3]:
+        load.wait()
+    low[...] = lax.dot_general(
+        hidden[...], first[...], over_last, preferred_element_type=jnp.float32
+    ).astype(jnp.bfloat16)
+    stores = [
+        pltpu.make_async_copy(low.at[here, :], low_out, store_sems.at[i])
+        for i, (here, low_out) in enumerate(zip(parts, (low_one, low_two)))
+    ]
+    for store in stores:
+        store.start()
+    loads[3].wait()
+    for cut, load in zip(cuts, loads[4:]):
+        load.wait()
+        out[:, cut] = jnp.dot(
+            hidden[...], down[:, cut], preferred_element_type=jnp.float32
+        ) + adapter_scale * jnp.dot(low[...], second[:, cut], preferred_element_type=jnp.float32)
+        for here, out_hbm in zip(parts, (out_one, out_two)):
+            store = pltpu.make_async_copy(
+                out.at[here, cut], out_hbm.at[:, cut], store_sems.at[len(stores)]
+            )
+            store.start()
+            stores.append(store)
+    for store in stores:
+        store.wait()
+
+
+def combine(me, capacity, blocks, out_ref, scaled_ref, pair_ref, base):
+    count, tokens, width = len(blocks), blocks[0].shape[0], out_ref.shape[1]
+    slots = count * capacity
+    hits, weights = [], []
+    for block in blocks:
+        meta = block[0:16, width : width + lanes].astype(jnp.float32)
+        match = meta[0:8] == me.astype(jnp.float32)
+        hits.append(jnp.sum(jnp.where(match, 1.0, 0.0), axis=0, keepdims=True))
+        weights.append(jnp.sum(jnp.where(match, meta[8:16], 0.0), axis=0, keepdims=True))
+    hit = jnp.concatenate(hits, axis=0)
+    weight = jnp.concatenate(weights, axis=0)
+    before = (
+        lax.broadcasted_iota(jnp.int32, (lanes, lanes), 0)
+        < lax.broadcasted_iota(jnp.int32, (lanes, lanes), 1)
+    )
+    earlier = jnp.dot(
+        hit.astype(jnp.bfloat16),
+        jnp.where(before, 1.0, 0.0).astype(jnp.bfloat16),
+        preferred_element_type=jnp.float32,
+    )
+    source = jnp.bitwise_xor(lax.broadcasted_iota(jnp.int32, (count, lanes), 0), me % count)
+    target = jnp.where(hit > 0.0, (source * capacity).astype(jnp.float32) + earlier, -1.0)
+    per = lanes // tokens
+    lane = lax.broadcasted_iota(jnp.int32, (1, lanes), 1)
+    slot = lax.broadcasted_iota(jnp.int32, (slots, lanes), 0).astype(jnp.float32)
+
+    def merged(rows, q):
+        row = rows[per * q : per * q + 1]
+        for r in range(1, per):
+            shifted = pltpu.roll(rows[per * q + r : per * q + r + 1], tokens * r, 1)
+            row = jnp.where(lane >= tokens * r, shifted, row)
+        return row
+
+    picks, column = [], jnp.zeros((slots, 1), jnp.float32)
+    for q in range(count // per):
+        pick = jnp.where(slot == merged(target, q), 1.0, 0.0)
+        column = column + jnp.sum(pick * merged(weight, q), axis=1, keepdims=True)
+        picks.append(pick)
+    picker = jnp.concatenate([pick.astype(jnp.bfloat16) for pick in picks], axis=1)
+    grads = jnp.zeros((slots, 1), jnp.float32)
+    for cut in pieces(width, 512):
+        gathered_rows = jnp.concatenate([block[:, cut] for block in blocks], axis=0)
+        rows = jnp.dot(picker, gathered_rows, preferred_element_type=jnp.float32)
+        grads = grads + jnp.sum(rows * out_ref[:, cut], axis=1, keepdims=True)
+        scaled_ref[:, cut] = (rows * column).astype(jnp.bfloat16)
+    for q in range(count // per):
+        row = jnp.sum(picks[q] * grads, axis=0, keepdims=True)
+        for r in range(per):
+            s = base + per * q + r
+            pair_ref[s : s + 1, :] = row if r == 0 else pltpu.roll(row, lanes - tokens * r, 1)
+
+
+def backward(part, half, scaled_ref, low_ref, operands, outs):
+    hidden_ref, down_ref, first_ref, second_ref = operands
+    put_cotangent, put_first, put_second = outs
+    slots = scaled_ref.shape[0]
+    row_base = pl.multiple_of(jnp.bitwise_xor(half, part) * slots, slots)
+    scaled = scaled_ref[...]
+    lowered = lax.dot_general(
+        scaled, second_ref[...], over_last, preferred_element_type=jnp.float32
+    ).astype(jnp.bfloat16)
+    put_second(
+        adapter_scale
+        * lax.dot_general(low_ref[...], scaled, over_first, preferred_element_type=jnp.float32)
+    )
+    put_first(
+        adapter_scale
+        * lax.dot_general(
+            lowered,
+            hidden_ref[pl.ds(row_base, slots), :],
+            over_first,
+            preferred_element_type=jnp.float32,
+        )
+    )
+    fixed = lax.dot_general(scaled, down_ref[...], over_last, preferred_element_type=jnp.float32)
+    adapter = jnp.dot(lowered, first_ref[...], preferred_element_type=jnp.float32)
+    put_cotangent((fixed + adapter_scale * adapter).astype(jnp.bfloat16))
+
+
+def first_kernel(count, capacity, *refs):
+    blocks, refs = refs[:count], refs[count:]
+    (out_ref, low_ref), operands, refs = refs[:2], refs[2:6], refs[6:]
+    cot_ref, dfirst_ref, dsecond_ref, pair_ref, scaled_ref = refs
+    me = lax.axis_index("expert")
+    combine(me, capacity, blocks, out_ref, scaled_ref, pair_ref, 0)
+
+    def put_cotangent(value):
+        cot_ref[...] = value
+
+    def put_first(value):
+        dfirst_ref[...] = value
+
+    def put_second(value):
+        dsecond_ref[...] = value
+
+    outs = put_cotangent, put_first, put_second
+    backward(0, me // count, scaled_ref, low_ref, operands, outs)
+
+
+def combine_kernel(count, capacity, *refs):
+    blocks, (out_ref, before_ref, scaled_ref, pair_ref) = refs[:count], refs[count:]
+    pair_ref[:count, :] = before_ref[...]
+    combine(
+        lax.axis_index("expert"), capacity, blocks, out_ref, scaled_ref, pair_ref, count
+    )
+
+
+def last_kernel(count, scaled_ref, low_ref, *refs):
+    operands, (cot_before, dfirst_before, dsecond_before) = refs[:4], refs[4:7]
+    cot_ref, dfirst_ref, dsecond_ref = refs[7:]
+    half = lax.axis_index("expert") // count
+    slots = scaled_ref.shape[0]
+    here = pl.ds(pl.multiple_of(half * slots, slots), slots)
+    there = pl.ds(pl.multiple_of((1 - half) * slots, slots), slots)
+    cot_ref[here, :] = cot_before[...]
+
+    def put_cotangent(value):
+        cot_ref[there, :] = value
+
+    def put_first(value):
+        dfirst_ref[...] = value + dfirst_before[...]
+
+    def put_second(value):
+        dsecond_ref[...] = value + dsecond_before[...]
+
+    backward(1, half, scaled_ref, low_ref, operands, (put_cotangent, put_first, put_second))
+
+
+vmem = pl.BlockSpec(memory_space=pltpu.VMEM)
+hbm = pl.BlockSpec(memory_space=pltpu.HBM)
+
+
+def gathered(
+    output_cotangent,
+    route,
+    routing_weights,
+    hidden,
+    down_weight,
+    first_adapter_factors,
+    second_adapter_factors,
+):
+    _, _, sources, capacity, hidden_width = hidden.shape
+    tokens, width = output_cotangent.shape
+    rank = first_adapter_factors.shape[2]
+    count = lax.axis_size("expert")
+    slots = sources * capacity
+    half = count // 2
+    bf16, f32 = jnp.bfloat16, jnp.float32
+
+    def swap(array, distance):
+        return lax.ppermute(array, "expert", [(i, i ^ distance) for i in range(count)])
+
+    def call(limit, kernel, outs, ins, scratch, *operands, results=vmem):
+        return pl.pallas_call(
+            kernel,
+            out_shape=tuple(jax.ShapeDtypeStruct(*out) for out in outs),
+            in_specs=ins,
+            out_specs=(results,) * len(outs),
+            scratch_shapes=scratch,
+            compiler_params=pltpu.CompilerParams(vmem_limit_bytes=limit * mebibyte),
+            name=getattr(kernel, "func", kernel).__name__,
+        )(*operands)
+
+    route_rows = route.T
+    payload, wanted = call(
+        60,
+        pack_kernel,
+        [((tokens, width + lanes), bf16), (route_rows.shape, jnp.int32)],
+        [hbm] * 3,
+        [
+            pltpu.VMEM(route_rows.shape, jnp.int32),
+            pltpu.VMEM(route_rows.shape, bf16),
+            pltpu.SemaphoreType.DMA((3,)),
+        ],
+        output_cotangent,
+        route_rows,
+        routing_weights.T,
+    )
+    hidden_rows = hidden.reshape(slots, hidden_width)
+    weights = (down_weight[0], first_adapter_factors[0].T, second_adapter_factors[0])
+    steps = len(pieces(width, 512))
+    low, low_late, out, out_late = call(
+        62,
+        forward_kernel,
+        [((slots // 2, rank), bf16)] * 2 + [((slots // 2, width), f32)] * 2,
+        [hbm] * 4,
+        [pltpu.VMEM(array.shape, bf16) for array in (hidden_rows, *weights)]
+        + [pltpu.VMEM((slots, rank), bf16), pltpu.VMEM((slots, width), f32)]
+        + [pltpu.SemaphoreType.DMA((4 + steps,)), pltpu.SemaphoreType.DMA((2 + 2 * steps,))],
+        hidden_rows,
+        *weights,
+        results=hbm,
+    )
+
+    blocks = {0: payload}
+    far = [d for d in range(4, count, 4)]
+    near = [d for d in far if d < half]
+    late = [d for d in far if d >= half]
+    for d in far:
+        blocks[d] = swap(payload, d)
+    blocks[2] = swap(payload, 2)
+    blocks[half], out, low = lax.optimization_barrier((blocks[half], out, low))
+    for d in far:
+        blocks[d + 2] = swap(blocks[d], 2)
+    for d in [0] + near:
+        blocks[d + 1] = swap(blocks[d], 1)
+        blocks[d + 3] = swap(blocks[d + 2], 1)
+    blocks[late[-1]], out = lax.optimization_barrier((blocks[late[-1]], out))
+    grads = [((rank, hidden_width), f32), ((rank, width), f32)]
+    *partial, pair = call(
+        24,
+        functools.partial(first_kernel, half, capacity),
+        [((slots // 2, hidden_width), bf16), *grads, ((half, lanes), f32)],
+        [vmem] * (half + 6),
+        [pltpu.VMEM((slots // 2, width), bf16)],
+        *[blocks[s] for s in range(half)],
+        out,
+        low,
+        hidden_rows,
+        *weights,
+    )
+    for d in late:
+        blocks[d + 2], partial, pair = lax.optimization_barrier((blocks[d + 2], partial, pair))
+        blocks[d + 1] = swap(blocks[d], 1)
+        blocks[d + 3] = swap(blocks[d + 2], 1)
+    scaled, pair = call(
+        24,
+        functools.partial(combine_kernel, half, capacity),
+        [((slots // 2, width), bf16), ((count, lanes), f32)],
+        [vmem] * (half + 2),
+        [],
+        *[blocks[s] for s in range(half, count)],
+        out_late,
+        pair,
+    )
+    cotangent, dfirst, dsecond = call(
+        24,
+        functools.partial(last_kernel, half),
+        [((slots, hidden_width), bf16), *grads],
+        [vmem] * 9,
+        [],
+        scaled,
+        low_late,
+        hidden_rows,
+        *weights,
+        *partial,
+    )
+
+    distance = lax.broadcasted_iota(jnp.int32, pair.shape, 0)
+    moved = [swap(pair, d) for d in (1, 2, 3)]
+    for d, values in zip((1, 2, 3), moved):
+        pair = jnp.where(jnp.bitwise_and(distance, 3) == d, values, pair)
+    moved = [swap(pair, d) for d in far]
+    for d, values in zip(far, moved):
+        pair = jnp.where(distance - jnp.bitwise_and(distance, 3) == d, values, pair)
+    hop = lax.broadcasted_iota(jnp.int32, (count, 1, 1), 0)
+    gradient = jnp.sum(jnp.where(wanted[None] == hop, pair[:, None, :tokens], 0.0), axis=0)
+    return (
+        cotangent.reshape(hidden.shape),
+        dfirst.T[None],
+        dsecond[None],
+        gradient.T,
+    )
+
+
+def local(output_cotangent, route, routing_weights, hidden, *parameters):
+    resident, pairs, sources, capacity, hidden_width = hidden.shape
+    count = lax.axis_size("expert")
+    tokens, top = route.shape
+    gather = (
+        pairs * lax.axis_size("dp") == 1
+        and resident == 1
+        and sources == count
+        and count & (count - 1) == 0
+        and 16 <= count <= 256
+        and lanes % tokens == 0
+        and (count // 2) % (lanes // tokens) == 0
+        and (count // 2 * capacity) % 16 == 0
+        and output_cotangent.shape[1] % 512 == 0
+        and hidden_width % 256 == 0
+        and top == 8
+        and 16 <= tokens <= 2 * capacity
+    )
+    form = gathered if gather else dispatched
+    return form(output_cotangent, route, routing_weights, hidden, *parameters)
+
+
 def solution(mesh):
     in_specs = (
         P(("groups", "expert", "dp"), None),

time: 88.5 us -> 45.8 us (0.52)
  waiting for transfers between devices: 38.3 us -> 5.16 us
  matrix products: 21.6 us -> 0 us
  Pallas kernels: 0 us -> 12.1 us
  starting transfers between devices: 20 us -> 22.5 us
  other arithmetic: 2.79 us -> 0.79 us
    all_to_all x3 -> x0, waiting for transfers between devices: 38.3 us -> none  [the longest x1 26.5 us: local(): lax.all_to_all(send_rows, 'expert', split_axis=0, concat_axis=0, tiled=True)]
    ppermute x0 -> x21, starting transfers between devices: none -> 22.5 us  [swap(): lax.ppermute(array, 'expert', [(i, i ^ distance) for i in range(count)])]
    dot_general x9 -> x0, matrix products: 21.6 us -> none  [the longest x1 4.17 us: local(): jnp.einsum('ejcf,efd->jecd', hidden_inputs, lax.all_gather(down_weight, '...]
    all_to_all x3 -> x0, starting transfers between devices: 20 us -> none  [the longest x1 9.11 us: local(): lax.all_to_all(slot_grad, 'expert', split_axis=0, concat_axis=0, tiled=True)]
    pallas_call x0 -> x5, Pallas kernels: none -> 12.1 us  [call(): pl.pallas_call(kernel, out_shape=tuple((jax.ShapeDtypeStruct(*out) for ou...]
    ppermute x0 -> x21, waiting for transfers between devices: none -> 5.16 us  [swap(): lax.ppermute(array, 'expert', [(i, i ^ distance) for i in range(count)])]
    unnamed x13 -> x22, local copies, waits for them, and re-layouts: 0.7 us -> 4.13 us
    gather x5 -> x0, local copies, waits for them, and re-layouts: 2.26 us -> none  [slot_positions(): return jnp.take_along_axis(earlier, route, axis=1)]
  transfers between devices with their start and end apart: 3 -> 21, of which waited for: 3 -> 5; matrix products, arithmetic and copies ran while one was open for 7% -> 0% of each run, Pallas kernels for 0% -> 21%
where the time goes in v2:
time: 45.8 us; the launch traced here: 45.5 us
  starting transfers between devices  22.5 us (49%)
  Pallas kernels  12.1 us (26%)
  waiting for transfers between devices  5.16 us (11%)
  local copies, waits for them, and re-layouts  4.13 us (9%)
  other arithmetic  0.79 us (2%)
  between operations  0.78 us (2%)
    ppermute x21, starting transfers between devices, swap(): lax.ppermute(array, 'expert', [(i, i ^ distance) for i in range(count)])  22.5 us
    pallas_call x5, Pallas kernels, call(): pl.pallas_call(kernel, out_shape=tuple((jax.ShapeDtypeStruct(*out) for ou...  12.1 us
    ppermute x21, waiting for transfers between devices, swap(): lax.ppermute(array, 'expert', [(i, i ^ distance) for i in range(count)])  5.16 us
    unnamed x22, local copies, waits for them, and re-layouts  4.13 us
  transfers between devices with their start and end apart: 21, of which 5 were waited for; matrix products, arithmetic and copies ran while one was open for 0% of the time, Pallas kernels for 21%

profile of v2, /device:TPU:0, one launch (start us, length us, event | category | flops | bytes accessed | tf_op | source)
XLA Modules:
  0.0 45.5 jit_solution(11389064443604567817)
XLA Ops:
  0.6 1.6 %pack_kernel.1 = (bf16[32,2176]{1,0:T(8,128)(2,1)}, s32[8,32]{1,0:T(8,128)}) custom-call(bf16[32,2048]{1,0:T(8,128)(2,1)} %cotangent_hbm.1, s32[8,32]{1,0:T(8,128)} %bitcast.26, bf16[8,32]{1,0:T(8,128)(2,1)} %bitcast.28), custom_call_target="tpu_custom_call" | custom-call | tf_op jit(solution)/shard_map/pack_kernel/pallas_call | solution.py:351
  2.3 3.1 %collective-permute-start.6 = (bf16[32,2176]{1,0:T(8,128)(2,1)}, bf16[32,2176]{1,0:T(8,128)(2,1)S(1)}, u32[]{:S(2)}, u32[]{:S(2)}) collective-permute-start(bf16[32,2176]{1,0:T(8,128)(2,1)} %get-tuple-element.34.refs_0_), channel_id=1, source_target_pairs={{0,4},{1,5},{2,6},{3,7},{4,0},{5,1},{6,2},{7,3},{8,12},{9,13},{10,... | collective-permute-start | bytes 417800 | tf_op jit(solution)/shard_map/ppermute | solution.py:348
  5.4 2.6 %collective-permute-start = (bf16[32,2176]{1,0:T(8,128)(2,1)}, bf16[32,2176]{1,0:T(8,128)(2,1)S(1)}, u32[]{:S(2)}, u32[]{:S(2)}) collective-permute-start(bf16[32,2176]{1,0:T(8,128)(2,1)} %get-tuple-element.34.refs_0_), channel_id=1, source_target_pairs={{0,8},{1,9},{2,10},{3,11},{4,12},{5,13},{6,14},{7,15},{8,0},{9,1},... | collective-permute-start | bytes 417800 | tf_op jit(solution)/shard_map/ppermute | solution.py:348
  7.9 1.5 %collective-permute-start.4 = (bf16[32,2176]{1,0:T(8,128)(2,1)}, bf16[32,2176]{1,0:T(8,128)(2,1)S(1)}, u32[]{:S(2)}, u32[]{:S(2)}) collective-permute-start(bf16[32,2176]{1,0:T(8,128)(2,1)} %get-tuple-element.34.refs_0_), channel_id=1, source_target_pairs={{0,2},{1,3},{2,0},{3,1},{4,6},{5,7},{6,4},{7,5},{8,10},{9,11},{10,... | collective-permute-start | bytes 417800 | tf_op jit(solution)/shard_map/ppermute | solution.py:348
  9.4 2.0 %collective-permute-done.6.refs_4_ = bf16[32,2176]{1,0:T(8,128)(2,1)S(1)} collective-permute-done((bf16[32,2176]{1,0:T(8,128)(2,1)}, bf16[32,2176]{1,0:T(8,128)(2,1)S(1)}, u32[]{:S(2)}, u32[]{:S(2)}) %collective-permute-start.6) | collective-permute-done | bytes 139296 | tf_op jit(solution)/shard_map/ppermute | solution.py:348
  11.4 1.8 %collective-permute-start.8 = (bf16[32,2176]{1,0:T(8,128)(2,1)S(1)}, bf16[32,2176]{1,0:T(8,128)(2,1)S(1)}, u32[]{:S(2)}, u32[]{:S(2)}) collective-permute-start(bf16[32,2176]{1,0:T(8,128)(2,1)S(1)} %collective-permute-done.6.refs_4_), channel_id=1, source_target_pairs={{0,2},{1,3},{2,0},{3,1},{4,6},{5,7},{6,4},{7,5},{8,10},{9,11},{10,... | collective-permute-start | bytes 417800 | tf_op jit(solution)/shard_map/ppermute | solution.py:348
  13.2 3.0 %collective-permute-start.10 = (bf16[32,2176]{1,0:T(8,128)(2,1)}, bf16[32,2176]{1,0:T(8,128)(2,1)S(1)}, u32[]{:S(2)}, u32[]{:S(2)}) collective-permute-start(bf16[32,2176]{1,0:T(8,128)(2,1)} %get-tuple-element.34.refs_0_), channel_id=1, source_target_pairs={{0,12},{1,13},{2,14},{3,15},{4,8},{5,9},{6,10},{7,11},{8,4},{9,5},... | collective-permute-start | bytes 417800 | tf_op jit(solution)/shard_map/ppermute | solution.py:348
  16.2 0.0 collective-permute-start.3
  16.3 0.0 copy-start.7
  16.3 5.0 %forward_kernel.1 = (bf16[192,32]{1,0:T(8,128)(2,1)}, bf16[192,32]{1,0:T(8,128)(2,1)}, f32[192,2048]{1,0:T(8,128)}, f32[192,2048]{1,0:T(8,128)}) custom-call(bf16[384,768]{1,0:T(8,128)(2,1)} %bitcast.17, bf16[768,2048]{1,0:T(8,128)(2,1)} %bitcast.14, bf16[32,768]{1,0:T(8,128)(2,1)} %bitcast.23, bf16[32,2048]{1,0:T(8,128)(2,1)} %bitcast.20), custom_call_target="tpu_custom_call" | custom-call | tf_op jit(solution)/shard_map/forward_kernel/pallas_call | solution.py:351
  21.3 0.0 collective-permute-done.refs_0_
  21.3 0.6 %collective-permute-start.7 = (bf16[32,2176]{1,0:T(8,128)(2,1)S(1)}, bf16[32,2176]{1,0:T(8,128)(2,1)S(1)}, u32[]{:S(2)}, u32[]{:S(2)}) collective-permute-start(bf16[32,2176]{1,0:T(8,128)(2,1)S(1)} %collective-permute-done.6.refs_4_), channel_id=1, source_target_pairs={{0,1},{1,0},{2,3},{3,2},{4,5},{5,4},{6,7},{7,6},{8,9},{9,8},{10,11... | collective-permute-start | bytes 417800 | tf_op jit(solution)/shard_map/ppermute | solution.py:348
  21.8 0.0 collective-permute-done.4.refs_2_
  21.8 0.1 collective-permute-start.5
  21.9 0.0 collective-permute-done.8.refs_6_
  21.9 0.4 collective-permute-start.9
  22.3 0.0 collective-permute-done.10.refs_4_
  22.4 0.5 %collective-permute-start.2 = (bf16[32,2176]{1,0:T(8,128)(2,1)S(1)}, bf16[32,2176]{1,0:T(8,128)(2,1)S(1)}, u32[]{:S(2)}, u32[]{:S(2)}) collective-permute-start(bf16[32,2176]{1,0:T(8,128)(2,1)S(1)} %collective-permute-done.refs_0_), channel_id=1, source_target_pairs={{0,2},{1,3},{2,0},{3,1},{4,6},{5,7},{6,4},{7,5},{8,10},{9,11},{10,... | collective-permute-start | bytes 417800 | tf_op jit(solution)/shard_map/ppermute | solution.py:348
  22.9 0.0 collective-permute-done.3.refs_1_
  22.9 1.5 %collective-permute-start.13 = (bf16[32,2176]{1,0:T(8,128)(2,1)S(1)}, bf16[32,2176]{1,0:T(8,128)(2,1)S(1)}, u32[]{:S(2)}, u32[]{:S(2)}) collective-permute-start(bf16[32,2176]{1,0:T(8,128)(2,1)S(1)} %collective-permute-done.10.refs_4_), channel_id=1, source_target_pairs={{0,2},{1,3},{2,0},{3,1},{4,6},{5,7},{6,4},{7,5},{8,10},{9,11},{10,... | collective-permute-start | bytes 417800 | tf_op jit(solution)/shard_map/ppermute | solution.py:348
  24.4 0.0 collective-permute-done.7.refs_5_
  24.4 0.0 collective-permute-start.1
  24.4 0.0 collective-permute-done.5.refs_3_
  24.4 0.5 %collective-permute-start.12 = (bf16[32,2176]{1,0:T(8,128)(2,1)S(1)}, bf16[32,2176]{1,0:T(8,128)(2,1)S(1)}, u32[]{:S(2)}, u32[]{:S(2)}) collective-permute-start(bf16[32,2176]{1,0:T(8,128)(2,1)S(1)} %collective-permute-done.10.refs_4_), channel_id=1, source_target_pairs={{0,1},{1,0},{2,3},{3,2},{4,5},{5,4},{6,7},{7,6},{8,9},{9,8},{10,11... | collective-permute-start | bytes 417800 | tf_op jit(solution)/shard_map/ppermute | solution.py:348
  24.9 0.0 collective-permute-done.9.refs_7_
  24.9 0.0 copy-done.2
  24.9 0.0 copy-done.5
  24.9 0.0 copy-done.6
  24.9 0.0 copy-done.7
  24.9 0.0 copy-start
  24.9 1.9 %copy-done = bf16[1,768,2048]{2,1,0:T(8,128)(2,1)S(1)} copy-done((bf16[1,768,2048]{2,1,0:T(8,128)(2,1)S(1)}, bf16[1,768,2048]{2,1,0:T(8,128)(2,1)}, u32[]{:S(2)}) %copy-start) | copy-done | bytes 3145752
  26.8 1.4 %copy-done.4 = f32[192,2048]{1,0:T(8,128)S(1)} copy-done((f32[192,2048]{1,0:T(8,128)S(1)}, f32[192,2048]{1,0:T(8,128)}, u32[]{:S(2)}) %copy-start.4) | copy-done | bytes 1572888
  28.2 0.8 %copy-done.9 = bf16[192,32]{1,0:T(8,128)(2,1)S(1)} copy-done((bf16[192,32]{1,0:T(8,128)(2,1)S(1)}, bf16[192,32]{1,0:T(8,128)(2,1)}, u32[]{:S(2)}) %copy-start.9) | copy-done | bytes 12312
  29.0 2.2 %first_kernel.1 = (bf16[192,768]{1,0:T(8,128)(2,1)S(1)}, f32[32,768]{1,0:T(8,128)S(1)}, f32[32,2048]{1,0:T(8,128)S(1)}, f32[8,128]{1,0:T(8,128)S(1)}) custom-call(bf16[32,2176]{1,0:T(8,128)(2,1)S(1)} %copy-done.7, bf16[32,2176]{1,0:T(8,128)(2,1)S(1)} %collective-permute-done.3.refs_1_, bf16[32,2176]{1,0:T(8,128)(2,1)S(1)} %collective-permute-done.4.refs_2_, ...), custom_call_target="tpu_custom_call" | custom-call | tf_op jit(solution)/shard_map/first_kernel/pallas_call | solution.py:351
  31.2 0.0 copy-start.8
  31.3 0.0 collective-permute-done.2.refs_2_
  31.3 0.0 collective-permute-done.13.refs_6_
  31.3 0.1 collective-permute-start.14
  31.4 0.4 collective-permute-start.11
  31.9 0.0 collective-permute-done.12.refs_5_
  31.9 0.0 collective-permute-done.1.refs_1_
  31.9 0.8 %collective-permute-done.14.refs_7_ = bf16[32,2176]{1,0:T(8,128)(2,1)S(1)} collective-permute-done((bf16[32,2176]{1,0:T(8,128)(2,1)S(1)}, bf16[32,2176]{1,0:T(8,128)(2,1)S(1)}, u32[]{:S(2)}, u32[]{:S(2)}) %collective-permute-start.14) | collective-permute-done | bytes 139296 | tf_op jit(solution)/shard_map/ppermute | solution.py:348
  32.7 0.2 collective-permute-done.11.refs_3_
  32.9 0.0 copy-done.3
  32.9 0.8 %combine_kernel.1 = (bf16[192,2048]{1,0:T(8,128)(2,1)S(1)}, f32[16,128]{1,0:T(8,128)S(1)}) custom-call(bf16[32,2176]{1,0:T(8,128)(2,1)S(1)} %collective-permute-done.refs_0_, bf16[32,2176]{1,0:T(8,128)(2,1)S(1)} %collective-permute-done.1.refs_1_, bf16[32,2176]{1,0:T(8,128)(2,1)S(1)} %collective-permute-done.2.refs_2_, ...), custom_call_target="tpu_custom_call" | custom-call | tf_op jit(solution)/shard_map/combine_kernel/pallas_call | solution.py:351
  33.7 0.5 %collective-permute-start.15 = (f32[16,128]{1,0:T(8,128)S(1)}, f32[16,128]{1,0:T(8,128)S(1)}, u32[]{:S(2)}, u32[]{:S(2)}) collective-permute-start(f32[16,128]{1,0:T(8,128)S(1)} %get-tuple-element.63), channel_id=1, source_target_pairs={{0,3},{1,2},{2,1},{3,0},{4,7},{5,6},{6,5},{7,4},{8,11},{9,10},{10,... | collective-permute-start | bytes 24584 | tf_op jit(solution)/shard_map/ppermute | solution.py:348
  34.1 1.5 %collective-permute-start.16 = (f32[16,128]{1,0:T(8,128)S(1)}, f32[16,128]{1,0:T(8,128)S(1)}, u32[]{:S(2)}, u32[]{:S(2)}) collective-permute-start(f32[16,128]{1,0:T(8,128)S(1)} %get-tuple-element.63), channel_id=1, source_target_pairs={{0,2},{1,3},{2,0},{3,1},{4,6},{5,7},{6,4},{7,5},{8,10},{9,11},{10,... | collective-permute-start | bytes 24584 | tf_op jit(solution)/shard_map/ppermute | solution.py:348
  35.6 0.0 collective-permute-start.17
  35.6 1.1 %collective-permute-done.15 = f32[16,128]{1,0:T(8,128)S(1)} collective-permute-done((f32[16,128]{1,0:T(8,128)S(1)}, f32[16,128]{1,0:T(8,128)S(1)}, u32[]{:S(2)}, u32[]{:S(2)}) %collective-permute-start.15) | collective-permute-done | bytes 8224 | tf_op jit(solution)/shard_map/ppermute | solution.py:348
  36.8 1.0 %collective-permute-done.16 = f32[16,128]{1,0:T(8,128)S(1)} collective-permute-done((f32[16,128]{1,0:T(8,128)S(1)}, f32[16,128]{1,0:T(8,128)S(1)}, u32[]{:S(2)}, u32[]{:S(2)}) %collective-permute-start.16) | collective-permute-done | bytes 8224 | tf_op jit(solution)/shard_map/ppermute | solution.py:348
  37.8 0.0 collective-permute-done.17
  37.8 0.1 select_select_fusion
  37.9 1.1 %collective-permute-start.18 = (f32[16,128]{1,0:T(8,128)S(1)}, f32[16,128]{1,0:T(8,128)S(1)}, u32[]{:S(2)}, u32[]{:S(2)}) collective-permute-start(f32[16,128]{1,0:T(8,128)S(1)} %select_select_fusion), channel_id=1, source_target_pairs={{0,12},{1,13},{2,14},{3,15},{4,8},{5,9},{6,10},{7,11},{8,4},{9,5},... | collective-permute-start | bytes 24584 | tf_op jit(solution)/shard_map/ppermute | solution.py:348
  38.9 0.2 collective-permute-start.19
  39.1 3.2 %collective-permute-start.20 = (f32[16,128]{1,0:T(8,128)S(1)}, f32[16,128]{1,0:T(8,128)S(1)}, u32[]{:S(2)}, u32[]{:S(2)}) collective-permute-start(f32[16,128]{1,0:T(8,128)S(1)} %select_select_fusion), channel_id=1, source_target_pairs={{0,4},{1,5},{2,6},{3,7},{4,0},{5,1},{6,2},{7,3},{8,12},{9,13},{10,... | collective-permute-start | bytes 24584 | tf_op jit(solution)/shard_map/ppermute | solution.py:348
  42.3 0.0 copy-done.1
  42.3 0.0 copy-done.8
  42.3 0.0 copy-start.10
  42.3 2.5 %last_kernel.1 = (bf16[384,768]{1,0:T(8,128)(2,1)}, f32[32,768]{1,0:T(8,128)}, f32[32,2048]{1,0:T(8,128)}) custom-call(bf16[192,2048]{1,0:T(8,128)(2,1)S(1)} %get-tuple-element.54.scaled_ref, bf16[192,32]{1,0:T(8,128)(2,1)S(1)} %copy-done.8, bf16[384,768]{1,0:T(8,128)(2,1)S(1)} %bitcast.19, bf16[768,2048]{1,0:T(8,128)(2,1)S(1)} %bitcast.16, ...), custom_call_target="tpu_custom_call" | custom-call | tf_op jit(solution)/shard_map/last_kernel/pallas_call | solution.py:351
  44.8 0.0 collective-permute-done.18
  44.8 0.0 collective-permute-done.19
  44.8 0.0 collective-permute-done.20
  44.8 0.1 slice_select_fusion
  44.9 0.6 %select_reduce_fusion = f32[8,32]{1,0:T(8,128)} fusion(f32[16,32]{1,0:T(8,128)S(1)} %slice_select_fusion, s32[8,32]{1,0:T(8,128)S(1)} %copy-done.10), kind=kLoop, calls=%fused_computation | loop fusion | flops 12032 | bytes 4096 | tf_op jit(solution)/shard_map/reduce_sum | solution.py:454
  (12 shorter events, 0.0 us)
Async XLA Ops:
  2.3 9.1 %collective-permute-start.6 = (bf16[32,2176]{1,0:T(8,128)(2,1)}, bf16[32,2176]{1,0:T(8,128)(2,1)S(1)}, u32[]{:S(2)}, u32[]{:S(2)}) collective-permute-start(bf16[32,2176]{1,0:T(8,128)(2,1)} %get-tuple-element.34.refs_0_), channel_id=1, source_target_pairs={{0,4},{1,5},{2,6},{3,7},{4,0},{5,1},{6,2},{7,3},{8,12},{9,13},{10,... | collective-permute-start | bytes 417800 | tf_op jit(solution)/shard_map/ppermute | solution.py:348
  5.4 15.9 %collective-permute-start = (bf16[32,2176]{1,0:T(8,128)(2,1)}, bf16[32,2176]{1,0:T(8,128)(2,1)S(1)}, u32[]{:S(2)}, u32[]{:S(2)}) collective-permute-start(bf16[32,2176]{1,0:T(8,128)(2,1)} %get-tuple-element.34.refs_0_), channel_id=1, source_target_pairs={{0,8},{1,9},{2,10},{3,11},{4,12},{5,13},{6,14},{7,15},{8,0},{9,1},... | collective-permute-start | bytes 417800 | tf_op jit(solution)/shard_map/ppermute | solution.py:348
  7.9 13.9 %collective-permute-start.4 = (bf16[32,2176]{1,0:T(8,128)(2,1)}, bf16[32,2176]{1,0:T(8,128)(2,1)S(1)}, u32[]{:S(2)}, u32[]{:S(2)}) collective-permute-start(bf16[32,2176]{1,0:T(8,128)(2,1)} %get-tuple-element.34.refs_0_), channel_id=1, source_target_pairs={{0,2},{1,3},{2,0},{3,1},{4,6},{5,7},{6,4},{7,5},{8,10},{9,11},{10,... | collective-permute-start | bytes 417800 | tf_op jit(solution)/shard_map/ppermute | solution.py:348
  11.4 10.5 %collective-permute-start.8 = (bf16[32,2176]{1,0:T(8,128)(2,1)S(1)}, bf16[32,2176]{1,0:T(8,128)(2,1)S(1)}, u32[]{:S(2)}, u32[]{:S(2)}) collective-permute-start(bf16[32,2176]{1,0:T(8,128)(2,1)S(1)} %collective-permute-done.6.refs_4_), channel_id=1, source_target_pairs={{0,2},{1,3},{2,0},{3,1},{4,6},{5,7},{6,4},{7,5},{8,10},{9,11},{10,... | collective-permute-start | bytes 417800 | tf_op jit(solution)/shard_map/ppermute | solution.py:348
  13.2 9.1 %collective-permute-start.10 = (bf16[32,2176]{1,0:T(8,128)(2,1)}, bf16[32,2176]{1,0:T(8,128)(2,1)S(1)}, u32[]{:S(2)}, u32[]{:S(2)}) collective-permute-start(bf16[32,2176]{1,0:T(8,128)(2,1)} %get-tuple-element.34.refs_0_), channel_id=1, source_target_pairs={{0,12},{1,13},{2,14},{3,15},{4,8},{5,9},{6,10},{7,11},{8,4},{9,5},... | collective-permute-start | bytes 417800 | tf_op jit(solution)/shard_map/ppermute | solution.py:348
  16.2 6.7 %collective-permute-start.3 = (bf16[32,2176]{1,0:T(8,128)(2,1)}, bf16[32,2176]{1,0:T(8,128)(2,1)S(1)}, u32[]{:S(2)}, u32[]{:S(2)}) collective-permute-start(bf16[32,2176]{1,0:T(8,128)(2,1)} %get-tuple-element.34.refs_0_), channel_id=1, source_target_pairs={{0,1},{1,0},{2,3},{3,2},{4,5},{5,4},{6,7},{7,6},{8,9},{9,8},{10,11... | collective-permute-start | bytes 417800 | tf_op jit(solution)/shard_map/ppermute | solution.py:348
  16.2 8.7 %copy-start.2 = (bf16[1,1,16,24,768]{4,3,2,1,0:T(8,128)(2,1)S(1)}, bf16[1,1,16,24,768]{4,3,2,1,0:T(8,128)(2,1)}, u32[]{:S(2)}) copy-start(bf16[1,1,16,24,768]{4,3,2,1,0:T(8,128)(2,1)} %param.10) | copy-start | bytes 1769476
  16.2 8.7 %copy-start.5 = (bf16[1,32,2048]{2,1,0:T(8,128)(2,1)S(1)}, bf16[1,32,2048]{2,1,0:T(8,128)(2,1)}, u32[]{:S(2)}) copy-start(bf16[1,32,2048]{2,1,0:T(8,128)(2,1)} %param.13) | copy-start | bytes 393220
  16.2 8.7 %copy-start.6 = (bf16[1,768,32]{1,2,0:T(8,128)(2,1)S(1)}, bf16[1,768,32]{1,2,0:T(8,128)(2,1)}, u32[]{:S(2)}) copy-start(bf16[1,768,32]{1,2,0:T(8,128)(2,1)} %param.12) | copy-start | bytes 147460
  16.3 8.7 %copy-start.7 = (bf16[32,2176]{1,0:T(8,128)(2,1)S(1)}, bf16[32,2176]{1,0:T(8,128)(2,1)}, u32[]{:S(2)}) copy-start(bf16[32,2176]{1,0:T(8,128)(2,1)} %get-tuple-element.34.refs_0_) | copy-start | bytes 417796
  21.3 3.1 %collective-permute-start.7 = (bf16[32,2176]{1,0:T(8,128)(2,1)S(1)}, bf16[32,2176]{1,0:T(8,128)(2,1)S(1)}, u32[]{:S(2)}, u32[]{:S(2)}) collective-permute-start(bf16[32,2176]{1,0:T(8,128)(2,1)S(1)} %collective-permute-done.6.refs_4_), channel_id=1, source_target_pairs={{0,1},{1,0},{2,3},{3,2},{4,5},{5,4},{6,7},{7,6},{8,9},{9,8},{10,11... | collective-permute-start | bytes 417800 | tf_op jit(solution)/shard_map/ppermute | solution.py:348
  21.8 2.6 %collective-permute-start.5 = (bf16[32,2176]{1,0:T(8,128)(2,1)S(1)}, bf16[32,2176]{1,0:T(8,128)(2,1)S(1)}, u32[]{:S(2)}, u32[]{:S(2)}) collective-permute-start(bf16[32,2176]{1,0:T(8,128)(2,1)S(1)} %collective-permute-done.4.refs_2_), channel_id=1, source_target_pairs={{0,1},{1,0},{2,3},{3,2},{4,5},{5,4},{6,7},{7,6},{8,9},{9,8},{10,11... | collective-permute-start | bytes 417800 | tf_op jit(solution)/shard_map/ppermute | solution.py:348
  21.9 3.0 %collective-permute-start.9 = (bf16[32,2176]{1,0:T(8,128)(2,1)S(1)}, bf16[32,2176]{1,0:T(8,128)(2,1)S(1)}, u32[]{:S(2)}, u32[]{:S(2)}) collective-permute-start(bf16[32,2176]{1,0:T(8,128)(2,1)S(1)} %collective-permute-done.8.refs_6_), channel_id=1, source_target_pairs={{0,1},{1,0},{2,3},{3,2},{4,5},{5,4},{6,7},{7,6},{8,9},{9,8},{10,11... | collective-permute-start | bytes 417800 | tf_op jit(solution)/shard_map/ppermute | solution.py:348
  22.4 8.9 %collective-permute-start.2 = (bf16[32,2176]{1,0:T(8,128)(2,1)S(1)}, bf16[32,2176]{1,0:T(8,128)(2,1)S(1)}, u32[]{:S(2)}, u32[]{:S(2)}) collective-permute-start(bf16[32,2176]{1,0:T(8,128)(2,1)S(1)} %collective-permute-done.refs_0_), channel_id=1, source_target_pairs={{0,2},{1,3},{2,0},{3,1},{4,6},{5,7},{6,4},{7,5},{8,10},{9,11},{10,... | collective-permute-start | bytes 417800 | tf_op jit(solution)/shard_map/ppermute | solution.py:348
  22.9 8.4 %collective-permute-start.13 = (bf16[32,2176]{1,0:T(8,128)(2,1)S(1)}, bf16[32,2176]{1,0:T(8,128)(2,1)S(1)}, u32[]{:S(2)}, u32[]{:S(2)}) collective-permute-start(bf16[32,2176]{1,0:T(8,128)(2,1)S(1)} %collective-permute-done.10.refs_4_), channel_id=1, source_target_pairs={{0,2},{1,3},{2,0},{3,1},{4,6},{5,7},{6,4},{7,5},{8,10},{9,11},{10,... | collective-permute-start | bytes 417800 | tf_op jit(solution)/shard_map/ppermute | solution.py:348
  24.4 7.5 %collective-permute-start.1 = (bf16[32,2176]{1,0:T(8,128)(2,1)S(1)}, bf16[32,2176]{1,0:T(8,128)(2,1)S(1)}, u32[]{:S(2)}, u32[]{:S(2)}) collective-permute-start(bf16[32,2176]{1,0:T(8,128)(2,1)S(1)} %collective-permute-done.refs_0_), channel_id=1, source_target_pairs={{0,1},{1,0},{2,3},{3,2},{4,5},{5,4},{6,7},{7,6},{8,9},{9,8},{10,11... | collective-permute-start | bytes 417800 | tf_op jit(solution)/shard_map/ppermute | solution.py:348
  24.4 7.5 %collective-permute-start.12 = (bf16[32,2176]{1,0:T(8,128)(2,1)S(1)}, bf16[32,2176]{1,0:T(8,128)(2,1)S(1)}, u32[]{:S(2)}, u32[]{:S(2)}) collective-permute-start(bf16[32,2176]{1,0:T(8,128)(2,1)S(1)} %collective-permute-done.10.refs_4_), channel_id=1, source_target_pairs={{0,1},{1,0},{2,3},{3,2},{4,5},{5,4},{6,7},{7,6},{8,9},{9,8},{10,11... | collective-permute-start | bytes 417800 | tf_op jit(solution)/shard_map/ppermute | solution.py:348
  24.9 1.9 %copy-start = (bf16[1,768,2048]{2,1,0:T(8,128)(2,1)S(1)}, bf16[1,768,2048]{2,1,0:T(8,128)(2,1)}, u32[]{:S(2)}) copy-start(bf16[1,768,2048]{2,1,0:T(8,128)(2,1)} %param.11) | copy-start | bytes 9437188
  26.8 1.4 %copy-start.4 = (f32[192,2048]{1,0:T(8,128)S(1)}, f32[192,2048]{1,0:T(8,128)}, u32[]{:S(2)}) copy-start(f32[192,2048]{1,0:T(8,128)} %get-tuple-element.39.refs_8_) | copy-start | bytes 4718596
  28.2 0.8 %copy-start.9 = (bf16[192,32]{1,0:T(8,128)(2,1)S(1)}, bf16[192,32]{1,0:T(8,128)(2,1)}, u32[]{:S(2)}) copy-start(bf16[192,32]{1,0:T(8,128)(2,1)} %get-tuple-element.40.refs_9_) | copy-start | bytes 36868
  29.0 3.9 %copy-start.3 = (f32[192,2048]{1,0:T(8,128)S(1)}, f32[192,2048]{1,0:T(8,128)}, u32[]{:S(2)}) copy-start(f32[192,2048]{1,0:T(8,128)} %get-tuple-element.52.refs_8_) | copy-start | bytes 4718596
  29.0 13.2 %copy-start.1 = (bf16[1,768,2048]{2,1,0:T(8,128)(2,1)S(1)}, bf16[1,768,2048]{2,1,0:T(8,128)(2,1)}, u32[]{:S(2)}) copy-start(bf16[1,768,2048]{2,1,0:T(8,128)(2,1)} %param.11) | copy-start | bytes 9437188
  31.2 11.0 %copy-start.8 = (bf16[192,32]{1,0:T(8,128)(2,1)S(1)}, bf16[192,32]{1,0:T(8,128)(2,1)}, u32[]{:S(2)}) copy-start(bf16[192,32]{1,0:T(8,128)(2,1)} %get-tuple-element.55.low_ref) | copy-start | bytes 36868
  31.3 1.4 %collective-permute-start.14 = (bf16[32,2176]{1,0:T(8,128)(2,1)S(1)}, bf16[32,2176]{1,0:T(8,128)(2,1)S(1)}, u32[]{:S(2)}, u32[]{:S(2)}) collective-permute-start(bf16[32,2176]{1,0:T(8,128)(2,1)S(1)} %collective-permute-done.13.refs_6_), channel_id=1, source_target_pairs={{0,1},{1,0},{2,3},{3,2},{4,5},{5,4},{6,7},{7,6},{8,9},{9,8},{10,11... | collective-permute-start | bytes 417800 | tf_op jit(solution)/shard_map/ppermute | solution.py:348
  31.4 1.5 %collective-permute-start.11 = (bf16[32,2176]{1,0:T(8,128)(2,1)S(1)}, bf16[32,2176]{1,0:T(8,128)(2,1)S(1)}, u32[]{:S(2)}, u32[]{:S(2)}) collective-permute-start(bf16[32,2176]{1,0:T(8,128)(2,1)S(1)} %collective-permute-done.2.refs_2_), channel_id=1, source_target_pairs={{0,1},{1,0},{2,3},{3,2},{4,5},{5,4},{6,7},{7,6},{8,9},{9,8},{10,11... | collective-permute-start | bytes 417800 | tf_op jit(solution)/shard_map/ppermute | solution.py:348
  33.7 3.1 %collective-permute-start.15 = (f32[16,128]{1,0:T(8,128)S(1)}, f32[16,128]{1,0:T(8,128)S(1)}, u32[]{:S(2)}, u32[]{:S(2)}) collective-permute-start(f32[16,128]{1,0:T(8,128)S(1)} %get-tuple-element.63), channel_id=1, source_target_pairs={{0,3},{1,2},{2,1},{3,0},{4,7},{5,6},{6,5},{7,4},{8,11},{9,10},{10,... | collective-permute-start | bytes 24584 | tf_op jit(solution)/shard_map/ppermute | solution.py:348
  34.1 3.7 %collective-permute-start.16 = (f32[16,128]{1,0:T(8,128)S(1)}, f32[16,128]{1,0:T(8,128)S(1)}, u32[]{:S(2)}, u32[]{:S(2)}) collective-permute-start(f32[16,128]{1,0:T(8,128)S(1)} %get-tuple-element.63), channel_id=1, source_target_pairs={{0,2},{1,3},{2,0},{3,1},{4,6},{5,7},{6,4},{7,5},{8,10},{9,11},{10,... | collective-permute-start | bytes 24584 | tf_op jit(solution)/shard_map/ppermute | solution.py:348
  35.6 2.2 %collective-permute-start.17 = (f32[16,128]{1,0:T(8,128)S(1)}, f32[16,128]{1,0:T(8,128)S(1)}, u32[]{:S(2)}, u32[]{:S(2)}) collective-permute-start(f32[16,128]{1,0:T(8,128)S(1)} %get-tuple-element.63), channel_id=1, source_target_pairs={{0,1},{1,0},{2,3},{3,2},{4,5},{5,4},{6,7},{7,6},{8,9},{9,8},{10,11... | collective-permute-start | bytes 24584 | tf_op jit(solution)/shard_map/ppermute | solution.py:348
  37.9 7.0 %collective-permute-start.18 = (f32[16,128]{1,0:T(8,128)S(1)}, f32[16,128]{1,0:T(8,128)S(1)}, u32[]{:S(2)}, u32[]{:S(2)}) collective-permute-start(f32[16,128]{1,0:T(8,128)S(1)} %select_select_fusion), channel_id=1, source_target_pairs={{0,12},{1,13},{2,14},{3,15},{4,8},{5,9},{6,10},{7,11},{8,4},{9,5},... | collective-permute-start | bytes 24584 | tf_op jit(solution)/shard_map/ppermute | solution.py:348
  38.9 5.9 %collective-permute-start.19 = (f32[16,128]{1,0:T(8,128)S(1)}, f32[16,128]{1,0:T(8,128)S(1)}, u32[]{:S(2)}, u32[]{:S(2)}) collective-permute-start(f32[16,128]{1,0:T(8,128)S(1)} %select_select_fusion), channel_id=1, source_target_pairs={{0,8},{1,9},{2,10},{3,11},{4,12},{5,13},{6,14},{7,15},{8,0},{9,1},... | collective-permute-start | bytes 24584 | tf_op jit(solution)/shard_map/ppermute | solution.py:348
  39.1 5.7 %collective-permute-start.20 = (f32[16,128]{1,0:T(8,128)S(1)}, f32[16,128]{1,0:T(8,128)S(1)}, u32[]{:S(2)}, u32[]{:S(2)}) collective-permute-start(f32[16,128]{1,0:T(8,128)S(1)} %select_select_fusion), channel_id=1, source_target_pairs={{0,4},{1,5},{2,6},{3,7},{4,0},{5,1},{6,2},{7,3},{8,12},{9,13},{10,... | collective-permute-start | bytes 24584 | tf_op jit(solution)/shard_map/ppermute | solution.py:348
  42.3 2.7 %copy-start.10 = (s32[8,32]{1,0:T(8,128)S(1)}, s32[8,32]{1,0:T(8,128)}, u32[]{:S(2)}) copy-start(s32[8,32]{1,0:T(8,128)} %get-tuple-element.62) | copy-start | bytes 3076

commit v3 on v2

--- a/solution.py
+++ b/solution.py
@@ -152,10 +152,7 @@
     down,
     first,
     second,
-    low,
-    out,
-    load_sems,
-    store_sems,
+    sems,
 ):
     slots = out_one.shape[0]
     half = lax.axis_index("expert") // (lax.axis_size("expert") // 2)
@@ -166,33 +163,23 @@
         [(hidden_hbm.at[pl.ds(base, slots), :], hidden.at[here, :]) for base, here in zip(bases, parts)]
         + [(first_hbm, first), (second_hbm, second)]
         + [(down_hbm.at[:, cut], down.at[:, cut]) for cut in cuts],
-        load_sems,
+        sems,
     )
     for load in loads[:3]:
         load.wait()
-    low[...] = lax.dot_general(
+    low = lax.dot_general(
         hidden[...], first[...], over_last, preferred_element_type=jnp.float32
     ).astype(jnp.bfloat16)
-    stores = [
-        pltpu.make_async_copy(low.at[here, :], low_out, store_sems.at[i])
-        for i, (here, low_out) in enumerate(zip(parts, (low_one, low_two)))
-    ]
-    for store in stores:
-        store.start()
+    low_one[...] = low[:slots]
+    low_two[...] = low[slots:]
     loads[3].wait()
     for cut, load in zip(cuts, loads[4:]):
         load.wait()
-        out[:, cut] = jnp.dot(
+        values = jnp.dot(
             hidden[...], down[:, cut], preferred_element_type=jnp.float32
-        ) + adapter_scale * jnp.dot(low[...], second[:, cut], preferred_element_type=jnp.float32)
-        for here, out_hbm in zip(parts, (out_one, out_two)):
-            store = pltpu.make_async_copy(
-                out.at[here, cut], out_hbm.at[:, cut], store_sems.at[len(stores)]
-            )
-            store.start()
-            stores.append(store)
-    for store in stores:
-        store.wait()
+        ) + adapter_scale * jnp.dot(low, second[:, cut], preferred_element_type=jnp.float32)
+        out_one[:, cut] = values[:slots]
+        out_two[:, cut] = values[slots:]
 
 
 def combine(me, capacity, blocks, out_ref, scaled_ref, pair_ref, base):
@@ -247,11 +234,10 @@
             pair_ref[s : s + 1, :] = row if r == 0 else pltpu.roll(row, lanes - tokens * r, 1)
 
 
-def backward(part, half, scaled_ref, low_ref, operands, outs):
+def backward(part, scaled_ref, low_ref, operands, outs):
     hidden_ref, down_ref, first_ref, second_ref = operands
     put_cotangent, put_first, put_second = outs
     slots = scaled_ref.shape[0]
-    row_base = pl.multiple_of(jnp.bitwise_xor(half, part) * slots, slots)
     scaled = scaled_ref[...]
     lowered = lax.dot_general(
         scaled, second_ref[...], over_last, preferred_element_type=jnp.float32
@@ -264,7 +250,7 @@
         adapter_scale
         * lax.dot_general(
             lowered,
-            hidden_ref[pl.ds(row_base, slots), :],
+            hidden_ref[slots * part : slots * (part + 1), :],
             over_first,
             preferred_element_type=jnp.float32,
         )
@@ -291,7 +277,7 @@
         dsecond_ref[...] = value
 
     outs = put_cotangent, put_first, put_second
-    backward(0, me // count, scaled_ref, low_ref, operands, outs)
+    backward(0, scaled_ref, low_ref, operands, outs)
 
 
 def combine_kernel(count, capacity, *refs):
@@ -320,11 +306,7 @@
     def put_second(value):
         dsecond_ref[...] = value + dsecond_before[...]
 
-    backward(1, half, scaled_ref, low_ref, operands, (put_cotangent, put_first, put_second))
-
-
-vmem = pl.BlockSpec(memory_space=pltpu.VMEM)
-hbm = pl.BlockSpec(memory_space=pltpu.HBM)
+    backward(1, scaled_ref, low_ref, operands, (put_cotangent, put_first, put_second))
 
 
 def gathered(
@@ -347,23 +329,23 @@
     def swap(array, distance):
         return lax.ppermute(array, "expert", [(i, i ^ distance) for i in range(count)])
 
-    def call(limit, kernel, outs, ins, scratch, *operands, results=vmem):
+    def call(limit, kernel, outs, spaces, scratch, *operands, held_out=pltpu.VMEM):
         return pl.pallas_call(
             kernel,
-            out_shape=tuple(jax.ShapeDtypeStruct(*out) for out in outs),
-            in_specs=ins,
-            out_specs=(results,) * len(outs),
+            out_shape=tuple(held_out(*out) for out in outs),
+            in_specs=[pl.BlockSpec(memory_space=space) for space in spaces],
+            out_specs=(pl.BlockSpec(memory_space=pltpu.VMEM),) * len(outs),
             scratch_shapes=scratch,
             compiler_params=pltpu.CompilerParams(vmem_limit_bytes=limit * mebibyte),
             name=getattr(kernel, "func", kernel).__name__,
-        )(*operands)
+        )(*map(pltpu.with_memory_space_constraint, operands, spaces))
 
     route_rows = route.T
     payload, wanted = call(
-        60,
+        8,
         pack_kernel,
         [((tokens, width + lanes), bf16), (route_rows.shape, jnp.int32)],
-        [hbm] * 3,
+        [pltpu.HBM] * 3,
         [
             pltpu.VMEM(route_rows.shape, jnp.int32),
             pltpu.VMEM(route_rows.shape, bf16),
@@ -373,20 +355,21 @@
         route_rows,
         routing_weights.T,
     )
-    hidden_rows = hidden.reshape(slots, hidden_width)
-    weights = (down_weight[0], first_adapter_factors[0].T, second_adapter_factors[0])
-    steps = len(pieces(width, 512))
-    low, low_late, out, out_late = call(
-        62,
+    parameters = (
+        hidden.reshape(slots, hidden_width),
+        down_weight[0],
+        first_adapter_factors[0].T,
+        second_adapter_factors[0],
+    )
+    low, low_late, out, out_late, *held = call(
+        24,
         forward_kernel,
-        [((slots // 2, rank), bf16)] * 2 + [((slots // 2, width), f32)] * 2,
-        [hbm] * 4,
-        [pltpu.VMEM(array.shape, bf16) for array in (hidden_rows, *weights)]
-        + [pltpu.VMEM((slots, rank), bf16), pltpu.VMEM((slots, width), f32)]
-        + [pltpu.SemaphoreType.DMA((4 + steps,)), pltpu.SemaphoreType.DMA((2 + 2 * steps,))],
-        hidden_rows,
-        *weights,
-        results=hbm,
+        [((slots // 2, rank), bf16)] * 2
+        + [((slots // 2, width), f32)] * 2
+        + [(array.shape, bf16) for array in parameters],
+        [pltpu.HBM] * 4,
+        [pltpu.SemaphoreType.DMA((4 + len(pieces(width, 512)),))],
+        *parameters,
     )
 
     blocks = {0: payload}
@@ -396,25 +379,24 @@
     for d in far:
         blocks[d] = swap(payload, d)
     blocks[2] = swap(payload, 2)
-    blocks[half], out, low = lax.optimization_barrier((blocks[half], out, low))
+    for d in far:
+        blocks[d], out, low = lax.optimization_barrier((blocks[d], out, low))
     for d in far:
         blocks[d + 2] = swap(blocks[d], 2)
     for d in [0] + near:
         blocks[d + 1] = swap(blocks[d], 1)
         blocks[d + 3] = swap(blocks[d + 2], 1)
-    blocks[late[-1]], out = lax.optimization_barrier((blocks[late[-1]], out))
     grads = [((rank, hidden_width), f32), ((rank, width), f32)]
     *partial, pair = call(
         24,
         functools.partial(first_kernel, half, capacity),
         [((slots // 2, hidden_width), bf16), *grads, ((half, lanes), f32)],
-        [vmem] * (half + 6),
+        [pltpu.VMEM] * (half + 6),
         [pltpu.VMEM((slots // 2, width), bf16)],
         *[blocks[s] for s in range(half)],
         out,
         low,
-        hidden_rows,
-        *weights,
+        *held,
     )
     for d in late:
         blocks[d + 2], partial, pair = lax.optimization_barrier((blocks[d + 2], partial, pair))
@@ -424,7 +406,7 @@
         24,
         functools.partial(combine_kernel, half, capacity),
         [((slots // 2, width), bf16), ((count, lanes), f32)],
-        [vmem] * (half + 2),
+        [pltpu.VMEM] * (half + 2),
         [],
         *[blocks[s] for s in range(half, count)],
         out_late,
@@ -434,19 +416,22 @@
         24,
         functools.partial(last_kernel, half),
         [((slots, hidden_width), bf16), *grads],
-        [vmem] * 9,
+        [pltpu.VMEM] * 9,
         [],
         scaled,
         low_late,
-        hidden_rows,
-        *weights,
+        *held,
         *partial,
+        held_out=jax.ShapeDtypeStruct,
     )
 
     distance = lax.broadcasted_iota(jnp.int32, pair.shape, 0)
     moved = [swap(pair, d) for d in (1, 2, 3)]
     for d, values in zip((1, 2, 3), moved):
         pair = jnp.where(jnp.bitwise_and(distance, 3) == d, values, pair)
+    pair, cotangent, dfirst, dsecond = lax.optimization_barrier(
+        (pair, cotangent, dfirst, dsecond)
+    )
     moved = [swap(pair, d) for d in far]
     for d, values in zip(far, moved):
         pair = jnp.where(distance - jnp.bitwise_and(distance, 3) == d, values, pair)

time: 45.8 us -> 41.5 us (0.906)
  waiting for transfers between devices: 5.16 us -> 9.6 us
  local copies, waits for them, and re-layouts: 4.13 us -> 0 us
  starting transfers between devices: 22.5 us -> 19.8 us
  Pallas kernels: 12.1 us -> 10.4 us
    ppermute x21, waiting for transfers between devices: 5.16 us -> 9.6 us  [swap(): lax.ppermute(array, 'expert', [(i, i ^ distance) for i in range(count)])]
    unnamed x22 -> x0, local copies, waits for them, and re-layouts: 4.13 us -> none
    ppermute x21, starting transfers between devices: 22.5 us -> 19.8 us  [swap(): lax.ppermute(array, 'expert', [(i, i ^ distance) for i in range(count)])]
    pallas_call x5, Pallas kernels: 12.1 us -> 10.4 us  [call(): pl.pallas_call(kernel, out_shape=tuple((held_out(*out) for out in outs)),...]
  transfers between devices with their start and end apart: 21 -> 21, of which waited for: 5 -> 10; matrix products, arithmetic and copies ran while one was open for 0% -> 0% of each run, Pallas kernels for 21% -> 21%
where the time goes in v3:
time: 41.5 us; the launch traced here: 41.3 us
  starting transfers between devices  19.8 us (48%)
  Pallas kernels  10.4 us (25%)
  waiting for transfers between devices  9.6 us (23%)
  other arithmetic  0.79 us (2%)
  between operations  0.7 us (2%)
    ppermute x21, starting transfers between devices, swap(): lax.ppermute(array, 'expert', [(i, i ^ distance) for i in range(count)])  19.8 us
    pallas_call x5, Pallas kernels, call(): pl.pallas_call(kernel, out_shape=tuple((held_out(*out) for out in outs)),...  10.4 us
    ppermute x21, waiting for transfers between devices, swap(): lax.ppermute(array, 'expert', [(i, i ^ distance) for i in range(count)])  9.6 us
  transfers between devices with their start and end apart: 21, of which 10 were waited for; matrix products, arithmetic and copies ran while one was open for 0% of the time, Pallas kernels for 21%

profile of v3, /device:TPU:0, one launch (start us, length us, event | category | flops | bytes accessed | tf_op | source)
XLA Modules:
  0.0 41.3 jit_solution(15874965730784439590)
XLA Ops:
  0.6 1.0 %pack_kernel.1 = (bf16[32,2176]{1,0:T(8,128)(2,1)S(1)}, s32[8,32]{1,0:T(8,128)S(1)}) custom-call(bf16[32,2048]{1,0:T(8,128)(2,1)} %cotangent_hbm.1, s32[8,32]{1,0:T(8,128)} %bitcast.18, bf16[8,32]{1,0:T(8,128)(2,1)} %bitcast.20), custom_call_target="tpu_custom_call" | custom-call | tf_op jit(solution)/shard_map/pack_kernel/pallas_call | solution.py:333
  1.6 3.1 %collective-permute-start.1 = (bf16[32,2176]{1,0:T(8,128)(2,1)S(1)}, bf16[32,2176]{1,0:T(8,128)(2,1)S(1)}, u32[]{:S(2)}, u32[]{:S(2)}) collective-permute-start(bf16[32,2176]{1,0:T(8,128)(2,1)S(1)} %get-tuple-element.46.refs_0_), channel_id=1, source_target_pairs={{0,4},{1,5},{2,6},{3,7},{4,0},{5,1},{6,2},{7,3},{8,12},{9,13},{10,... | collective-permute-start | bytes 417800 | tf_op jit(solution)/shard_map/ppermute | solution.py:330
  4.7 2.6 %collective-permute-start = (bf16[32,2176]{1,0:T(8,128)(2,1)S(1)}, bf16[32,2176]{1,0:T(8,128)(2,1)S(1)}, u32[]{:S(2)}, u32[]{:S(2)}) collective-permute-start(bf16[32,2176]{1,0:T(8,128)(2,1)S(1)} %get-tuple-element.46.refs_0_), channel_id=1, source_target_pairs={{0,8},{1,9},{2,10},{3,11},{4,12},{5,13},{6,14},{7,15},{8,0},{9,1},... | collective-permute-start | bytes 417800 | tf_op jit(solution)/shard_map/ppermute | solution.py:330
  7.3 1.5 %collective-permute-start.5 = (bf16[32,2176]{1,0:T(8,128)(2,1)S(1)}, bf16[32,2176]{1,0:T(8,128)(2,1)S(1)}, u32[]{:S(2)}, u32[]{:S(2)}) collective-permute-start(bf16[32,2176]{1,0:T(8,128)(2,1)S(1)} %get-tuple-element.46.refs_0_), channel_id=1, source_target_pairs={{0,2},{1,3},{2,0},{3,1},{4,6},{5,7},{6,4},{7,5},{8,10},{9,11},{10,... | collective-permute-start | bytes 417800 | tf_op jit(solution)/shard_map/ppermute | solution.py:330
  8.8 3.9 %forward_kernel.1 = (bf16[192,32]{1,0:T(8,128)(2,1)S(1)}, bf16[192,32]{1,0:T(8,128)(2,1)S(1)}, f32[192,2048]{1,0:T(8,128)S(1)}, f32[192,2048]{1,0:T(8,128)S(1)},...) custom-call(bf16[384,768]{1,0:T(8,128)(2,1)} %bitcast.15, ...), custom_call_target="tpu_custom_call" | custom-call | tf_op jit(solution)/shard_map/forward_kernel/pallas_call | solution.py:333
  12.7 0.0 collective-permute-done.1.refs_4_
  12.7 0.6 %collective-permute-start.8 = (bf16[32,2176]{1,0:T(8,128)(2,1)S(1)}, bf16[32,2176]{1,0:T(8,128)(2,1)S(1)}, u32[]{:S(2)}, u32[]{:S(2)}) collective-permute-start(bf16[32,2176]{1,0:T(8,128)(2,1)S(1)} %collective-permute-done.1.refs_4_), channel_id=1, source_target_pairs={{0,2},{1,3},{2,0},{3,1},{4,6},{5,7},{6,4},{7,5},{8,10},{9,11},{10,... | collective-permute-start | bytes 417800 | tf_op jit(solution)/shard_map/ppermute | solution.py:330
  13.3 2.0 %collective-permute-start.10 = (bf16[32,2176]{1,0:T(8,128)(2,1)S(1)}, bf16[32,2176]{1,0:T(8,128)(2,1)S(1)}, u32[]{:S(2)}, u32[]{:S(2)}) collective-permute-start(bf16[32,2176]{1,0:T(8,128)(2,1)S(1)} %get-tuple-element.46.refs_0_), channel_id=1, source_target_pairs={{0,12},{1,13},{2,14},{3,15},{4,8},{5,9},{6,10},{7,11},{8,4},{9,5},... | collective-permute-start | bytes 417800 | tf_op jit(solution)/shard_map/ppermute | solution.py:330
  15.4 0.0 collective-permute-start.4
  15.4 0.0 collective-permute-done.refs_0_
  15.4 0.5 %collective-permute-start.7 = (bf16[32,2176]{1,0:T(8,128)(2,1)S(1)}, bf16[32,2176]{1,0:T(8,128)(2,1)S(1)}, u32[]{:S(2)}, u32[]{:S(2)}) collective-permute-start(bf16[32,2176]{1,0:T(8,128)(2,1)S(1)} %collective-permute-done.1.refs_4_), channel_id=1, source_target_pairs={{0,1},{1,0},{2,3},{3,2},{4,5},{5,4},{6,7},{7,6},{8,9},{9,8},{10,11... | collective-permute-start | bytes 417800 | tf_op jit(solution)/shard_map/ppermute | solution.py:330
  15.9 0.0 collective-permute-done.5.refs_2_
  15.9 0.1 collective-permute-start.6
  16.0 1.9 %collective-permute-done.8.refs_6_ = bf16[32,2176]{1,0:T(8,128)(2,1)S(1)} collective-permute-done((bf16[32,2176]{1,0:T(8,128)(2,1)S(1)}, bf16[32,2176]{1,0:T(8,128)(2,1)S(1)}, u32[]{:S(2)}, u32[]{:S(2)}) %collective-permute-start.8) | collective-permute-done | bytes 139296 | tf_op jit(solution)/shard_map/ppermute | solution.py:330
  17.8 0.0 collective-permute-start.9
  17.8 2.4 %collective-permute-done.10.refs_4_ = bf16[32,2176]{1,0:T(8,128)(2,1)S(1)} collective-permute-done((bf16[32,2176]{1,0:T(8,128)(2,1)S(1)}, bf16[32,2176]{1,0:T(8,128)(2,1)S(1)}, u32[]{:S(2)}, u32[]{:S(2)}) %collective-permute-start.10) | collective-permute-done | bytes 139296 | tf_op jit(solution)/shard_map/ppermute | solution.py:330
  20.3 1.5 %collective-permute-start.3 = (bf16[32,2176]{1,0:T(8,128)(2,1)S(1)}, bf16[32,2176]{1,0:T(8,128)(2,1)S(1)}, u32[]{:S(2)}, u32[]{:S(2)}) collective-permute-start(bf16[32,2176]{1,0:T(8,128)(2,1)S(1)} %collective-permute-done.refs_0_), channel_id=1, source_target_pairs={{0,2},{1,3},{2,0},{3,1},{4,6},{5,7},{6,4},{7,5},{8,10},{9,11},{10,... | collective-permute-start | bytes 417800 | tf_op jit(solution)/shard_map/ppermute | solution.py:330
  21.8 0.0 collective-permute-done.4.refs_1_
  21.8 0.5 %collective-permute-start.13 = (bf16[32,2176]{1,0:T(8,128)(2,1)S(1)}, bf16[32,2176]{1,0:T(8,128)(2,1)S(1)}, u32[]{:S(2)}, u32[]{:S(2)}) collective-permute-start(bf16[32,2176]{1,0:T(8,128)(2,1)S(1)} %collective-permute-done.10.refs_4_), channel_id=1, source_target_pairs={{0,2},{1,3},{2,0},{3,1},{4,6},{5,7},{6,4},{7,5},{8,10},{9,11},{10,... | collective-permute-start | bytes 417800 | tf_op jit(solution)/shard_map/ppermute | solution.py:330
  22.3 0.0 collective-permute-done.7.refs_5_
  22.3 0.0 collective-permute-start.12
  22.3 0.0 collective-permute-done.6.refs_3_
  22.3 0.5 %collective-permute-start.2 = (bf16[32,2176]{1,0:T(8,128)(2,1)S(1)}, bf16[32,2176]{1,0:T(8,128)(2,1)S(1)}, u32[]{:S(2)}, u32[]{:S(2)}) collective-permute-start(bf16[32,2176]{1,0:T(8,128)(2,1)S(1)} %collective-permute-done.refs_0_), channel_id=1, source_target_pairs={{0,1},{1,0},{2,3},{3,2},{4,5},{5,4},{6,7},{7,6},{8,9},{9,8},{10,11... | collective-permute-start | bytes 417800 | tf_op jit(solution)/shard_map/ppermute | solution.py:330
  22.8 0.0 collective-permute-done.9.refs_7_
  22.8 2.2 %first_kernel.1 = (bf16[192,768]{1,0:T(8,128)(2,1)S(1)}, f32[32,768]{1,0:T(8,128)S(1)}, f32[32,2048]{1,0:T(8,128)S(1)}, f32[8,128]{1,0:T(8,128)S(1)}) custom-call(bf16[32,2176]{1,0:T(8,128)(2,1)S(1)} %get-tuple-element.46.refs_0_, bf16[32,2176]{1,0:T(8,128)(2,1)S(1)} %collective-permute-done.4.refs_1_, bf16[32,2176]{1,0:T(8,128)(2,1)S(1)} %collective-permute-done.5.refs_2_, ...), custom_call_target="tpu_custom_call" | custom-call | tf_op jit(solution)/shard_map/first_kernel/pallas_call | solution.py:333
  25.0 0.4 collective-permute-done.3.refs_2_
  25.4 1.5 %collective-permute-done.13.refs_6_ = bf16[32,2176]{1,0:T(8,128)(2,1)S(1)} collective-permute-done((bf16[32,2176]{1,0:T(8,128)(2,1)S(1)}, bf16[32,2176]{1,0:T(8,128)(2,1)S(1)}, u32[]{:S(2)}, u32[]{:S(2)}) %collective-permute-start.13) | collective-permute-done | bytes 139296 | tf_op jit(solution)/shard_map/ppermute | solution.py:330
  26.9 0.0 collective-permute-start.14
  26.9 0.5 %collective-permute-start.11 = (bf16[32,2176]{1,0:T(8,128)(2,1)S(1)}, bf16[32,2176]{1,0:T(8,128)(2,1)S(1)}, u32[]{:S(2)}, u32[]{:S(2)}) collective-permute-start(bf16[32,2176]{1,0:T(8,128)(2,1)S(1)} %collective-permute-done.3.refs_2_), channel_id=1, source_target_pairs={{0,1},{1,0},{2,3},{3,2},{4,5},{5,4},{6,7},{7,6},{8,9},{9,8},{10,11... | collective-permute-start | bytes 417800 | tf_op jit(solution)/shard_map/ppermute | solution.py:330
  27.4 0.0 collective-permute-done.12.refs_5_
  27.4 0.0 collective-permute-done.2.refs_1_
  27.4 0.8 %collective-permute-done.14.refs_7_ = bf16[32,2176]{1,0:T(8,128)(2,1)S(1)} collective-permute-done((bf16[32,2176]{1,0:T(8,128)(2,1)S(1)}, bf16[32,2176]{1,0:T(8,128)(2,1)S(1)}, u32[]{:S(2)}, u32[]{:S(2)}) %collective-permute-start.14) | collective-permute-done | bytes 139296 | tf_op jit(solution)/shard_map/ppermute | solution.py:330
  28.3 0.2 collective-permute-done.11.refs_3_
  28.5 0.8 %combine_kernel.1 = (bf16[192,2048]{1,0:T(8,128)(2,1)S(1)}, f32[16,128]{1,0:T(8,128)S(1)}) custom-call(bf16[32,2176]{1,0:T(8,128)(2,1)S(1)} %collective-permute-done.refs_0_, bf16[32,2176]{1,0:T(8,128)(2,1)S(1)} %collective-permute-done.2.refs_1_, bf16[32,2176]{1,0:T(8,128)(2,1)S(1)} %collective-permute-done.3.refs_2_, ...), custom_call_target="tpu_custom_call" | custom-call | tf_op jit(solution)/shard_map/combine_kernel/pallas_call | solution.py:333
  29.2 1.3 %collective-permute-start.15 = (f32[16,128]{1,0:T(8,128)S(1)}, f32[16,128]{1,0:T(8,128)S(1)}, u32[]{:S(2)}, u32[]{:S(2)}) collective-permute-start(f32[16,128]{1,0:T(8,128)S(1)} %get-tuple-element.74), channel_id=1, source_target_pairs={{0,3},{1,2},{2,1},{3,0},{4,7},{5,6},{6,5},{7,4},{8,11},{9,10},{10,... | collective-permute-start | bytes 24584 | tf_op jit(solution)/shard_map/ppermute | solution.py:330
  30.6 0.6 %collective-permute-start.16 = (f32[16,128]{1,0:T(8,128)S(1)}, f32[16,128]{1,0:T(8,128)S(1)}, u32[]{:S(2)}, u32[]{:S(2)}) collective-permute-start(f32[16,128]{1,0:T(8,128)S(1)} %get-tuple-element.74), channel_id=1, source_target_pairs={{0,2},{1,3},{2,0},{3,1},{4,6},{5,7},{6,4},{7,5},{8,10},{9,11},{10,... | collective-permute-start | bytes 24584 | tf_op jit(solution)/shard_map/ppermute | solution.py:330
  31.2 0.0 collective-permute-start.17
  31.2 2.5 %last_kernel.1 = (bf16[384,768]{1,0:T(8,128)(2,1)}, f32[32,768]{1,0:T(8,128)}, f32[32,2048]{1,0:T(8,128)}) custom-call(bf16[192,2048]{1,0:T(8,128)(2,1)S(1)} %get-tuple-element.75.scaled_ref, bf16[192,32]{1,0:T(8,128)(2,1)S(1)} %get-tuple-element.76.low_ref, bf16[384,768]{1,0:T(8,128)(2,1)S(1)} %get-tuple-element.57.refs_10_.refs_0_, ...), custom_call_target="tpu_custom_call" | custom-call | tf_op jit(solution)/shard_map/last_kernel/pallas_call | solution.py:333
  33.7 0.0 collective-permute-done.15
  33.7 0.5 %collective-permute-done.16 = f32[16,128]{1,0:T(8,128)S(1)} collective-permute-done((f32[16,128]{1,0:T(8,128)S(1)}, f32[16,128]{1,0:T(8,128)S(1)}, u32[]{:S(2)}, u32[]{:S(2)}) %collective-permute-start.16) | collective-permute-done | bytes 8224 | tf_op jit(solution)/shard_map/ppermute | solution.py:330
  34.2 0.0 collective-permute-done.17
  34.2 0.1 select_select_fusion
  34.3 1.5 %collective-permute-start.18 = (f32[16,128]{1,0:T(8,128)S(1)}, f32[16,128]{1,0:T(8,128)S(1)}, u32[]{:S(2)}, u32[]{:S(2)}) collective-permute-start(f32[16,128]{1,0:T(8,128)S(1)} %select_select_fusion), channel_id=1, source_target_pairs={{0,12},{1,13},{2,14},{3,15},{4,8},{5,9},{6,10},{7,11},{8,4},{9,5},... | collective-permute-start | bytes 24584 | tf_op jit(solution)/shard_map/ppermute | solution.py:330
  35.8 1.1 %collective-permute-start.19 = (f32[16,128]{1,0:T(8,128)S(1)}, f32[16,128]{1,0:T(8,128)S(1)}, u32[]{:S(2)}, u32[]{:S(2)}) collective-permute-start(f32[16,128]{1,0:T(8,128)S(1)} %select_select_fusion), channel_id=1, source_target_pairs={{0,8},{1,9},{2,10},{3,11},{4,12},{5,13},{6,14},{7,15},{8,0},{9,1},... | collective-permute-start | bytes 24584 | tf_op jit(solution)/shard_map/ppermute | solution.py:330
  36.9 1.7 %collective-permute-start.20 = (f32[16,128]{1,0:T(8,128)S(1)}, f32[16,128]{1,0:T(8,128)S(1)}, u32[]{:S(2)}, u32[]{:S(2)}) collective-permute-start(f32[16,128]{1,0:T(8,128)S(1)} %select_select_fusion), channel_id=1, source_target_pairs={{0,4},{1,5},{2,6},{3,7},{4,0},{5,1},{6,2},{7,3},{8,12},{9,13},{10,... | collective-permute-start | bytes 24584 | tf_op jit(solution)/shard_map/ppermute | solution.py:330
  38.7 1.1 %collective-permute-done.18 = f32[16,128]{1,0:T(8,128)S(1)} collective-permute-done((f32[16,128]{1,0:T(8,128)S(1)}, f32[16,128]{1,0:T(8,128)S(1)}, u32[]{:S(2)}, u32[]{:S(2)}) %collective-permute-start.18) | collective-permute-done | bytes 8224 | tf_op jit(solution)/shard_map/ppermute | solution.py:330
  39.7 0.6 %collective-permute-done.19 = f32[16,128]{1,0:T(8,128)S(1)} collective-permute-done((f32[16,128]{1,0:T(8,128)S(1)}, f32[16,128]{1,0:T(8,128)S(1)}, u32[]{:S(2)}, u32[]{:S(2)}) %collective-permute-start.19) | collective-permute-done | bytes 8224 | tf_op jit(solution)/shard_map/ppermute | solution.py:330
  40.3 0.2 collective-permute-done.20
  40.6 0.1 slice_select_fusion
  40.7 0.6 %select_reduce_fusion = f32[8,32]{1,0:T(8,128)} fusion(f32[16,32]{1,0:T(8,128)S(1)} %slice_select_fusion, s32[8,32]{1,0:T(8,128)S(1)} %get-tuple-element.86), kind=kLoop, calls=%fused_computation | loop fusion | flops 12032 | bytes 4096 | tf_op jit(solution)/shard_map/reduce_sum | solution.py:439
  (4 shorter events, 0.0 us)
Async XLA Ops:
  1.6 11.1 %collective-permute-start.1 = (bf16[32,2176]{1,0:T(8,128)(2,1)S(1)}, bf16[32,2176]{1,0:T(8,128)(2,1)S(1)}, u32[]{:S(2)}, u32[]{:S(2)}) collective-permute-start(bf16[32,2176]{1,0:T(8,128)(2,1)S(1)} %get-tuple-element.46.refs_0_), channel_id=1, source_target_pairs={{0,4},{1,5},{2,6},{3,7},{4,0},{5,1},{6,2},{7,3},{8,12},{9,13},{10,... | collective-permute-start | bytes 417800 | tf_op jit(solution)/shard_map/ppermute | solution.py:330
  4.7 10.7 %collective-permute-start = (bf16[32,2176]{1,0:T(8,128)(2,1)S(1)}, bf16[32,2176]{1,0:T(8,128)(2,1)S(1)}, u32[]{:S(2)}, u32[]{:S(2)}) collective-permute-start(bf16[32,2176]{1,0:T(8,128)(2,1)S(1)} %get-tuple-element.46.refs_0_), channel_id=1, source_target_pairs={{0,8},{1,9},{2,10},{3,11},{4,12},{5,13},{6,14},{7,15},{8,0},{9,1},... | collective-permute-start | bytes 417800 | tf_op jit(solution)/shard_map/ppermute | solution.py:330
  7.3 8.6 %collective-permute-start.5 = (bf16[32,2176]{1,0:T(8,128)(2,1)S(1)}, bf16[32,2176]{1,0:T(8,128)(2,1)S(1)}, u32[]{:S(2)}, u32[]{:S(2)}) collective-permute-start(bf16[32,2176]{1,0:T(8,128)(2,1)S(1)} %get-tuple-element.46.refs_0_), channel_id=1, source_target_pairs={{0,2},{1,3},{2,0},{3,1},{4,6},{5,7},{6,4},{7,5},{8,10},{9,11},{10,... | collective-permute-start | bytes 417800 | tf_op jit(solution)/shard_map/ppermute | solution.py:330
  12.7 5.1 %collective-permute-start.8 = (bf16[32,2176]{1,0:T(8,128)(2,1)S(1)}, bf16[32,2176]{1,0:T(8,128)(2,1)S(1)}, u32[]{:S(2)}, u32[]{:S(2)}) collective-permute-start(bf16[32,2176]{1,0:T(8,128)(2,1)S(1)} %collective-permute-done.1.refs_4_), channel_id=1, source_target_pairs={{0,2},{1,3},{2,0},{3,1},{4,6},{5,7},{6,4},{7,5},{8,10},{9,11},{10,... | collective-permute-start | bytes 417800 | tf_op jit(solution)/shard_map/ppermute | solution.py:330
  13.3 7.0 %collective-permute-start.10 = (bf16[32,2176]{1,0:T(8,128)(2,1)S(1)}, bf16[32,2176]{1,0:T(8,128)(2,1)S(1)}, u32[]{:S(2)}, u32[]{:S(2)}) collective-permute-start(bf16[32,2176]{1,0:T(8,128)(2,1)S(1)} %get-tuple-element.46.refs_0_), channel_id=1, source_target_pairs={{0,12},{1,13},{2,14},{3,15},{4,8},{5,9},{6,10},{7,11},{8,4},{9,5},... | collective-permute-start | bytes 417800 | tf_op jit(solution)/shard_map/ppermute | solution.py:330
  15.4 6.4 %collective-permute-start.4 = (bf16[32,2176]{1,0:T(8,128)(2,1)S(1)}, bf16[32,2176]{1,0:T(8,128)(2,1)S(1)}, u32[]{:S(2)}, u32[]{:S(2)}) collective-permute-start(bf16[32,2176]{1,0:T(8,128)(2,1)S(1)} %get-tuple-element.46.refs_0_), channel_id=1, source_target_pairs={{0,1},{1,0},{2,3},{3,2},{4,5},{5,4},{6,7},{7,6},{8,9},{9,8},{10,11... | collective-permute-start | bytes 417800 | tf_op jit(solution)/shard_map/ppermute | solution.py:330
  15.4 6.9 %collective-permute-start.7 = (bf16[32,2176]{1,0:T(8,128)(2,1)S(1)}, bf16[32,2176]{1,0:T(8,128)(2,1)S(1)}, u32[]{:S(2)}, u32[]{:S(2)}) collective-permute-start(bf16[32,2176]{1,0:T(8,128)(2,1)S(1)} %collective-permute-done.1.refs_4_), channel_id=1, source_target_pairs={{0,1},{1,0},{2,3},{3,2},{4,5},{5,4},{6,7},{7,6},{8,9},{9,8},{10,11... | collective-permute-start | bytes 417800 | tf_op jit(solution)/shard_map/ppermute | solution.py:330
  15.9 6.4 %collective-permute-start.6 = (bf16[32,2176]{1,0:T(8,128)(2,1)S(1)}, bf16[32,2176]{1,0:T(8,128)(2,1)S(1)}, u32[]{:S(2)}, u32[]{:S(2)}) collective-permute-start(bf16[32,2176]{1,0:T(8,128)(2,1)S(1)} %collective-permute-done.5.refs_2_), channel_id=1, source_target_pairs={{0,1},{1,0},{2,3},{3,2},{4,5},{5,4},{6,7},{7,6},{8,9},{9,8},{10,11... | collective-permute-start | bytes 417800 | tf_op jit(solution)/shard_map/ppermute | solution.py:330
  17.8 5.0 %collective-permute-start.9 = (bf16[32,2176]{1,0:T(8,128)(2,1)S(1)}, bf16[32,2176]{1,0:T(8,128)(2,1)S(1)}, u32[]{:S(2)}, u32[]{:S(2)}) collective-permute-start(bf16[32,2176]{1,0:T(8,128)(2,1)S(1)} %collective-permute-done.8.refs_6_), channel_id=1, source_target_pairs={{0,1},{1,0},{2,3},{3,2},{4,5},{5,4},{6,7},{7,6},{8,9},{9,8},{10,11... | collective-permute-start | bytes 417800 | tf_op jit(solution)/shard_map/ppermute | solution.py:330
  20.3 5.1 %collective-permute-start.3 = (bf16[32,2176]{1,0:T(8,128)(2,1)S(1)}, bf16[32,2176]{1,0:T(8,128)(2,1)S(1)}, u32[]{:S(2)}, u32[]{:S(2)}) collective-permute-start(bf16[32,2176]{1,0:T(8,128)(2,1)S(1)} %collective-permute-done.refs_0_), channel_id=1, source_target_pairs={{0,2},{1,3},{2,0},{3,1},{4,6},{5,7},{6,4},{7,5},{8,10},{9,11},{10,... | collective-permute-start | bytes 417800 | tf_op jit(solution)/shard_map/ppermute | solution.py:330
  21.8 5.1 %collective-permute-start.13 = (bf16[32,2176]{1,0:T(8,128)(2,1)S(1)}, bf16[32,2176]{1,0:T(8,128)(2,1)S(1)}, u32[]{:S(2)}, u32[]{:S(2)}) collective-permute-start(bf16[32,2176]{1,0:T(8,128)(2,1)S(1)} %collective-permute-done.10.refs_4_), channel_id=1, source_target_pairs={{0,2},{1,3},{2,0},{3,1},{4,6},{5,7},{6,4},{7,5},{8,10},{9,11},{10,... | collective-permute-start | bytes 417800 | tf_op jit(solution)/shard_map/ppermute | solution.py:330
  22.3 5.1 %collective-permute-start.12 = (bf16[32,2176]{1,0:T(8,128)(2,1)S(1)}, bf16[32,2176]{1,0:T(8,128)(2,1)S(1)}, u32[]{:S(2)}, u32[]{:S(2)}) collective-permute-start(bf16[32,2176]{1,0:T(8,128)(2,1)S(1)} %collective-permute-done.10.refs_4_), channel_id=1, source_target_pairs={{0,1},{1,0},{2,3},{3,2},{4,5},{5,4},{6,7},{7,6},{8,9},{9,8},{10,11... | collective-permute-start | bytes 417800 | tf_op jit(solution)/shard_map/ppermute | solution.py:330
  22.3 5.1 %collective-permute-start.2 = (bf16[32,2176]{1,0:T(8,128)(2,1)S(1)}, bf16[32,2176]{1,0:T(8,128)(2,1)S(1)}, u32[]{:S(2)}, u32[]{:S(2)}) collective-permute-start(bf16[32,2176]{1,0:T(8,128)(2,1)S(1)} %collective-permute-done.refs_0_), channel_id=1, source_target_pairs={{0,1},{1,0},{2,3},{3,2},{4,5},{5,4},{6,7},{7,6},{8,9},{9,8},{10,11... | collective-permute-start | bytes 417800 | tf_op jit(solution)/shard_map/ppermute | solution.py:330
  26.9 1.4 %collective-permute-start.14 = (bf16[32,2176]{1,0:T(8,128)(2,1)S(1)}, bf16[32,2176]{1,0:T(8,128)(2,1)S(1)}, u32[]{:S(2)}, u32[]{:S(2)}) collective-permute-start(bf16[32,2176]{1,0:T(8,128)(2,1)S(1)} %collective-permute-done.13.refs_6_), channel_id=1, source_target_pairs={{0,1},{1,0},{2,3},{3,2},{4,5},{5,4},{6,7},{7,6},{8,9},{9,8},{10,11... | collective-permute-start | bytes 417800 | tf_op jit(solution)/shard_map/ppermute | solution.py:330
  26.9 1.6 %collective-permute-start.11 = (bf16[32,2176]{1,0:T(8,128)(2,1)S(1)}, bf16[32,2176]{1,0:T(8,128)(2,1)S(1)}, u32[]{:S(2)}, u32[]{:S(2)}) collective-permute-start(bf16[32,2176]{1,0:T(8,128)(2,1)S(1)} %collective-permute-done.3.refs_2_), channel_id=1, source_target_pairs={{0,1},{1,0},{2,3},{3,2},{4,5},{5,4},{6,7},{7,6},{8,9},{9,8},{10,11... | collective-permute-start | bytes 417800 | tf_op jit(solution)/shard_map/ppermute | solution.py:330
  29.2 4.5 %collective-permute-start.15 = (f32[16,128]{1,0:T(8,128)S(1)}, f32[16,128]{1,0:T(8,128)S(1)}, u32[]{:S(2)}, u32[]{:S(2)}) collective-permute-start(f32[16,128]{1,0:T(8,128)S(1)} %get-tuple-element.74), channel_id=1, source_target_pairs={{0,3},{1,2},{2,1},{3,0},{4,7},{5,6},{6,5},{7,4},{8,11},{9,10},{10,... | collective-permute-start | bytes 24584 | tf_op jit(solution)/shard_map/ppermute | solution.py:330
  30.6 3.7 %collective-permute-start.16 = (f32[16,128]{1,0:T(8,128)S(1)}, f32[16,128]{1,0:T(8,128)S(1)}, u32[]{:S(2)}, u32[]{:S(2)}) collective-permute-start(f32[16,128]{1,0:T(8,128)S(1)} %get-tuple-element.74), channel_id=1, source_target_pairs={{0,2},{1,3},{2,0},{3,1},{4,6},{5,7},{6,4},{7,5},{8,10},{9,11},{10,... | collective-permute-start | bytes 24584 | tf_op jit(solution)/shard_map/ppermute | solution.py:330
  31.2 3.0 %collective-permute-start.17 = (f32[16,128]{1,0:T(8,128)S(1)}, f32[16,128]{1,0:T(8,128)S(1)}, u32[]{:S(2)}, u32[]{:S(2)}) collective-permute-start(f32[16,128]{1,0:T(8,128)S(1)} %get-tuple-element.74), channel_id=1, source_target_pairs={{0,1},{1,0},{2,3},{3,2},{4,5},{5,4},{6,7},{7,6},{8,9},{9,8},{10,11... | collective-permute-start | bytes 24584 | tf_op jit(solution)/shard_map/ppermute | solution.py:330
  34.3 5.5 %collective-permute-start.18 = (f32[16,128]{1,0:T(8,128)S(1)}, f32[16,128]{1,0:T(8,128)S(1)}, u32[]{:S(2)}, u32[]{:S(2)}) collective-permute-start(f32[16,128]{1,0:T(8,128)S(1)} %select_select_fusion), channel_id=1, source_target_pairs={{0,12},{1,13},{2,14},{3,15},{4,8},{5,9},{6,10},{7,11},{8,4},{9,5},... | collective-permute-start | bytes 24584 | tf_op jit(solution)/shard_map/ppermute | solution.py:330
  35.8 4.5 %collective-permute-start.19 = (f32[16,128]{1,0:T(8,128)S(1)}, f32[16,128]{1,0:T(8,128)S(1)}, u32[]{:S(2)}, u32[]{:S(2)}) collective-permute-start(f32[16,128]{1,0:T(8,128)S(1)} %select_select_fusion), channel_id=1, source_target_pairs={{0,8},{1,9},{2,10},{3,11},{4,12},{5,13},{6,14},{7,15},{8,0},{9,1},... | collective-permute-start | bytes 24584 | tf_op jit(solution)/shard_map/ppermute | solution.py:330
  36.9 3.7 %collective-permute-start.20 = (f32[16,128]{1,0:T(8,128)S(1)}, f32[16,128]{1,0:T(8,128)S(1)}, u32[]{:S(2)}, u32[]{:S(2)}) collective-permute-start(f32[16,128]{1,0:T(8,128)S(1)} %select_select_fusion), channel_id=1, source_target_pairs={{0,4},{1,5},{2,6},{3,7},{4,0},{5,1},{6,2},{7,3},{8,12},{9,13},{10,... | collective-permute-start | bytes 24584 | tf_op jit(solution)/shard_map/ppermute | solution.py:330

commit v4 on v3

--- a/solution.py
+++ b/solution.py
@@ -139,42 +139,28 @@
     return [slice(start, start + size) for start in range(0, total, size)]
 
 
+def load_kernel(hidden_hbm, down_hbm, first_hbm, second_hbm, *refs):
+    (hidden, down, first, second), sems = refs[:4], refs[4]
+    slots = hidden.shape[0] // 2
+    half = lax.axis_index("expert") // (lax.axis_size("expert") // 2)
+    pairs = [(down_hbm, down), (first_hbm, first), (second_hbm, second)]
+    for part in (0, 1):
+        base = pl.multiple_of(jnp.bitwise_xor(half, part) * slots, slots)
+        pairs.append((hidden_hbm.at[pl.ds(base, slots), :], hidden.at[pl.ds(slots * part, slots), :]))
+    for copy in start_copies(pairs, sems):
+        copy.wait()
+
+
 def forward_kernel(
-    hidden_hbm,
-    down_hbm,
-    first_hbm,
-    second_hbm,
-    low_one,
-    low_two,
-    out_one,
-    out_two,
-    hidden,
-    down,
-    first,
-    second,
-    sems,
+    hidden, down, first, second, low_one, low_two, out_one, out_two
 ):
     slots = out_one.shape[0]
-    half = lax.axis_index("expert") // (lax.axis_size("expert") // 2)
-    cuts = pieces(out_one.shape[1], 512)
-    parts = [pl.ds(0, slots), pl.ds(slots, slots)]
-    bases = [pl.multiple_of(jnp.bitwise_xor(half, part) * slots, slots) for part in (0, 1)]
-    loads = start_copies(
-        [(hidden_hbm.at[pl.ds(base, slots), :], hidden.at[here, :]) for base, here in zip(bases, parts)]
-        + [(first_hbm, first), (second_hbm, second)]
-        + [(down_hbm.at[:, cut], down.at[:, cut]) for cut in cuts],
-        sems,
-    )
-    for load in loads[:3]:
-        load.wait()
     low = lax.dot_general(
         hidden[...], first[...], over_last, preferred_element_type=jnp.float32
     ).astype(jnp.bfloat16)
     low_one[...] = low[:slots]
     low_two[...] = low[slots:]
-    loads[3].wait()
-    for cut, load in zip(cuts, loads[4:]):
-        load.wait()
+    for cut in pieces(out_one.shape[1], 512):
         values = jnp.dot(
             hidden[...], down[:, cut], preferred_element_type=jnp.float32
         ) + adapter_scale * jnp.dot(low, second[:, cut], preferred_element_type=jnp.float32)
@@ -355,32 +341,41 @@
         route_rows,
         routing_weights.T,
     )
+    blocks = {0: payload}
+    far = [d for d in range(4, count, 4)]
+    near = [d for d in far if d < half]
+    late = [d for d in far if d >= half]
+    direct = [d for d in far if d & (d - 1) == 0]
+    for d in direct[::-1]:
+        blocks[d] = swap(payload, d)
+    blocks[2] = swap(payload, 2)
     parameters = (
         hidden.reshape(slots, hidden_width),
         down_weight[0],
         first_adapter_factors[0].T,
         second_adapter_factors[0],
     )
-    low, low_late, out, out_late, *held = call(
+    held = call(
+        8,
+        load_kernel,
+        [(array.shape, bf16) for array in parameters],
+        [pltpu.HBM] * 4,
+        [pltpu.SemaphoreType.DMA((5,))],
+        *parameters,
+    )
+    blocks[near[0]], held = lax.optimization_barrier((blocks[near[0]], held))
+    low, low_late, out, out_late = call(
         24,
         forward_kernel,
-        [((slots // 2, rank), bf16)] * 2
-        + [((slots // 2, width), f32)] * 2
-        + [(array.shape, bf16) for array in parameters],
-        [pltpu.HBM] * 4,
-        [pltpu.SemaphoreType.DMA((4 + len(pieces(width, 512)),))],
-        *parameters,
-    )
-
-    blocks = {0: payload}
-    far = [d for d in range(4, count, 4)]
-    near = [d for d in far if d < half]
-    late = [d for d in far if d >= half]
+        [((slots // 2, rank), bf16)] * 2 + [((slots // 2, width), f32)] * 2,
+        [pltpu.VMEM] * 4,
+        [],
+        *held,
+    )
+
     for d in far:
-        blocks[d] = swap(payload, d)
-    blocks[2] = swap(payload, 2)
-    for d in far:
-        blocks[d], out, low = lax.optimization_barrier((blocks[d], out, low))
+        if d not in direct:
+            blocks[d] = swap(blocks[half], d - half)
     for d in far:
         blocks[d + 2] = swap(blocks[d], 2)
     for d in [0] + near:
@@ -426,15 +421,15 @@
     )
 
     distance = lax.broadcasted_iota(jnp.int32, pair.shape, 0)
+    moved = [swap(pair, d) for d in far]
+    for d, values in zip(far, moved):
+        pair = jnp.where(distance - jnp.bitwise_and(distance, 3) == d, values, pair)
+    pair, cotangent, dfirst, dsecond = lax.optimization_barrier(
+        (pair, cotangent, dfirst, dsecond)
+    )
     moved = [swap(pair, d) for d in (1, 2, 3)]
     for d, values in zip((1, 2, 3), moved):
         pair = jnp.where(jnp.bitwise_and(distance, 3) == d, values, pair)
-    pair, cotangent, dfirst, dsecond = lax.optimization_barrier(
-        (pair, cotangent, dfirst, dsecond)
-    )
-    moved = [swap(pair, d) for d in far]
-    for d, values in zip(far, moved):
-        pair = jnp.where(distance - jnp.bitwise_and(distance, 3) == d, values, pair)
     hop = lax.broadcasted_iota(jnp.int32, (count, 1, 1), 0)
     gradient = jnp.sum(jnp.where(wanted[None] == hop, pair[:, None, :tokens], 0.0), axis=0)
     return (

time: 41.5 us -> 39.6 us (0.954)
  waiting for transfers between devices: 9.6 us -> 7.06 us
    ppermute x21, waiting for transfers between devices: 9.6 us -> 7.06 us  [swap(): lax.ppermute(array, 'expert', [(i, i ^ distance) for i in range(count)])]
    pallas_call x5 -> x6, Pallas kernels: 10.4 us -> 10.8 us  [call(): pl.pallas_call(kernel, out_shape=tuple((held_out(*out) for out in outs)),...]
  transfers between devices with their start and end apart: 21 -> 21, of which waited for: 10 -> 8; matrix products, arithmetic and copies ran while one was open for 0% -> 0% of each run, Pallas kernels for 21% -> 23%
where the time goes in v4:
time: 39.6 us; the launch traced here: 39.4 us
  starting transfers between devices  19.9 us (50%)
  Pallas kernels  10.8 us (27%)
  waiting for transfers between devices  7.06 us (18%)
  other arithmetic  0.79 us (2%)
  between operations  0.75 us (2%)
    ppermute x21, starting transfers between devices, swap(): lax.ppermute(array, 'expert', [(i, i ^ distance) for i in range(count)])  19.9 us
    pallas_call x6, Pallas kernels, call(): pl.pallas_call(kernel, out_shape=tuple((held_out(*out) for out in outs)),...  10.8 us
    ppermute x21, waiting for transfers between devices, swap(): lax.ppermute(array, 'expert', [(i, i ^ distance) for i in range(count)])  7.06 us
  transfers between devices with their start and end apart: 21, of which 8 were waited for; matrix products, arithmetic and copies ran while one was open for 0% of the time, Pallas kernels for 23%

profile of v4, /device:TPU:0, one launch (start us, length us, event | category | flops | bytes accessed | tf_op | source)
XLA Modules:
  0.0 39.4 jit_solution(604885486681190467)
XLA Ops:
  0.6 1.0 %pack_kernel.1 = (bf16[32,2176]{1,0:T(8,128)(2,1)S(1)}, s32[8,32]{1,0:T(8,128)S(1)}) custom-call(bf16[32,2048]{1,0:T(8,128)(2,1)} %cotangent_hbm.1, s32[8,32]{1,0:T(8,128)} %bitcast.18, bf16[8,32]{1,0:T(8,128)(2,1)} %bitcast.20), custom_call_target="tpu_custom_call" | custom-call | tf_op jit(solution)/shard_map/pack_kernel/pallas_call | solution.py:319
  1.6 3.1 %collective-permute-start.6 = (bf16[32,2176]{1,0:T(8,128)(2,1)S(1)}, bf16[32,2176]{1,0:T(8,128)(2,1)S(1)}, u32[]{:S(2)}, u32[]{:S(2)}) collective-permute-start(bf16[32,2176]{1,0:T(8,128)(2,1)S(1)} %get-tuple-element.42.refs_0_), channel_id=1, source_target_pairs={{0,4},{1,5},{2,6},{3,7},{4,0},{5,1},{6,2},{7,3},{8,12},{9,13},{10,... | collective-permute-start | bytes 417800 | tf_op jit(solution)/shard_map/ppermute | solution.py:316
  4.7 2.6 %collective-permute-start = (bf16[32,2176]{1,0:T(8,128)(2,1)S(1)}, bf16[32,2176]{1,0:T(8,128)(2,1)S(1)}, u32[]{:S(2)}, u32[]{:S(2)}) collective-permute-start(bf16[32,2176]{1,0:T(8,128)(2,1)S(1)} %get-tuple-element.42.refs_0_), channel_id=1, source_target_pairs={{0,8},{1,9},{2,10},{3,11},{4,12},{5,13},{6,14},{7,15},{8,0},{9,1},... | collective-permute-start | bytes 417800 | tf_op jit(solution)/shard_map/ppermute | solution.py:316
  7.3 1.5 %collective-permute-start.4 = (bf16[32,2176]{1,0:T(8,128)(2,1)S(1)}, bf16[32,2176]{1,0:T(8,128)(2,1)S(1)}, u32[]{:S(2)}, u32[]{:S(2)}) collective-permute-start(bf16[32,2176]{1,0:T(8,128)(2,1)S(1)} %get-tuple-element.42.refs_0_), channel_id=1, source_target_pairs={{0,2},{1,3},{2,0},{3,1},{4,6},{5,7},{6,4},{7,5},{8,10},{9,11},{10,... | collective-permute-start | bytes 417800 | tf_op jit(solution)/shard_map/ppermute | solution.py:316
  8.8 2.1 %load_kernel.1 = (bf16[384,768]{1,0:T(8,128)(2,1)S(1)}, bf16[768,2048]{1,0:T(8,128)(2,1)S(1)}, bf16[32,768]{1,0:T(8,128)(2,1)S(1)}, bf16[32,2048]{1,0:T(8,128)(2,1)S(1)}) custom-call(bf16[384,768]{1,0:T(8,128)(2,1)} %bitcast.15, bf16[768,2048]{1,0:T(8,128)(2,1)} %bitcast.14, bf16[32,768]{1,0:T(8,128)(2,1)} %bitcast.17, bf16[32,2048]{1,0:T(8,128)(2,1)} %bitcast.16), custom_call_target="tpu_custom_call" | custom-call | tf_op jit(solution)/shard_map/load_kernel/pallas_call | solution.py:319
  10.9 0.0 collective-permute-done.6.refs_4_
  10.9 1.5 %collective-permute-start.8 = (bf16[32,2176]{1,0:T(8,128)(2,1)S(1)}, bf16[32,2176]{1,0:T(8,128)(2,1)S(1)}, u32[]{:S(2)}, u32[]{:S(2)}) collective-permute-start(bf16[32,2176]{1,0:T(8,128)(2,1)S(1)} %collective-permute-done.6.refs_4_), channel_id=1, source_target_pairs={{0,2},{1,3},{2,0},{3,1},{4,6},{5,7},{6,4},{7,5},{8,10},{9,11},{10,... | collective-permute-start | bytes 417800 | tf_op jit(solution)/shard_map/ppermute | solution.py:316
  12.4 0.0 collective-permute-start.3
  12.4 1.4 %collective-permute-done.refs_0_ = bf16[32,2176]{1,0:T(8,128)(2,1)S(1)} collective-permute-done((bf16[32,2176]{1,0:T(8,128)(2,1)S(1)}, bf16[32,2176]{1,0:T(8,128)(2,1)S(1)}, u32[]{:S(2)}, u32[]{:S(2)}) %collective-permute-start) | collective-permute-done | bytes 139296 | tf_op jit(solution)/shard_map/ppermute | solution.py:316
  13.8 0.4 %collective-permute-start.11 = (bf16[32,2176]{1,0:T(8,128)(2,1)S(1)}, bf16[32,2176]{1,0:T(8,128)(2,1)S(1)}, u32[]{:S(2)}, u32[]{:S(2)}) collective-permute-start(bf16[32,2176]{1,0:T(8,128)(2,1)S(1)} %collective-permute-done.refs_0_), channel_id=1, source_target_pairs={{0,4},{1,5},{2,6},{3,7},{4,0},{5,1},{6,2},{7,3},{8,12},{9,13},{10,... | collective-permute-start | bytes 417800 | tf_op jit(solution)/shard_map/ppermute | solution.py:316
  14.2 0.0 collective-permute-start.7
  14.2 0.0 collective-permute-done.4.refs_2_
  14.2 0.5 %collective-permute-start.5 = (bf16[32,2176]{1,0:T(8,128)(2,1)S(1)}, bf16[32,2176]{1,0:T(8,128)(2,1)S(1)}, u32[]{:S(2)}, u32[]{:S(2)}) collective-permute-start(bf16[32,2176]{1,0:T(8,128)(2,1)S(1)} %collective-permute-done.4.refs_2_), channel_id=1, source_target_pairs={{0,1},{1,0},{2,3},{3,2},{4,5},{5,4},{6,7},{7,6},{8,9},{9,8},{10,11... | collective-permute-start | bytes 417800 | tf_op jit(solution)/shard_map/ppermute | solution.py:316
  14.7 1.3 %collective-permute-done.8.refs_6_ = bf16[32,2176]{1,0:T(8,128)(2,1)S(1)} collective-permute-done((bf16[32,2176]{1,0:T(8,128)(2,1)S(1)}, bf16[32,2176]{1,0:T(8,128)(2,1)S(1)}, u32[]{:S(2)}, u32[]{:S(2)}) %collective-permute-start.8) | collective-permute-done | bytes 139296 | tf_op jit(solution)/shard_map/ppermute | solution.py:316
  16.0 0.0 collective-permute-start.9
  16.0 0.0 collective-permute-done.3.refs_1_
  16.0 1.4 %collective-permute-start.2 = (bf16[32,2176]{1,0:T(8,128)(2,1)S(1)}, bf16[32,2176]{1,0:T(8,128)(2,1)S(1)}, u32[]{:S(2)}, u32[]{:S(2)}) collective-permute-start(bf16[32,2176]{1,0:T(8,128)(2,1)S(1)} %collective-permute-done.refs_0_), channel_id=1, source_target_pairs={{0,2},{1,3},{2,0},{3,1},{4,6},{5,7},{6,4},{7,5},{8,10},{9,11},{10,... | collective-permute-start | bytes 417800 | tf_op jit(solution)/shard_map/ppermute | solution.py:316
  17.4 1.4 %collective-permute-done.11.refs_4_ = bf16[32,2176]{1,0:T(8,128)(2,1)S(1)} collective-permute-done((bf16[32,2176]{1,0:T(8,128)(2,1)S(1)}, bf16[32,2176]{1,0:T(8,128)(2,1)S(1)}, u32[]{:S(2)}, u32[]{:S(2)}) %collective-permute-start.11) | collective-permute-done | bytes 139296 | tf_op jit(solution)/shard_map/ppermute | solution.py:316
  18.8 1.5 %collective-permute-start.13 = (bf16[32,2176]{1,0:T(8,128)(2,1)S(1)}, bf16[32,2176]{1,0:T(8,128)(2,1)S(1)}, u32[]{:S(2)}, u32[]{:S(2)}) collective-permute-start(bf16[32,2176]{1,0:T(8,128)(2,1)S(1)} %collective-permute-done.11.refs_4_), channel_id=1, source_target_pairs={{0,2},{1,3},{2,0},{3,1},{4,6},{5,7},{6,4},{7,5},{8,10},{9,11},{10,... | collective-permute-start | bytes 417800 | tf_op jit(solution)/shard_map/ppermute | solution.py:316
  20.3 2.3 %forward_kernel.1 = (bf16[192,32]{1,0:T(8,128)(2,1)S(1)}, bf16[192,32]{1,0:T(8,128)(2,1)S(1)}, f32[192,2048]{1,0:T(8,128)S(1)}, f32[192,2048]{1,0:T(8,128)S(1)}) custom-call(bf16[384,768]{1,0:T(8,128)(2,1)S(1)} %get-tuple-element.48.hidden.refs_10_.refs_0_, bf16[768,2048]{1,0:T(8,128)(2,1)S(1)} %get-tuple-element.49.down.refs_11_.refs_1_, ...), custom_call_target="tpu_custom_call" | custom-call | tf_op jit(solution)/shard_map/forward_kernel/pallas_call | solution.py:319
  22.6 0.0 collective-permute-done.7.refs_5_
  22.6 0.1 collective-permute-start.1
  22.7 0.0 collective-permute-done.5.refs_3_
  22.7 0.5 %collective-permute-start.12 = (bf16[32,2176]{1,0:T(8,128)(2,1)S(1)}, bf16[32,2176]{1,0:T(8,128)(2,1)S(1)}, u32[]{:S(2)}, u32[]{:S(2)}) collective-permute-start(bf16[32,2176]{1,0:T(8,128)(2,1)S(1)} %collective-permute-done.11.refs_4_), channel_id=1, source_target_pairs={{0,1},{1,0},{2,3},{3,2},{4,5},{5,4},{6,7},{7,6},{8,9},{9,8},{10,11... | collective-permute-start | bytes 417800 | tf_op jit(solution)/shard_map/ppermute | solution.py:316
  23.2 0.0 collective-permute-done.9.refs_7_
  23.2 2.2 %first_kernel.1 = (bf16[192,768]{1,0:T(8,128)(2,1)S(1)}, f32[32,768]{1,0:T(8,128)S(1)}, f32[32,2048]{1,0:T(8,128)S(1)}, f32[8,128]{1,0:T(8,128)S(1)}) custom-call(bf16[32,2176]{1,0:T(8,128)(2,1)S(1)} %get-tuple-element.42.refs_0_, bf16[32,2176]{1,0:T(8,128)(2,1)S(1)} %collective-permute-done.3.refs_1_, bf16[32,2176]{1,0:T(8,128)(2,1)S(1)} %collective-permute-done.4.refs_2_, ...), custom_call_target="tpu_custom_call" | custom-call | tf_op jit(solution)/shard_map/first_kernel/pallas_call | solution.py:319
  25.4 0.0 collective-permute-done.2.refs_2_
  25.4 0.0 collective-permute-done.13.refs_6_
  25.4 0.2 collective-permute-start.14
  25.6 0.4 %collective-permute-start.10 = (bf16[32,2176]{1,0:T(8,128)(2,1)S(1)}, bf16[32,2176]{1,0:T(8,128)(2,1)S(1)}, u32[]{:S(2)}, u32[]{:S(2)}) collective-permute-start(bf16[32,2176]{1,0:T(8,128)(2,1)S(1)} %collective-permute-done.2.refs_2_), channel_id=1, source_target_pairs={{0,1},{1,0},{2,3},{3,2},{4,5},{5,4},{6,7},{7,6},{8,9},{9,8},{10,11... | collective-permute-start | bytes 417800 | tf_op jit(solution)/shard_map/ppermute | solution.py:316
  26.0 0.0 collective-permute-done.1.refs_1_
  26.0 0.0 collective-permute-done.12.refs_5_
  26.0 0.8 %collective-permute-done.14.refs_7_ = bf16[32,2176]{1,0:T(8,128)(2,1)S(1)} collective-permute-done((bf16[32,2176]{1,0:T(8,128)(2,1)S(1)}, bf16[32,2176]{1,0:T(8,128)(2,1)S(1)}, u32[]{:S(2)}, u32[]{:S(2)}) %collective-permute-start.14) | collective-permute-done | bytes 139296 | tf_op jit(solution)/shard_map/ppermute | solution.py:316
  26.9 0.2 collective-permute-done.10.refs_3_
  27.0 0.7 %combine_kernel.1 = (bf16[192,2048]{1,0:T(8,128)(2,1)S(1)}, f32[16,128]{1,0:T(8,128)S(1)}) custom-call(bf16[32,2176]{1,0:T(8,128)(2,1)S(1)} %collective-permute-done.refs_0_, bf16[32,2176]{1,0:T(8,128)(2,1)S(1)} %collective-permute-done.1.refs_1_, bf16[32,2176]{1,0:T(8,128)(2,1)S(1)} %collective-permute-done.2.refs_2_, ...), custom_call_target="tpu_custom_call" | custom-call | tf_op jit(solution)/shard_map/combine_kernel/pallas_call | solution.py:319
  27.8 2.5 %collective-permute-start.15 = (f32[16,128]{1,0:T(8,128)S(1)}, f32[16,128]{1,0:T(8,128)S(1)}, u32[]{:S(2)}, u32[]{:S(2)}) collective-permute-start(f32[16,128]{1,0:T(8,128)S(1)} %get-tuple-element.66), channel_id=1, source_target_pairs={{0,12},{1,13},{2,14},{3,15},{4,8},{5,9},{6,10},{7,11},{8,4},{9,5},... | collective-permute-start | bytes 24584 | tf_op jit(solution)/shard_map/ppermute | solution.py:316
  30.3 0.0 collective-permute-start.16
  30.3 1.9 %collective-permute-start.17 = (f32[16,128]{1,0:T(8,128)S(1)}, f32[16,128]{1,0:T(8,128)S(1)}, u32[]{:S(2)}, u32[]{:S(2)}) collective-permute-start(f32[16,128]{1,0:T(8,128)S(1)} %get-tuple-element.66), channel_id=1, source_target_pairs={{0,4},{1,5},{2,6},{3,7},{4,0},{5,1},{6,2},{7,3},{8,12},{9,13},{10,... | collective-permute-start | bytes 24584 | tf_op jit(solution)/shard_map/ppermute | solution.py:316
  32.2 2.5 %last_kernel.1 = (bf16[384,768]{1,0:T(8,128)(2,1)}, f32[32,768]{1,0:T(8,128)}, f32[32,2048]{1,0:T(8,128)}) custom-call(bf16[192,2048]{1,0:T(8,128)(2,1)S(1)} %get-tuple-element.67.scaled_ref, bf16[192,32]{1,0:T(8,128)(2,1)S(1)} %get-tuple-element.68.low_ref, bf16[384,768]{1,0:T(8,128)(2,1)S(1)} %get-tuple-element.48.hidden.refs_10_.refs_0_, ...), custom_call_target="tpu_custom_call" | custom-call | tf_op jit(solution)/shard_map/last_kernel/pallas_call | solution.py:319
  34.7 0.0 collective-permute-done.15
  34.7 0.1 collective-permute-done.16
  34.9 0.0 collective-permute-done.17
  34.9 0.1 select_select_fusion
  35.0 0.0 collective-permute-start.18
  35.0 1.6 %collective-permute-start.19 = (f32[16,128]{1,0:T(8,128)S(1)}, f32[16,128]{1,0:T(8,128)S(1)}, u32[]{:S(2)}, u32[]{:S(2)}) collective-permute-start(f32[16,128]{1,0:T(8,128)S(1)} %select_select_fusion), channel_id=1, source_target_pairs={{0,2},{1,3},{2,0},{3,1},{4,6},{5,7},{6,4},{7,5},{8,10},{9,11},{10,... | collective-permute-start | bytes 24584 | tf_op jit(solution)/shard_map/ppermute | solution.py:316
  36.5 0.3 collective-permute-start.20
  36.8 1.3 %collective-permute-done.18 = f32[16,128]{1,0:T(8,128)S(1)} collective-permute-done((f32[16,128]{1,0:T(8,128)S(1)}, f32[16,128]{1,0:T(8,128)S(1)}, u32[]{:S(2)}, u32[]{:S(2)}) %collective-permute-start.18) | collective-permute-done | bytes 8224 | tf_op jit(solution)/shard_map/ppermute | solution.py:316
  38.1 0.6 %collective-permute-done.19 = f32[16,128]{1,0:T(8,128)S(1)} collective-permute-done((f32[16,128]{1,0:T(8,128)S(1)}, f32[16,128]{1,0:T(8,128)S(1)}, u32[]{:S(2)}, u32[]{:S(2)}) %collective-permute-start.19) | collective-permute-done | bytes 8224 | tf_op jit(solution)/shard_map/ppermute | solution.py:316
  38.7 0.0 collective-permute-done.20
  38.7 0.1 slice_select_fusion
  38.8 0.6 %select_reduce_fusion = f32[8,32]{1,0:T(8,128)} fusion(f32[16,32]{1,0:T(8,128)S(1)} %slice_select_fusion, s32[8,32]{1,0:T(8,128)S(1)} %get-tuple-element.78), kind=kLoop, calls=%fused_computation | loop fusion | flops 12032 | bytes 4096 | tf_op jit(solution)/shard_map/reduce_sum | solution.py:434
  (4 shorter events, 0.0 us)
Async XLA Ops:
  1.6 9.3 %collective-permute-start.6 = (bf16[32,2176]{1,0:T(8,128)(2,1)S(1)}, bf16[32,2176]{1,0:T(8,128)(2,1)S(1)}, u32[]{:S(2)}, u32[]{:S(2)}) collective-permute-start(bf16[32,2176]{1,0:T(8,128)(2,1)S(1)} %get-tuple-element.42.refs_0_), channel_id=1, source_target_pairs={{0,4},{1,5},{2,6},{3,7},{4,0},{5,1},{6,2},{7,3},{8,12},{9,13},{10,... | collective-permute-start | bytes 417800 | tf_op jit(solution)/shard_map/ppermute | solution.py:316
  4.7 9.1 %collective-permute-start = (bf16[32,2176]{1,0:T(8,128)(2,1)S(1)}, bf16[32,2176]{1,0:T(8,128)(2,1)S(1)}, u32[]{:S(2)}, u32[]{:S(2)}) collective-permute-start(bf16[32,2176]{1,0:T(8,128)(2,1)S(1)} %get-tuple-element.42.refs_0_), channel_id=1, source_target_pairs={{0,8},{1,9},{2,10},{3,11},{4,12},{5,13},{6,14},{7,15},{8,0},{9,1},... | collective-permute-start | bytes 417800 | tf_op jit(solution)/shard_map/ppermute | solution.py:316
  7.3 6.9 %collective-permute-start.4 = (bf16[32,2176]{1,0:T(8,128)(2,1)S(1)}, bf16[32,2176]{1,0:T(8,128)(2,1)S(1)}, u32[]{:S(2)}, u32[]{:S(2)}) collective-permute-start(bf16[32,2176]{1,0:T(8,128)(2,1)S(1)} %get-tuple-element.42.refs_0_), channel_id=1, source_target_pairs={{0,2},{1,3},{2,0},{3,1},{4,6},{5,7},{6,4},{7,5},{8,10},{9,11},{10,... | collective-permute-start | bytes 417800 | tf_op jit(solution)/shard_map/ppermute | solution.py:316
  10.9 5.1 %collective-permute-start.8 = (bf16[32,2176]{1,0:T(8,128)(2,1)S(1)}, bf16[32,2176]{1,0:T(8,128)(2,1)S(1)}, u32[]{:S(2)}, u32[]{:S(2)}) collective-permute-start(bf16[32,2176]{1,0:T(8,128)(2,1)S(1)} %collective-permute-done.6.refs_4_), channel_id=1, source_target_pairs={{0,2},{1,3},{2,0},{3,1},{4,6},{5,7},{6,4},{7,5},{8,10},{9,11},{10,... | collective-permute-start | bytes 417800 | tf_op jit(solution)/shard_map/ppermute | solution.py:316
  12.4 3.6 %collective-permute-start.3 = (bf16[32,2176]{1,0:T(8,128)(2,1)S(1)}, bf16[32,2176]{1,0:T(8,128)(2,1)S(1)}, u32[]{:S(2)}, u32[]{:S(2)}) collective-permute-start(bf16[32,2176]{1,0:T(8,128)(2,1)S(1)} %get-tuple-element.42.refs_0_), channel_id=1, source_target_pairs={{0,1},{1,0},{2,3},{3,2},{4,5},{5,4},{6,7},{7,6},{8,9},{9,8},{10,11... | collective-permute-start | bytes 417800 | tf_op jit(solution)/shard_map/ppermute | solution.py:316
  13.8 5.1 %collective-permute-start.11 = (bf16[32,2176]{1,0:T(8,128)(2,1)S(1)}, bf16[32,2176]{1,0:T(8,128)(2,1)S(1)}, u32[]{:S(2)}, u32[]{:S(2)}) collective-permute-start(bf16[32,2176]{1,0:T(8,128)(2,1)S(1)} %collective-permute-done.refs_0_), channel_id=1, source_target_pairs={{0,4},{1,5},{2,6},{3,7},{4,0},{5,1},{6,2},{7,3},{8,12},{9,13},{10,... | collective-permute-start | bytes 417800 | tf_op jit(solution)/shard_map/ppermute | solution.py:316
  14.2 8.4 %collective-permute-start.7 = (bf16[32,2176]{1,0:T(8,128)(2,1)S(1)}, bf16[32,2176]{1,0:T(8,128)(2,1)S(1)}, u32[]{:S(2)}, u32[]{:S(2)}) collective-permute-start(bf16[32,2176]{1,0:T(8,128)(2,1)S(1)} %collective-permute-done.6.refs_4_), channel_id=1, source_target_pairs={{0,1},{1,0},{2,3},{3,2},{4,5},{5,4},{6,7},{7,6},{8,9},{9,8},{10,11... | collective-permute-start | bytes 417800 | tf_op jit(solution)/shard_map/ppermute | solution.py:316
  14.2 8.5 %collective-permute-start.5 = (bf16[32,2176]{1,0:T(8,128)(2,1)S(1)}, bf16[32,2176]{1,0:T(8,128)(2,1)S(1)}, u32[]{:S(2)}, u32[]{:S(2)}) collective-permute-start(bf16[32,2176]{1,0:T(8,128)(2,1)S(1)} %collective-permute-done.4.refs_2_), channel_id=1, source_target_pairs={{0,1},{1,0},{2,3},{3,2},{4,5},{5,4},{6,7},{7,6},{8,9},{9,8},{10,11... | collective-permute-start | bytes 417800 | tf_op jit(solution)/shard_map/ppermute | solution.py:316
  16.0 7.2 %collective-permute-start.9 = (bf16[32,2176]{1,0:T(8,128)(2,1)S(1)}, bf16[32,2176]{1,0:T(8,128)(2,1)S(1)}, u32[]{:S(2)}, u32[]{:S(2)}) collective-permute-start(bf16[32,2176]{1,0:T(8,128)(2,1)S(1)} %collective-permute-done.8.refs_6_), channel_id=1, source_target_pairs={{0,1},{1,0},{2,3},{3,2},{4,5},{5,4},{6,7},{7,6},{8,9},{9,8},{10,11... | collective-permute-start | bytes 417800 | tf_op jit(solution)/shard_map/ppermute | solution.py:316
  16.0 9.4 %collective-permute-start.2 = (bf16[32,2176]{1,0:T(8,128)(2,1)S(1)}, bf16[32,2176]{1,0:T(8,128)(2,1)S(1)}, u32[]{:S(2)}, u32[]{:S(2)}) collective-permute-start(bf16[32,2176]{1,0:T(8,128)(2,1)S(1)} %collective-permute-done.refs_0_), channel_id=1, source_target_pairs={{0,2},{1,3},{2,0},{3,1},{4,6},{5,7},{6,4},{7,5},{8,10},{9,11},{10,... | collective-permute-start | bytes 417800 | tf_op jit(solution)/shard_map/ppermute | solution.py:316
  18.8 6.6 %collective-permute-start.13 = (bf16[32,2176]{1,0:T(8,128)(2,1)S(1)}, bf16[32,2176]{1,0:T(8,128)(2,1)S(1)}, u32[]{:S(2)}, u32[]{:S(2)}) collective-permute-start(bf16[32,2176]{1,0:T(8,128)(2,1)S(1)} %collective-permute-done.11.refs_4_), channel_id=1, source_target_pairs={{0,2},{1,3},{2,0},{3,1},{4,6},{5,7},{6,4},{7,5},{8,10},{9,11},{10,... | collective-permute-start | bytes 417800 | tf_op jit(solution)/shard_map/ppermute | solution.py:316
  22.6 3.4 %collective-permute-start.1 = (bf16[32,2176]{1,0:T(8,128)(2,1)S(1)}, bf16[32,2176]{1,0:T(8,128)(2,1)S(1)}, u32[]{:S(2)}, u32[]{:S(2)}) collective-permute-start(bf16[32,2176]{1,0:T(8,128)(2,1)S(1)} %collective-permute-done.refs_0_), channel_id=1, source_target_pairs={{0,1},{1,0},{2,3},{3,2},{4,5},{5,4},{6,7},{7,6},{8,9},{9,8},{10,11... | collective-permute-start | bytes 417800 | tf_op jit(solution)/shard_map/ppermute | solution.py:316
  22.7 3.3 %collective-permute-start.12 = (bf16[32,2176]{1,0:T(8,128)(2,1)S(1)}, bf16[32,2176]{1,0:T(8,128)(2,1)S(1)}, u32[]{:S(2)}, u32[]{:S(2)}) collective-permute-start(bf16[32,2176]{1,0:T(8,128)(2,1)S(1)} %collective-permute-done.11.refs_4_), channel_id=1, source_target_pairs={{0,1},{1,0},{2,3},{3,2},{4,5},{5,4},{6,7},{7,6},{8,9},{9,8},{10,11... | collective-permute-start | bytes 417800 | tf_op jit(solution)/shard_map/ppermute | solution.py:316
  25.4 1.4 %collective-permute-start.14 = (bf16[32,2176]{1,0:T(8,128)(2,1)S(1)}, bf16[32,2176]{1,0:T(8,128)(2,1)S(1)}, u32[]{:S(2)}, u32[]{:S(2)}) collective-permute-start(bf16[32,2176]{1,0:T(8,128)(2,1)S(1)} %collective-permute-done.13.refs_6_), channel_id=1, source_target_pairs={{0,1},{1,0},{2,3},{3,2},{4,5},{5,4},{6,7},{7,6},{8,9},{9,8},{10,11... | collective-permute-start | bytes 417800 | tf_op jit(solution)/shard_map/ppermute | solution.py:316
  25.6 1.5 %collective-permute-start.10 = (bf16[32,2176]{1,0:T(8,128)(2,1)S(1)}, bf16[32,2176]{1,0:T(8,128)(2,1)S(1)}, u32[]{:S(2)}, u32[]{:S(2)}) collective-permute-start(bf16[32,2176]{1,0:T(8,128)(2,1)S(1)} %collective-permute-done.2.refs_2_), channel_id=1, source_target_pairs={{0,1},{1,0},{2,3},{3,2},{4,5},{5,4},{6,7},{7,6},{8,9},{9,8},{10,11... | collective-permute-start | bytes 417800 | tf_op jit(solution)/shard_map/ppermute | solution.py:316
  27.8 7.0 %collective-permute-start.15 = (f32[16,128]{1,0:T(8,128)S(1)}, f32[16,128]{1,0:T(8,128)S(1)}, u32[]{:S(2)}, u32[]{:S(2)}) collective-permute-start(f32[16,128]{1,0:T(8,128)S(1)} %get-tuple-element.66), channel_id=1, source_target_pairs={{0,12},{1,13},{2,14},{3,15},{4,8},{5,9},{6,10},{7,11},{8,4},{9,5},... | collective-permute-start | bytes 24584 | tf_op jit(solution)/shard_map/ppermute | solution.py:316
  30.3 4.5 %collective-permute-start.16 = (f32[16,128]{1,0:T(8,128)S(1)}, f32[16,128]{1,0:T(8,128)S(1)}, u32[]{:S(2)}, u32[]{:S(2)}) collective-permute-start(f32[16,128]{1,0:T(8,128)S(1)} %get-tuple-element.66), channel_id=1, source_target_pairs={{0,8},{1,9},{2,10},{3,11},{4,12},{5,13},{6,14},{7,15},{8,0},{9,1},... | collective-permute-start | bytes 24584 | tf_op jit(solution)/shard_map/ppermute | solution.py:316
  30.3 4.5 %collective-permute-start.17 = (f32[16,128]{1,0:T(8,128)S(1)}, f32[16,128]{1,0:T(8,128)S(1)}, u32[]{:S(2)}, u32[]{:S(2)}) collective-permute-start(f32[16,128]{1,0:T(8,128)S(1)} %get-tuple-element.66), channel_id=1, source_target_pairs={{0,4},{1,5},{2,6},{3,7},{4,0},{5,1},{6,2},{7,3},{8,12},{9,13},{10,... | collective-permute-start | bytes 24584 | tf_op jit(solution)/shard_map/ppermute | solution.py:316
  35.0 3.1 %collective-permute-start.18 = (f32[16,128]{1,0:T(8,128)S(1)}, f32[16,128]{1,0:T(8,128)S(1)}, u32[]{:S(2)}, u32[]{:S(2)}) collective-permute-start(f32[16,128]{1,0:T(8,128)S(1)} %select_select_fusion), channel_id=1, source_target_pairs={{0,3},{1,2},{2,1},{3,0},{4,7},{5,6},{6,5},{7,4},{8,11},{9,10},{10,... | collective-permute-start | bytes 24584 | tf_op jit(solution)/shard_map/ppermute | solution.py:316
  35.0 3.7 %collective-permute-start.19 = (f32[16,128]{1,0:T(8,128)S(1)}, f32[16,128]{1,0:T(8,128)S(1)}, u32[]{:S(2)}, u32[]{:S(2)}) collective-permute-start(f32[16,128]{1,0:T(8,128)S(1)} %select_select_fusion), channel_id=1, source_target_pairs={{0,2},{1,3},{2,0},{3,1},{4,6},{5,7},{6,4},{7,5},{8,10},{9,11},{10,... | collective-permute-start | bytes 24584 | tf_op jit(solution)/shard_map/ppermute | solution.py:316
  36.5 2.2 %collective-permute-start.20 = (f32[16,128]{1,0:T(8,128)S(1)}, f32[16,128]{1,0:T(8,128)S(1)}, u32[]{:S(2)}, u32[]{:S(2)}) collective-permute-start(f32[16,128]{1,0:T(8,128)S(1)} %select_select_fusion), channel_id=1, source_target_pairs={{0,1},{1,0},{2,3},{3,2},{4,5},{5,4},{6,7},{7,6},{8,9},{9,8},{10,11... | collective-permute-start | bytes 24584 | tf_op jit(solution)/shard_map/ppermute | solution.py:316

commit v5 on v4

--- a/solution.py
+++ b/solution.py
@@ -220,50 +220,28 @@
             pair_ref[s : s + 1, :] = row if r == 0 else pltpu.roll(row, lanes - tokens * r, 1)
 
 
-def backward(part, scaled_ref, low_ref, operands, outs):
-    hidden_ref, down_ref, first_ref, second_ref = operands
-    put_cotangent, put_first, put_second = outs
+def factor_sums(part, scaled_ref, low_ref, hidden_ref, second_ref):
     slots = scaled_ref.shape[0]
     scaled = scaled_ref[...]
     lowered = lax.dot_general(
         scaled, second_ref[...], over_last, preferred_element_type=jnp.float32
     ).astype(jnp.bfloat16)
-    put_second(
-        adapter_scale
-        * lax.dot_general(low_ref[...], scaled, over_first, preferred_element_type=jnp.float32)
-    )
-    put_first(
-        adapter_scale
-        * lax.dot_general(
-            lowered,
-            hidden_ref[slots * part : slots * (part + 1), :],
-            over_first,
-            preferred_element_type=jnp.float32,
-        )
-    )
-    fixed = lax.dot_general(scaled, down_ref[...], over_last, preferred_element_type=jnp.float32)
-    adapter = jnp.dot(lowered, first_ref[...], preferred_element_type=jnp.float32)
-    put_cotangent((fixed + adapter_scale * adapter).astype(jnp.bfloat16))
+    hidden = hidden_ref[slots * part : slots * (part + 1), :]
+    first = lax.dot_general(lowered, hidden, over_first, preferred_element_type=jnp.float32)
+    second = lax.dot_general(
+        low_ref[...], scaled, over_first, preferred_element_type=jnp.float32
+    )
+    return lowered, adapter_scale * first, adapter_scale * second
 
 
 def first_kernel(count, capacity, *refs):
     blocks, refs = refs[:count], refs[count:]
-    (out_ref, low_ref), operands, refs = refs[:2], refs[2:6], refs[6:]
-    cot_ref, dfirst_ref, dsecond_ref, pair_ref, scaled_ref = refs
-    me = lax.axis_index("expert")
-    combine(me, capacity, blocks, out_ref, scaled_ref, pair_ref, 0)
-
-    def put_cotangent(value):
-        cot_ref[...] = value
-
-    def put_first(value):
-        dfirst_ref[...] = value
-
-    def put_second(value):
-        dsecond_ref[...] = value
-
-    outs = put_cotangent, put_first, put_second
-    backward(0, scaled_ref, low_ref, operands, outs)
+    out_ref, low_ref, hidden_ref, second_ref = refs[:4]
+    scaled_ref, lowered_ref, dfirst_ref, dsecond_ref, pair_ref = refs[4:]
+    combine(lax.axis_index("expert"), capacity, blocks, out_ref, scaled_ref, pair_ref, 0)
+    lowered_ref[...], dfirst_ref[...], dsecond_ref[...] = factor_sums(
+        0, scaled_ref, low_ref, hidden_ref, second_ref
+    )
 
 
 def combine_kernel(count, capacity, *refs):
@@ -274,25 +252,40 @@
     )
 
 
-def last_kernel(count, scaled_ref, low_ref, *refs):
-    operands, (cot_before, dfirst_before, dsecond_before) = refs[:4], refs[4:7]
-    cot_ref, dfirst_ref, dsecond_ref = refs[7:]
+def cotangent_of(scaled_ref, lowered, down_ref, first_ref):
+    fixed = lax.dot_general(
+        scaled_ref[...], down_ref[...], over_last, preferred_element_type=jnp.float32
+    )
+    adapter = jnp.dot(lowered, first_ref[...], preferred_element_type=jnp.float32)
+    return (fixed + adapter_scale * adapter).astype(jnp.bfloat16)
+
+
+def late_kernel(
+    scaled_ref,
+    low_ref,
+    hidden_ref,
+    down_ref,
+    first_ref,
+    second_ref,
+    dfirst_before,
+    dsecond_before,
+    cot_ref,
+    dfirst_ref,
+    dsecond_ref,
+):
+    lowered, dfirst, dsecond = factor_sums(1, scaled_ref, low_ref, hidden_ref, second_ref)
+    dfirst_ref[...] = dfirst + dfirst_before[...]
+    dsecond_ref[...] = dsecond + dsecond_before[...]
+    cot_ref[...] = cotangent_of(scaled_ref, lowered, down_ref, first_ref)
+
+
+def cotangent_kernel(count, scaled_ref, lowered_ref, down_ref, first_ref, late_ref, cot_ref):
     half = lax.axis_index("expert") // count
     slots = scaled_ref.shape[0]
     here = pl.ds(pl.multiple_of(half * slots, slots), slots)
     there = pl.ds(pl.multiple_of((1 - half) * slots, slots), slots)
-    cot_ref[here, :] = cot_before[...]
-
-    def put_cotangent(value):
-        cot_ref[there, :] = value
-
-    def put_first(value):
-        dfirst_ref[...] = value + dfirst_before[...]
-
-    def put_second(value):
-        dsecond_ref[...] = value + dsecond_before[...]
-
-    backward(1, scaled_ref, low_ref, operands, (put_cotangent, put_first, put_second))
+    cot_ref[there, :] = late_ref[...]
+    cot_ref[here, :] = cotangent_of(scaled_ref, lowered_ref[...], down_ref, first_ref)
 
 
 def gathered(
@@ -315,10 +308,13 @@
     def swap(array, distance):
         return lax.ppermute(array, "expert", [(i, i ^ distance) for i in range(count)])
 
-    def call(limit, kernel, outs, spaces, scratch, *operands, held_out=pltpu.VMEM):
+    def call(limit, kernel, outs, spaces, scratch, *operands, plain=()):
         return pl.pallas_call(
             kernel,
-            out_shape=tuple(held_out(*out) for out in outs),
+            out_shape=tuple(
+                jax.ShapeDtypeStruct(*out) if i in plain else pltpu.VMEM(*out)
+                for i, out in enumerate(outs)
+            ),
             in_specs=[pl.BlockSpec(memory_space=space) for space in spaces],
             out_specs=(pl.BlockSpec(memory_space=pltpu.VMEM),) * len(outs),
             scratch_shapes=scratch,
@@ -381,23 +377,27 @@
     for d in [0] + near:
         blocks[d + 1] = swap(blocks[d], 1)
         blocks[d + 3] = swap(blocks[d + 2], 1)
+    hidden_held, down, first, second = held
     grads = [((rank, hidden_width), f32), ((rank, width), f32)]
-    *partial, pair = call(
+    lowered = ((slots // 2, rank), bf16)
+    scaled, *partial, pair = call(
         24,
         functools.partial(first_kernel, half, capacity),
-        [((slots // 2, hidden_width), bf16), *grads, ((half, lanes), f32)],
-        [pltpu.VMEM] * (half + 6),
-        [pltpu.VMEM((slots // 2, width), bf16)],
+        [((slots // 2, width), bf16), lowered, *grads, ((half, lanes), f32)],
+        [pltpu.VMEM] * (half + 4),
+        [],
         *[blocks[s] for s in range(half)],
         out,
         low,
-        *held,
+        hidden_held,
+        second,
     )
     for d in late:
         blocks[d + 2], partial, pair = lax.optimization_barrier((blocks[d + 2], partial, pair))
         blocks[d + 1] = swap(blocks[d], 1)
         blocks[d + 3] = swap(blocks[d + 2], 1)
-    scaled, pair = call(
+    lowered_early, dfirst, dsecond = partial
+    scaled_late, pair = call(
         24,
         functools.partial(combine_kernel, half, capacity),
         [((slots // 2, width), bf16), ((count, lanes), f32)],
@@ -407,25 +407,41 @@
         out_late,
         pair,
     )
+    late_rows = ((slots // 2, hidden_width), bf16)
     cotangent, dfirst, dsecond = call(
         24,
-        functools.partial(last_kernel, half),
-        [((slots, hidden_width), bf16), *grads],
-        [pltpu.VMEM] * 9,
+        late_kernel,
+        [late_rows, *grads],
+        [pltpu.VMEM] * 8,
         [],
-        scaled,
+        scaled_late,
         low_late,
         *held,
-        *partial,
-        held_out=jax.ShapeDtypeStruct,
+        dfirst,
+        dsecond,
+        plain=(1, 2),
     )
 
     distance = lax.broadcasted_iota(jnp.int32, pair.shape, 0)
-    moved = [swap(pair, d) for d in far]
-    for d, values in zip(far, moved):
+    order = near + late[::-1]
+    moved = [swap(pair, d) for d in order]
+    for d, values in zip(order, moved):
         pair = jnp.where(distance - jnp.bitwise_and(distance, 3) == d, values, pair)
     pair, cotangent, dfirst, dsecond = lax.optimization_barrier(
         (pair, cotangent, dfirst, dsecond)
+    )
+    (cotangent,) = call(
+        24,
+        functools.partial(cotangent_kernel, half),
+        [((slots, hidden_width), bf16)],
+        [pltpu.VMEM] * 5,
+        [],
+        scaled,
+        lowered_early,
+        down,
+        first,
+        cotangent,
+        plain=(0,),
     )
     moved = [swap(pair, d) for d in (1, 2, 3)]
     for d, values in zip((1, 2, 3), moved):

time: 39.6 us -> 39 us (0.985)
  starting transfers between devices: 19.9 us -> 19 us
  Pallas kernels: 10.8 us -> 11.4 us
    ppermute x21, starting transfers between devices: 19.9 us -> 19 us  [swap(): lax.ppermute(array, 'expert', [(i, i ^ distance) for i in range(count)])]
    pallas_call x6 -> x7, Pallas kernels: 10.8 us -> 11.4 us  [call(): pl.pallas_call(kernel, out_shape=tuple((jax.ShapeDtypeStruct(*out) if i i...]
  transfers between devices with their start and end apart: 21 -> 21, of which waited for: 8 -> 7; matrix products, arithmetic and copies ran while one was open for 0% -> 0% of each run, Pallas kernels for 23% -> 25%
where the time goes in v5:
time: 39 us; the launch traced here: 38.8 us
  starting transfers between devices  19 us (49%)
  Pallas kernels  11.4 us (29%)
  waiting for transfers between devices  6.89 us (18%)
  other arithmetic  0.8 us (2%)
  between operations  0.75 us (2%)
    ppermute x21, starting transfers between devices, swap(): lax.ppermute(array, 'expert', [(i, i ^ distance) for i in range(count)])  19 us
    pallas_call x7, Pallas kernels, call(): pl.pallas_call(kernel, out_shape=tuple((jax.ShapeDtypeStruct(*out) if i i...  11.4 us
    ppermute x21, waiting for transfers between devices, swap(): lax.ppermute(array, 'expert', [(i, i ^ distance) for i in range(count)])  6.89 us
  transfers between devices with their start and end apart: 21, of which 7 were waited for; matrix products, arithmetic and copies ran while one was open for 0% of the time, Pallas kernels for 25%

profile of v5, /device:TPU:0, one launch (start us, length us, event | category | flops | bytes accessed | tf_op | source)
XLA Modules:
  0.0 38.8 jit_solution(213607254269929567)
XLA Ops:
  0.6 1.0 %pack_kernel.1 = (bf16[32,2176]{1,0:T(8,128)(2,1)S(1)}, s32[8,32]{1,0:T(8,128)S(1)}) custom-call(bf16[32,2048]{1,0:T(8,128)(2,1)} %cotangent_hbm.1, s32[8,32]{1,0:T(8,128)} %bitcast.19, bf16[8,32]{1,0:T(8,128)(2,1)} %bitcast.21), custom_call_target="tpu_custom_call" | custom-call | tf_op jit(solution)/shard_map/pack_kernel/pallas_call | solution.py:312
  1.6 3.1 %collective-permute-start.3 = (bf16[32,2176]{1,0:T(8,128)(2,1)S(1)}, bf16[32,2176]{1,0:T(8,128)(2,1)S(1)}, u32[]{:S(2)}, u32[]{:S(2)}) collective-permute-start(bf16[32,2176]{1,0:T(8,128)(2,1)S(1)} %get-tuple-element.43.refs_0_), channel_id=1, source_target_pairs={{0,4},{1,5},{2,6},{3,7},{4,0},{5,1},{6,2},{7,3},{8,12},{9,13},{10,... | collective-permute-start | bytes 417800 | tf_op jit(solution)/shard_map/ppermute | solution.py:309
  4.7 2.6 %collective-permute-start.7 = (bf16[32,2176]{1,0:T(8,128)(2,1)S(1)}, bf16[32,2176]{1,0:T(8,128)(2,1)S(1)}, u32[]{:S(2)}, u32[]{:S(2)}) collective-permute-start(bf16[32,2176]{1,0:T(8,128)(2,1)S(1)} %get-tuple-element.43.refs_0_), channel_id=1, source_target_pairs={{0,8},{1,9},{2,10},{3,11},{4,12},{5,13},{6,14},{7,15},{8,0},{9,1},... | collective-permute-start | bytes 417800 | tf_op jit(solution)/shard_map/ppermute | solution.py:309
  7.3 1.5 %collective-permute-start.1 = (bf16[32,2176]{1,0:T(8,128)(2,1)S(1)}, bf16[32,2176]{1,0:T(8,128)(2,1)S(1)}, u32[]{:S(2)}, u32[]{:S(2)}) collective-permute-start(bf16[32,2176]{1,0:T(8,128)(2,1)S(1)} %get-tuple-element.43.refs_0_), channel_id=1, source_target_pairs={{0,2},{1,3},{2,0},{3,1},{4,6},{5,7},{6,4},{7,5},{8,10},{9,11},{10,... | collective-permute-start | bytes 417800 | tf_op jit(solution)/shard_map/ppermute | solution.py:309
  8.8 2.1 %load_kernel.1 = (bf16[384,768]{1,0:T(8,128)(2,1)S(1)}, bf16[768,2048]{1,0:T(8,128)(2,1)S(1)}, bf16[32,768]{1,0:T(8,128)(2,1)S(1)}, bf16[32,2048]{1,0:T(8,128)(2,1)S(1)}) custom-call(bf16[384,768]{1,0:T(8,128)(2,1)} %bitcast.16, bf16[768,2048]{1,0:T(8,128)(2,1)} %bitcast.14, bf16[32,768]{1,0:T(8,128)(2,1)} %bitcast.18, bf16[32,2048]{1,0:T(8,128)(2,1)} %bitcast.17), custom_call_target="tpu_custom_call" | custom-call | tf_op jit(solution)/shard_map/load_kernel/pallas_call | solution.py:312
  10.9 0.0 collective-permute-done.3.refs_4_
  10.9 1.5 %collective-permute-start.5 = (bf16[32,2176]{1,0:T(8,128)(2,1)S(1)}, bf16[32,2176]{1,0:T(8,128)(2,1)S(1)}, u32[]{:S(2)}, u32[]{:S(2)}) collective-permute-start(bf16[32,2176]{1,0:T(8,128)(2,1)S(1)} %collective-permute-done.3.refs_4_), channel_id=1, source_target_pairs={{0,2},{1,3},{2,0},{3,1},{4,6},{5,7},{6,4},{7,5},{8,10},{9,11},{10,... | collective-permute-start | bytes 417800 | tf_op jit(solution)/shard_map/ppermute | solution.py:309
  12.4 0.0 collective-permute-start
  12.4 1.4 %collective-permute-done.7.refs_0_ = bf16[32,2176]{1,0:T(8,128)(2,1)S(1)} collective-permute-done((bf16[32,2176]{1,0:T(8,128)(2,1)S(1)}, bf16[32,2176]{1,0:T(8,128)(2,1)S(1)}, u32[]{:S(2)}, u32[]{:S(2)}) %collective-permute-start.7) | collective-permute-done | bytes 139296 | tf_op jit(solution)/shard_map/ppermute | solution.py:309
  13.8 0.4 %collective-permute-start.8 = (bf16[32,2176]{1,0:T(8,128)(2,1)S(1)}, bf16[32,2176]{1,0:T(8,128)(2,1)S(1)}, u32[]{:S(2)}, u32[]{:S(2)}) collective-permute-start(bf16[32,2176]{1,0:T(8,128)(2,1)S(1)} %collective-permute-done.7.refs_0_), channel_id=1, source_target_pairs={{0,4},{1,5},{2,6},{3,7},{4,0},{5,1},{6,2},{7,3},{8,12},{9,13},{10,... | collective-permute-start | bytes 417800 | tf_op jit(solution)/shard_map/ppermute | solution.py:309
  14.2 0.0 collective-permute-start.4
  14.2 0.0 collective-permute-done.1.refs_2_
  14.2 0.5 %collective-permute-start.2 = (bf16[32,2176]{1,0:T(8,128)(2,1)S(1)}, bf16[32,2176]{1,0:T(8,128)(2,1)S(1)}, u32[]{:S(2)}, u32[]{:S(2)}) collective-permute-start(bf16[32,2176]{1,0:T(8,128)(2,1)S(1)} %collective-permute-done.1.refs_2_), channel_id=1, source_target_pairs={{0,1},{1,0},{2,3},{3,2},{4,5},{5,4},{6,7},{7,6},{8,9},{9,8},{10,11... | collective-permute-start | bytes 417800 | tf_op jit(solution)/shard_map/ppermute | solution.py:309
  14.7 1.3 %collective-permute-done.5.refs_6_ = bf16[32,2176]{1,0:T(8,128)(2,1)S(1)} collective-permute-done((bf16[32,2176]{1,0:T(8,128)(2,1)S(1)}, bf16[32,2176]{1,0:T(8,128)(2,1)S(1)}, u32[]{:S(2)}, u32[]{:S(2)}) %collective-permute-start.5) | collective-permute-done | bytes 139296 | tf_op jit(solution)/shard_map/ppermute | solution.py:309
  16.0 0.0 collective-permute-start.6
  16.0 0.0 collective-permute-done.refs_1_
  16.0 1.4 %collective-permute-start.10 = (bf16[32,2176]{1,0:T(8,128)(2,1)S(1)}, bf16[32,2176]{1,0:T(8,128)(2,1)S(1)}, u32[]{:S(2)}, u32[]{:S(2)}) collective-permute-start(bf16[32,2176]{1,0:T(8,128)(2,1)S(1)} %collective-permute-done.7.refs_0_), channel_id=1, source_target_pairs={{0,2},{1,3},{2,0},{3,1},{4,6},{5,7},{6,4},{7,5},{8,10},{9,11},{10,... | collective-permute-start | bytes 417800 | tf_op jit(solution)/shard_map/ppermute | solution.py:309
  17.4 1.4 %collective-permute-done.8.refs_4_ = bf16[32,2176]{1,0:T(8,128)(2,1)S(1)} collective-permute-done((bf16[32,2176]{1,0:T(8,128)(2,1)S(1)}, bf16[32,2176]{1,0:T(8,128)(2,1)S(1)}, u32[]{:S(2)}, u32[]{:S(2)}) %collective-permute-start.8) | collective-permute-done | bytes 139296 | tf_op jit(solution)/shard_map/ppermute | solution.py:309
  18.8 1.5 %collective-permute-start.9 = (bf16[32,2176]{1,0:T(8,128)(2,1)S(1)}, bf16[32,2176]{1,0:T(8,128)(2,1)S(1)}, u32[]{:S(2)}, u32[]{:S(2)}) collective-permute-start(bf16[32,2176]{1,0:T(8,128)(2,1)S(1)} %collective-permute-done.8.refs_4_), channel_id=1, source_target_pairs={{0,2},{1,3},{2,0},{3,1},{4,6},{5,7},{6,4},{7,5},{8,10},{9,11},{10,... | collective-permute-start | bytes 417800 | tf_op jit(solution)/shard_map/ppermute | solution.py:309
  20.3 2.3 %forward_kernel.1 = (bf16[192,32]{1,0:T(8,128)(2,1)S(1)}, bf16[192,32]{1,0:T(8,128)(2,1)S(1)}, f32[192,2048]{1,0:T(8,128)S(1)}, f32[192,2048]{1,0:T(8,128)S(1)}) custom-call(bf16[384,768]{1,0:T(8,128)(2,1)S(1)} %get-tuple-element.49.hidden.refs_10_.hidden_ref, bf16[768,2048]{1,0:T(8,128)(2,1)S(1)} %get-tuple-element.50.down.down_ref, ...), custom_call_target="tpu_custom_call" | custom-call | tf_op jit(solution)/shard_map/forward_kernel/pallas_call | solution.py:312
  22.6 0.0 collective-permute-done.4.refs_5_
  22.6 0.1 collective-permute-start.11
  22.7 0.0 collective-permute-done.2.refs_3_
  22.7 0.5 %collective-permute-start.13 = (bf16[32,2176]{1,0:T(8,128)(2,1)S(1)}, bf16[32,2176]{1,0:T(8,128)(2,1)S(1)}, u32[]{:S(2)}, u32[]{:S(2)}) collective-permute-start(bf16[32,2176]{1,0:T(8,128)(2,1)S(1)} %collective-permute-done.8.refs_4_), channel_id=1, source_target_pairs={{0,1},{1,0},{2,3},{3,2},{4,5},{5,4},{6,7},{7,6},{8,9},{9,8},{10,11... | collective-permute-start | bytes 417800 | tf_op jit(solution)/shard_map/ppermute | solution.py:309
  23.2 0.0 collective-permute-done.6.refs_7_
  23.2 1.4 %first_kernel.1 = (bf16[192,2048]{1,0:T(8,128)(2,1)S(1)}, bf16[192,32]{1,0:T(8,128)(2,1)S(1)}, f32[32,768]{1,0:T(8,128)S(1)}, f32[32,2048]{1,0:T(8,128)S(1)}, f32[8,128]{1,0:T(8,128)S(1)}) custom-call(bf16[32,2176]{1,0:T(8,128)(2,1)S(1)} %get-tuple-element.43.refs_0_, bf16[32,2176]{1,0:T(8,128)(2,1)S(1)} %collective-permute-done.refs_1_, ...), custom_call_target="tpu_custom_call" | custom-call | tf_op jit(solution)/shard_map/first_kernel/pallas_call | solution.py:312
  24.6 0.0 collective-permute-done.10.refs_2_
  24.6 0.5 %collective-permute-done.9.refs_6_ = bf16[32,2176]{1,0:T(8,128)(2,1)S(1)} collective-permute-done((bf16[32,2176]{1,0:T(8,128)(2,1)S(1)}, bf16[32,2176]{1,0:T(8,128)(2,1)S(1)}, u32[]{:S(2)}, u32[]{:S(2)}) %collective-permute-start.9) | collective-permute-done | bytes 139296 | tf_op jit(solution)/shard_map/ppermute | solution.py:309
  25.1 0.0 collective-permute-start.14
  25.1 0.5 %collective-permute-start.12 = (bf16[32,2176]{1,0:T(8,128)(2,1)S(1)}, bf16[32,2176]{1,0:T(8,128)(2,1)S(1)}, u32[]{:S(2)}, u32[]{:S(2)}) collective-permute-start(bf16[32,2176]{1,0:T(8,128)(2,1)S(1)} %collective-permute-done.10.refs_2_), channel_id=1, source_target_pairs={{0,1},{1,0},{2,3},{3,2},{4,5},{5,4},{6,7},{7,6},{8,9},{9,8},{10,11... | collective-permute-start | bytes 417800 | tf_op jit(solution)/shard_map/ppermute | solution.py:309
  25.6 0.0 collective-permute-done.11.refs_1_
  25.6 0.0 collective-permute-done.13.refs_5_
  25.6 0.8 %collective-permute-done.14.refs_7_ = bf16[32,2176]{1,0:T(8,128)(2,1)S(1)} collective-permute-done((bf16[32,2176]{1,0:T(8,128)(2,1)S(1)}, bf16[32,2176]{1,0:T(8,128)(2,1)S(1)}, u32[]{:S(2)}, u32[]{:S(2)}) %collective-permute-start.14) | collective-permute-done | bytes 139296 | tf_op jit(solution)/shard_map/ppermute | solution.py:309
  26.4 0.2 collective-permute-done.12.refs_3_
  26.6 0.7 %combine_kernel.1 = (bf16[192,2048]{1,0:T(8,128)(2,1)S(1)}, f32[16,128]{1,0:T(8,128)S(1)}) custom-call(bf16[32,2176]{1,0:T(8,128)(2,1)S(1)} %collective-permute-done.7.refs_0_, bf16[32,2176]{1,0:T(8,128)(2,1)S(1)} %collective-permute-done.11.refs_1_, bf16[32,2176]{1,0:T(8,128)(2,1)S(1)} %collective-permute-done.10.refs_2_, ...), custom_call_target="tpu_custom_call" | custom-call | tf_op jit(solution)/shard_map/combine_kernel/pallas_call | solution.py:312
  27.4 1.3 %collective-permute-start.15 = (f32[16,128]{1,0:T(8,128)S(1)}, f32[16,128]{1,0:T(8,128)S(1)}, u32[]{:S(2)}, u32[]{:S(2)}) collective-permute-start(f32[16,128]{1,0:T(8,128)S(1)} %get-tuple-element.69), channel_id=1, source_target_pairs={{0,8},{1,9},{2,10},{3,11},{4,12},{5,13},{6,14},{7,15},{8,0},{9,1},... | collective-permute-start | bytes 24584 | tf_op jit(solution)/shard_map/ppermute | solution.py:309
  28.7 1.7 %collective-permute-start.16 = (f32[16,128]{1,0:T(8,128)S(1)}, f32[16,128]{1,0:T(8,128)S(1)}, u32[]{:S(2)}, u32[]{:S(2)}) collective-permute-start(f32[16,128]{1,0:T(8,128)S(1)} %get-tuple-element.69), channel_id=1, source_target_pairs={{0,12},{1,13},{2,14},{3,15},{4,8},{5,9},{6,10},{7,11},{8,4},{9,5},... | collective-permute-start | bytes 24584 | tf_op jit(solution)/shard_map/ppermute | solution.py:309
  30.4 0.5 %collective-permute-start.17 = (f32[16,128]{1,0:T(8,128)S(1)}, f32[16,128]{1,0:T(8,128)S(1)}, u32[]{:S(2)}, u32[]{:S(2)}) collective-permute-start(f32[16,128]{1,0:T(8,128)S(1)} %get-tuple-element.69), channel_id=1, source_target_pairs={{0,4},{1,5},{2,6},{3,7},{4,0},{5,1},{6,2},{7,3},{8,12},{9,13},{10,... | collective-permute-start | bytes 24584 | tf_op jit(solution)/shard_map/ppermute | solution.py:309
  30.9 2.0 %late_kernel.1 = (bf16[192,768]{1,0:T(8,128)(2,1)S(1)}, f32[32,768]{1,0:T(8,128)}, f32[32,2048]{1,0:T(8,128)}) custom-call(bf16[192,2048]{1,0:T(8,128)(2,1)S(1)} %get-tuple-element.70.scaled_ref, bf16[192,32]{1,0:T(8,128)(2,1)S(1)} %get-tuple-element.71.low_ref, bf16[384,768]{1,0:T(8,128)(2,1)S(1)} %get-tuple-element.49.hidden.refs_10_.hidden_ref, ...), custom_call_target="tpu_custom_call" | custom-call | tf_op jit(solution)/shard_map/late_kernel/pallas_call | solution.py:312
  32.9 0.0 collective-permute-done.15
  32.9 1.3 %collective-permute-done.16 = f32[16,128]{1,0:T(8,128)S(1)} collective-permute-done((f32[16,128]{1,0:T(8,128)S(1)}, f32[16,128]{1,0:T(8,128)S(1)}, u32[]{:S(2)}, u32[]{:S(2)}) %collective-permute-start.16) | collective-permute-done | bytes 8224 | tf_op jit(solution)/shard_map/ppermute | solution.py:309
  34.2 0.0 collective-permute-done.17
  34.2 0.1 select_select_fusion
  34.3 0.0 collective-permute-start.18
  34.3 1.5 %collective-permute-start.19 = (f32[16,128]{1,0:T(8,128)S(1)}, f32[16,128]{1,0:T(8,128)S(1)}, u32[]{:S(2)}, u32[]{:S(2)}) collective-permute-start(f32[16,128]{1,0:T(8,128)S(1)} %select_select_fusion), channel_id=1, source_target_pairs={{0,2},{1,3},{2,0},{3,1},{4,6},{5,7},{6,4},{7,5},{8,10},{9,11},{10,... | collective-permute-start | bytes 24584 | tf_op jit(solution)/shard_map/ppermute | solution.py:309
  35.8 0.3 collective-permute-start.20
  36.2 1.9 %cotangent_kernel.1 = bf16[384,768]{1,0:T(8,128)(2,1)} custom-call(bf16[192,2048]{1,0:T(8,128)(2,1)S(1)} %get-tuple-element.55.scaled_ref, bf16[192,32]{1,0:T(8,128)(2,1)S(1)} %get-tuple-element.64.lowered_ref, bf16[768,2048]{1,0:T(8,128)(2,1)S(1)} %get-tuple-element.50.down.down_ref, bf16[32,768]{1,0:T(8,128)(2,1)S(1)} %get-tuple-element.51.first.first_ref, ...), custom_call_target="tpu_custom_call" | custom-call | tf_op jit(solution)/shard_map/cotangent_kernel/pallas_call | solution.py:312
  38.1 0.0 collective-permute-done.18
  38.1 0.0 collective-permute-done.19
  38.1 0.0 collective-permute-done.20
  38.1 0.1 slice_select_fusion
  38.2 0.6 %select_reduce_fusion = f32[8,32]{1,0:T(8,128)} fusion(f32[16,32]{1,0:T(8,128)S(1)} %slice_select_fusion, s32[8,32]{1,0:T(8,128)S(1)} %get-tuple-element.80), kind=kLoop, calls=%fused_computation | loop fusion | flops 12032 | bytes 4096 | tf_op jit(solution)/shard_map/reduce_sum | solution.py:450
  (4 shorter events, 0.0 us)
Async XLA Ops:
  1.6 9.3 %collective-permute-start.3 = (bf16[32,2176]{1,0:T(8,128)(2,1)S(1)}, bf16[32,2176]{1,0:T(8,128)(2,1)S(1)}, u32[]{:S(2)}, u32[]{:S(2)}) collective-permute-start(bf16[32,2176]{1,0:T(8,128)(2,1)S(1)} %get-tuple-element.43.refs_0_), channel_id=1, source_target_pairs={{0,4},{1,5},{2,6},{3,7},{4,0},{5,1},{6,2},{7,3},{8,12},{9,13},{10,... | collective-permute-start | bytes 417800 | tf_op jit(solution)/shard_map/ppermute | solution.py:309
  4.7 9.1 %collective-permute-start.7 = (bf16[32,2176]{1,0:T(8,128)(2,1)S(1)}, bf16[32,2176]{1,0:T(8,128)(2,1)S(1)}, u32[]{:S(2)}, u32[]{:S(2)}) collective-permute-start(bf16[32,2176]{1,0:T(8,128)(2,1)S(1)} %get-tuple-element.43.refs_0_), channel_id=1, source_target_pairs={{0,8},{1,9},{2,10},{3,11},{4,12},{5,13},{6,14},{7,15},{8,0},{9,1},... | collective-permute-start | bytes 417800 | tf_op jit(solution)/shard_map/ppermute | solution.py:309
  7.3 6.9 %collective-permute-start.1 = (bf16[32,2176]{1,0:T(8,128)(2,1)S(1)}, bf16[32,2176]{1,0:T(8,128)(2,1)S(1)}, u32[]{:S(2)}, u32[]{:S(2)}) collective-permute-start(bf16[32,2176]{1,0:T(8,128)(2,1)S(1)} %get-tuple-element.43.refs_0_), channel_id=1, source_target_pairs={{0,2},{1,3},{2,0},{3,1},{4,6},{5,7},{6,4},{7,5},{8,10},{9,11},{10,... | collective-permute-start | bytes 417800 | tf_op jit(solution)/shard_map/ppermute | solution.py:309
  10.9 5.1 %collective-permute-start.5 = (bf16[32,2176]{1,0:T(8,128)(2,1)S(1)}, bf16[32,2176]{1,0:T(8,128)(2,1)S(1)}, u32[]{:S(2)}, u32[]{:S(2)}) collective-permute-start(bf16[32,2176]{1,0:T(8,128)(2,1)S(1)} %collective-permute-done.3.refs_4_), channel_id=1, source_target_pairs={{0,2},{1,3},{2,0},{3,1},{4,6},{5,7},{6,4},{7,5},{8,10},{9,11},{10,... | collective-permute-start | bytes 417800 | tf_op jit(solution)/shard_map/ppermute | solution.py:309
  12.4 3.6 %collective-permute-start = (bf16[32,2176]{1,0:T(8,128)(2,1)S(1)}, bf16[32,2176]{1,0:T(8,128)(2,1)S(1)}, u32[]{:S(2)}, u32[]{:S(2)}) collective-permute-start(bf16[32,2176]{1,0:T(8,128)(2,1)S(1)} %get-tuple-element.43.refs_0_), channel_id=1, source_target_pairs={{0,1},{1,0},{2,3},{3,2},{4,5},{5,4},{6,7},{7,6},{8,9},{9,8},{10,11... | collective-permute-start | bytes 417800 | tf_op jit(solution)/shard_map/ppermute | solution.py:309
  13.8 5.1 %collective-permute-start.8 = (bf16[32,2176]{1,0:T(8,128)(2,1)S(1)}, bf16[32,2176]{1,0:T(8,128)(2,1)S(1)}, u32[]{:S(2)}, u32[]{:S(2)}) collective-permute-start(bf16[32,2176]{1,0:T(8,128)(2,1)S(1)} %collective-permute-done.7.refs_0_), channel_id=1, source_target_pairs={{0,4},{1,5},{2,6},{3,7},{4,0},{5,1},{6,2},{7,3},{8,12},{9,13},{10,... | collective-permute-start | bytes 417800 | tf_op jit(solution)/shard_map/ppermute | solution.py:309
  14.2 8.4 %collective-permute-start.4 = (bf16[32,2176]{1,0:T(8,128)(2,1)S(1)}, bf16[32,2176]{1,0:T(8,128)(2,1)S(1)}, u32[]{:S(2)}, u32[]{:S(2)}) collective-permute-start(bf16[32,2176]{1,0:T(8,128)(2,1)S(1)} %collective-permute-done.3.refs_4_), channel_id=1, source_target_pairs={{0,1},{1,0},{2,3},{3,2},{4,5},{5,4},{6,7},{7,6},{8,9},{9,8},{10,11... | collective-permute-start | bytes 417800 | tf_op jit(solution)/shard_map/ppermute | solution.py:309
  14.2 8.5 %collective-permute-start.2 = (bf16[32,2176]{1,0:T(8,128)(2,1)S(1)}, bf16[32,2176]{1,0:T(8,128)(2,1)S(1)}, u32[]{:S(2)}, u32[]{:S(2)}) collective-permute-start(bf16[32,2176]{1,0:T(8,128)(2,1)S(1)} %collective-permute-done.1.refs_2_), channel_id=1, source_target_pairs={{0,1},{1,0},{2,3},{3,2},{4,5},{5,4},{6,7},{7,6},{8,9},{9,8},{10,11... | collective-permute-start | bytes 417800 | tf_op jit(solution)/shard_map/ppermute | solution.py:309
  16.0 7.2 %collective-permute-start.6 = (bf16[32,2176]{1,0:T(8,128)(2,1)S(1)}, bf16[32,2176]{1,0:T(8,128)(2,1)S(1)}, u32[]{:S(2)}, u32[]{:S(2)}) collective-permute-start(bf16[32,2176]{1,0:T(8,128)(2,1)S(1)} %collective-permute-done.5.refs_6_), channel_id=1, source_target_pairs={{0,1},{1,0},{2,3},{3,2},{4,5},{5,4},{6,7},{7,6},{8,9},{9,8},{10,11... | collective-permute-start | bytes 417800 | tf_op jit(solution)/shard_map/ppermute | solution.py:309
  16.0 8.6 %collective-permute-start.10 = (bf16[32,2176]{1,0:T(8,128)(2,1)S(1)}, bf16[32,2176]{1,0:T(8,128)(2,1)S(1)}, u32[]{:S(2)}, u32[]{:S(2)}) collective-permute-start(bf16[32,2176]{1,0:T(8,128)(2,1)S(1)} %collective-permute-done.7.refs_0_), channel_id=1, source_target_pairs={{0,2},{1,3},{2,0},{3,1},{4,6},{5,7},{6,4},{7,5},{8,10},{9,11},{10,... | collective-permute-start | bytes 417800 | tf_op jit(solution)/shard_map/ppermute | solution.py:309
  18.8 6.3 %collective-permute-start.9 = (bf16[32,2176]{1,0:T(8,128)(2,1)S(1)}, bf16[32,2176]{1,0:T(8,128)(2,1)S(1)}, u32[]{:S(2)}, u32[]{:S(2)}) collective-permute-start(bf16[32,2176]{1,0:T(8,128)(2,1)S(1)} %collective-permute-done.8.refs_4_), channel_id=1, source_target_pairs={{0,2},{1,3},{2,0},{3,1},{4,6},{5,7},{6,4},{7,5},{8,10},{9,11},{10,... | collective-permute-start | bytes 417800 | tf_op jit(solution)/shard_map/ppermute | solution.py:309
  22.6 3.0 %collective-permute-start.11 = (bf16[32,2176]{1,0:T(8,128)(2,1)S(1)}, bf16[32,2176]{1,0:T(8,128)(2,1)S(1)}, u32[]{:S(2)}, u32[]{:S(2)}) collective-permute-start(bf16[32,2176]{1,0:T(8,128)(2,1)S(1)} %collective-permute-done.7.refs_0_), channel_id=1, source_target_pairs={{0,1},{1,0},{2,3},{3,2},{4,5},{5,4},{6,7},{7,6},{8,9},{9,8},{10,11... | collective-permute-start | bytes 417800 | tf_op jit(solution)/shard_map/ppermute | solution.py:309
  22.7 2.9 %collective-permute-start.13 = (bf16[32,2176]{1,0:T(8,128)(2,1)S(1)}, bf16[32,2176]{1,0:T(8,128)(2,1)S(1)}, u32[]{:S(2)}, u32[]{:S(2)}) collective-permute-start(bf16[32,2176]{1,0:T(8,128)(2,1)S(1)} %collective-permute-done.8.refs_4_), channel_id=1, source_target_pairs={{0,1},{1,0},{2,3},{3,2},{4,5},{5,4},{6,7},{7,6},{8,9},{9,8},{10,11... | collective-permute-start | bytes 417800 | tf_op jit(solution)/shard_map/ppermute | solution.py:309
  25.1 1.4 %collective-permute-start.14 = (bf16[32,2176]{1,0:T(8,128)(2,1)S(1)}, bf16[32,2176]{1,0:T(8,128)(2,1)S(1)}, u32[]{:S(2)}, u32[]{:S(2)}) collective-permute-start(bf16[32,2176]{1,0:T(8,128)(2,1)S(1)} %collective-permute-done.9.refs_6_), channel_id=1, source_target_pairs={{0,1},{1,0},{2,3},{3,2},{4,5},{5,4},{6,7},{7,6},{8,9},{9,8},{10,11... | collective-permute-start | bytes 417800 | tf_op jit(solution)/shard_map/ppermute | solution.py:309
  25.1 1.6 %collective-permute-start.12 = (bf16[32,2176]{1,0:T(8,128)(2,1)S(1)}, bf16[32,2176]{1,0:T(8,128)(2,1)S(1)}, u32[]{:S(2)}, u32[]{:S(2)}) collective-permute-start(bf16[32,2176]{1,0:T(8,128)(2,1)S(1)} %collective-permute-done.10.refs_2_), channel_id=1, source_target_pairs={{0,1},{1,0},{2,3},{3,2},{4,5},{5,4},{6,7},{7,6},{8,9},{9,8},{10,11... | collective-permute-start | bytes 417800 | tf_op jit(solution)/shard_map/ppermute | solution.py:309
  27.4 5.5 %collective-permute-start.15 = (f32[16,128]{1,0:T(8,128)S(1)}, f32[16,128]{1,0:T(8,128)S(1)}, u32[]{:S(2)}, u32[]{:S(2)}) collective-permute-start(f32[16,128]{1,0:T(8,128)S(1)} %get-tuple-element.69), channel_id=1, source_target_pairs={{0,8},{1,9},{2,10},{3,11},{4,12},{5,13},{6,14},{7,15},{8,0},{9,1},... | collective-permute-start | bytes 24584 | tf_op jit(solution)/shard_map/ppermute | solution.py:309
  28.7 5.5 %collective-permute-start.16 = (f32[16,128]{1,0:T(8,128)S(1)}, f32[16,128]{1,0:T(8,128)S(1)}, u32[]{:S(2)}, u32[]{:S(2)}) collective-permute-start(f32[16,128]{1,0:T(8,128)S(1)} %get-tuple-element.69), channel_id=1, source_target_pairs={{0,12},{1,13},{2,14},{3,15},{4,8},{5,9},{6,10},{7,11},{8,4},{9,5},... | collective-permute-start | bytes 24584 | tf_op jit(solution)/shard_map/ppermute | solution.py:309
  30.4 3.8 %collective-permute-start.17 = (f32[16,128]{1,0:T(8,128)S(1)}, f32[16,128]{1,0:T(8,128)S(1)}, u32[]{:S(2)}, u32[]{:S(2)}) collective-permute-start(f32[16,128]{1,0:T(8,128)S(1)} %get-tuple-element.69), channel_id=1, source_target_pairs={{0,4},{1,5},{2,6},{3,7},{4,0},{5,1},{6,2},{7,3},{8,12},{9,13},{10,... | collective-permute-start | bytes 24584 | tf_op jit(solution)/shard_map/ppermute | solution.py:309
  34.3 3.8 %collective-permute-start.18 = (f32[16,128]{1,0:T(8,128)S(1)}, f32[16,128]{1,0:T(8,128)S(1)}, u32[]{:S(2)}, u32[]{:S(2)}) collective-permute-start(f32[16,128]{1,0:T(8,128)S(1)} %select_select_fusion), channel_id=1, source_target_pairs={{0,3},{1,2},{2,1},{3,0},{4,7},{5,6},{6,5},{7,4},{8,11},{9,10},{10,... | collective-permute-start | bytes 24584 | tf_op jit(solution)/shard_map/ppermute | solution.py:309
  34.3 3.8 %collective-permute-start.19 = (f32[16,128]{1,0:T(8,128)S(1)}, f32[16,128]{1,0:T(8,128)S(1)}, u32[]{:S(2)}, u32[]{:S(2)}) collective-permute-start(f32[16,128]{1,0:T(8,128)S(1)} %select_select_fusion), channel_id=1, source_target_pairs={{0,2},{1,3},{2,0},{3,1},{4,6},{5,7},{6,4},{7,5},{8,10},{9,11},{10,... | collective-permute-start | bytes 24584 | tf_op jit(solution)/shard_map/ppermute | solution.py:309
  35.8 2.2 %collective-permute-start.20 = (f32[16,128]{1,0:T(8,128)S(1)}, f32[16,128]{1,0:T(8,128)S(1)}, u32[]{:S(2)}, u32[]{:S(2)}) collective-permute-start(f32[16,128]{1,0:T(8,128)S(1)} %select_select_fusion), channel_id=1, source_target_pairs={{0,1},{1,0},{2,3},{3,2},{4,5},{5,4},{6,7},{7,6},{8,9},{9,8},{10,11... | collective-permute-start | bytes 24584 | tf_op jit(solution)/shard_map/ppermute | solution.py:309

commit v6 on v5

--- a/solution.py
+++ b/solution.py
@@ -392,8 +392,9 @@
         hidden_held,
         second,
     )
+    d = late[-1] + 2
+    blocks[d], partial, pair = lax.optimization_barrier((blocks[d], partial, pair))
     for d in late:
-        blocks[d + 2], partial, pair = lax.optimization_barrier((blocks[d + 2], partial, pair))
         blocks[d + 1] = swap(blocks[d], 1)
         blocks[d + 3] = swap(blocks[d + 2], 1)
     lowered_early, dfirst, dsecond = partial

time: 39 us -> 38.3 us (0.982)
  waiting for transfers between devices: 6.89 us -> 6.07 us
    ppermute x21, waiting for transfers between devices: 6.89 us -> 6.07 us  [swap(): lax.ppermute(array, 'expert', [(i, i ^ distance) for i in range(count)])]
  transfers between devices with their start and end apart: 21 -> 21, of which waited for: 7 -> 5; matrix products, arithmetic and copies ran while one was open for 0% -> 0% of each run, Pallas kernels for 25% -> 25%
where the time goes in v6:
time: 38.3 us; the launch traced here: 38.1 us
  starting transfers between devices  19.1 us (50%)
  Pallas kernels  11.3 us (30%)
  waiting for transfers between devices  6.07 us (16%)
  other arithmetic  0.8 us (2%)
  between operations  0.76 us (2%)
    ppermute x21, starting transfers between devices, swap(): lax.ppermute(array, 'expert', [(i, i ^ distance) for i in range(count)])  19.1 us
    pallas_call x7, Pallas kernels, call(): pl.pallas_call(kernel, out_shape=tuple((jax.ShapeDtypeStruct(*out) if i i...  11.3 us
    ppermute x21, waiting for transfers between devices, swap(): lax.ppermute(array, 'expert', [(i, i ^ distance) for i in range(count)])  6.07 us
  transfers between devices with their start and end apart: 21, of which 5 were waited for; matrix products, arithmetic and copies ran while one was open for 0% of the time, Pallas kernels for 25%

profile of v6, /device:TPU:0, one launch (start us, length us, event | category | flops | bytes accessed | tf_op | source)
XLA Modules:
  0.0 38.1 jit_solution(9881421175461627160)
XLA Ops:
  0.6 1.0 %pack_kernel.1 = (bf16[32,2176]{1,0:T(8,128)(2,1)S(1)}, s32[8,32]{1,0:T(8,128)S(1)}) custom-call(bf16[32,2048]{1,0:T(8,128)(2,1)} %cotangent_hbm.1, s32[8,32]{1,0:T(8,128)} %bitcast.19, bf16[8,32]{1,0:T(8,128)(2,1)} %bitcast.21), custom_call_target="tpu_custom_call" | custom-call | tf_op jit(solution)/shard_map/pack_kernel/pallas_call | solution.py:312
  1.6 3.1 %collective-permute-start.3 = (bf16[32,2176]{1,0:T(8,128)(2,1)S(1)}, bf16[32,2176]{1,0:T(8,128)(2,1)S(1)}, u32[]{:S(2)}, u32[]{:S(2)}) collective-permute-start(bf16[32,2176]{1,0:T(8,128)(2,1)S(1)} %get-tuple-element.38.refs_0_), channel_id=1, source_target_pairs={{0,4},{1,5},{2,6},{3,7},{4,0},{5,1},{6,2},{7,3},{8,12},{9,13},{10,... | collective-permute-start | bytes 417800 | tf_op jit(solution)/shard_map/ppermute | solution.py:309
  4.7 2.6 %collective-permute-start.7 = (bf16[32,2176]{1,0:T(8,128)(2,1)S(1)}, bf16[32,2176]{1,0:T(8,128)(2,1)S(1)}, u32[]{:S(2)}, u32[]{:S(2)}) collective-permute-start(bf16[32,2176]{1,0:T(8,128)(2,1)S(1)} %get-tuple-element.38.refs_0_), channel_id=1, source_target_pairs={{0,8},{1,9},{2,10},{3,11},{4,12},{5,13},{6,14},{7,15},{8,0},{9,1},... | collective-permute-start | bytes 417800 | tf_op jit(solution)/shard_map/ppermute | solution.py:309
  7.3 1.5 %collective-permute-start.1 = (bf16[32,2176]{1,0:T(8,128)(2,1)S(1)}, bf16[32,2176]{1,0:T(8,128)(2,1)S(1)}, u32[]{:S(2)}, u32[]{:S(2)}) collective-permute-start(bf16[32,2176]{1,0:T(8,128)(2,1)S(1)} %get-tuple-element.38.refs_0_), channel_id=1, source_target_pairs={{0,2},{1,3},{2,0},{3,1},{4,6},{5,7},{6,4},{7,5},{8,10},{9,11},{10,... | collective-permute-start | bytes 417800 | tf_op jit(solution)/shard_map/ppermute | solution.py:309
  8.8 0.0 collective-permute-start
  8.8 2.1 %load_kernel.1 = (bf16[384,768]{1,0:T(8,128)(2,1)S(1)}, bf16[768,2048]{1,0:T(8,128)(2,1)S(1)}, bf16[32,768]{1,0:T(8,128)(2,1)S(1)}, bf16[32,2048]{1,0:T(8,128)(2,1)S(1)}) custom-call(bf16[384,768]{1,0:T(8,128)(2,1)} %bitcast.16, bf16[768,2048]{1,0:T(8,128)(2,1)} %bitcast.14, bf16[32,768]{1,0:T(8,128)(2,1)} %bitcast.18, bf16[32,2048]{1,0:T(8,128)(2,1)} %bitcast.17), custom_call_target="tpu_custom_call" | custom-call | tf_op jit(solution)/shard_map/load_kernel/pallas_call | solution.py:312
  10.9 0.0 collective-permute-done.3.refs_4_
  10.9 1.5 %collective-permute-start.5 = (bf16[32,2176]{1,0:T(8,128)(2,1)S(1)}, bf16[32,2176]{1,0:T(8,128)(2,1)S(1)}, u32[]{:S(2)}, u32[]{:S(2)}) collective-permute-start(bf16[32,2176]{1,0:T(8,128)(2,1)S(1)} %collective-permute-done.3.refs_4_), channel_id=1, source_target_pairs={{0,2},{1,3},{2,0},{3,1},{4,6},{5,7},{6,4},{7,5},{8,10},{9,11},{10,... | collective-permute-start | bytes 417800 | tf_op jit(solution)/shard_map/ppermute | solution.py:309
  12.4 1.4 %collective-permute-done.7.refs_0_ = bf16[32,2176]{1,0:T(8,128)(2,1)S(1)} collective-permute-done((bf16[32,2176]{1,0:T(8,128)(2,1)S(1)}, bf16[32,2176]{1,0:T(8,128)(2,1)S(1)}, u32[]{:S(2)}, u32[]{:S(2)}) %collective-permute-start.7) | collective-permute-done | bytes 139296 | tf_op jit(solution)/shard_map/ppermute | solution.py:309
  13.8 0.4 %collective-permute-start.8 = (bf16[32,2176]{1,0:T(8,128)(2,1)S(1)}, bf16[32,2176]{1,0:T(8,128)(2,1)S(1)}, u32[]{:S(2)}, u32[]{:S(2)}) collective-permute-start(bf16[32,2176]{1,0:T(8,128)(2,1)S(1)} %collective-permute-done.7.refs_0_), channel_id=1, source_target_pairs={{0,4},{1,5},{2,6},{3,7},{4,0},{5,1},{6,2},{7,3},{8,12},{9,13},{10,... | collective-permute-start | bytes 417800 | tf_op jit(solution)/shard_map/ppermute | solution.py:309
  14.2 0.0 collective-permute-start.4
  14.2 0.0 collective-permute-done.1.refs_2_
  14.2 0.5 %collective-permute-start.2 = (bf16[32,2176]{1,0:T(8,128)(2,1)S(1)}, bf16[32,2176]{1,0:T(8,128)(2,1)S(1)}, u32[]{:S(2)}, u32[]{:S(2)}) collective-permute-start(bf16[32,2176]{1,0:T(8,128)(2,1)S(1)} %collective-permute-done.1.refs_2_), channel_id=1, source_target_pairs={{0,1},{1,0},{2,3},{3,2},{4,5},{5,4},{6,7},{7,6},{8,9},{9,8},{10,11... | collective-permute-start | bytes 417800 | tf_op jit(solution)/shard_map/ppermute | solution.py:309
  14.7 0.0 collective-permute-done.refs_1_
  14.7 1.5 %collective-permute-start.11 = (bf16[32,2176]{1,0:T(8,128)(2,1)S(1)}, bf16[32,2176]{1,0:T(8,128)(2,1)S(1)}, u32[]{:S(2)}, u32[]{:S(2)}) collective-permute-start(bf16[32,2176]{1,0:T(8,128)(2,1)S(1)} %collective-permute-done.7.refs_0_), channel_id=1, source_target_pairs={{0,2},{1,3},{2,0},{3,1},{4,6},{5,7},{6,4},{7,5},{8,10},{9,11},{10,... | collective-permute-start | bytes 417800 | tf_op jit(solution)/shard_map/ppermute | solution.py:309
  16.2 0.8 %collective-permute-done.5.refs_6_ = bf16[32,2176]{1,0:T(8,128)(2,1)S(1)} collective-permute-done((bf16[32,2176]{1,0:T(8,128)(2,1)S(1)}, bf16[32,2176]{1,0:T(8,128)(2,1)S(1)}, u32[]{:S(2)}, u32[]{:S(2)}) %collective-permute-start.5) | collective-permute-done | bytes 139296 | tf_op jit(solution)/shard_map/ppermute | solution.py:309
  17.0 0.0 collective-permute-start.6
  17.0 1.8 %collective-permute-done.8.refs_4_ = bf16[32,2176]{1,0:T(8,128)(2,1)S(1)} collective-permute-done((bf16[32,2176]{1,0:T(8,128)(2,1)S(1)}, bf16[32,2176]{1,0:T(8,128)(2,1)S(1)}, u32[]{:S(2)}, u32[]{:S(2)}) %collective-permute-start.8) | collective-permute-done | bytes 139296 | tf_op jit(solution)/shard_map/ppermute | solution.py:309
  18.8 1.5 %collective-permute-start.9 = (bf16[32,2176]{1,0:T(8,128)(2,1)S(1)}, bf16[32,2176]{1,0:T(8,128)(2,1)S(1)}, u32[]{:S(2)}, u32[]{:S(2)}) collective-permute-start(bf16[32,2176]{1,0:T(8,128)(2,1)S(1)} %collective-permute-done.8.refs_4_), channel_id=1, source_target_pairs={{0,2},{1,3},{2,0},{3,1},{4,6},{5,7},{6,4},{7,5},{8,10},{9,11},{10,... | collective-permute-start | bytes 417800 | tf_op jit(solution)/shard_map/ppermute | solution.py:309
  20.3 2.3 %forward_kernel.1 = (bf16[192,32]{1,0:T(8,128)(2,1)S(1)}, bf16[192,32]{1,0:T(8,128)(2,1)S(1)}, f32[192,2048]{1,0:T(8,128)S(1)}, f32[192,2048]{1,0:T(8,128)S(1)}) custom-call(bf16[384,768]{1,0:T(8,128)(2,1)S(1)} %get-tuple-element.44.hidden.refs_10_.hidden_ref, bf16[768,2048]{1,0:T(8,128)(2,1)S(1)} %get-tuple-element.45.down.down_ref, ...), custom_call_target="tpu_custom_call" | custom-call | tf_op jit(solution)/shard_map/forward_kernel/pallas_call | solution.py:312
  22.6 0.0 collective-permute-done.4.refs_5_
  22.6 0.1 collective-permute-start.10
  22.7 0.0 collective-permute-done.2.refs_3_
  22.7 0.5 %collective-permute-start.13 = (bf16[32,2176]{1,0:T(8,128)(2,1)S(1)}, bf16[32,2176]{1,0:T(8,128)(2,1)S(1)}, u32[]{:S(2)}, u32[]{:S(2)}) collective-permute-start(bf16[32,2176]{1,0:T(8,128)(2,1)S(1)} %collective-permute-done.8.refs_4_), channel_id=1, source_target_pairs={{0,1},{1,0},{2,3},{3,2},{4,5},{5,4},{6,7},{7,6},{8,9},{9,8},{10,11... | collective-permute-start | bytes 417800 | tf_op jit(solution)/shard_map/ppermute | solution.py:309
  23.2 0.0 collective-permute-done.11.refs_2_
  23.2 0.1 collective-permute-start.12
  23.3 0.0 collective-permute-done.6.refs_7_
  23.3 1.4 %first_kernel.1 = (bf16[192,2048]{1,0:T(8,128)(2,1)S(1)}, bf16[192,32]{1,0:T(8,128)(2,1)S(1)}, f32[32,768]{1,0:T(8,128)S(1)}, f32[32,2048]{1,0:T(8,128)S(1)}, f32[8,128]{1,0:T(8,128)S(1)}) custom-call(bf16[32,2176]{1,0:T(8,128)(2,1)S(1)} %get-tuple-element.38.refs_0_, bf16[32,2176]{1,0:T(8,128)(2,1)S(1)} %collective-permute-done.refs_1_, ...), custom_call_target="tpu_custom_call" | custom-call | tf_op jit(solution)/shard_map/first_kernel/pallas_call | solution.py:312
  24.7 0.0 collective-permute-done.9.refs_6_
  24.7 0.5 %collective-permute-start.14 = (bf16[32,2176]{1,0:T(8,128)(2,1)S(1)}, bf16[32,2176]{1,0:T(8,128)(2,1)S(1)}, u32[]{:S(2)}, u32[]{:S(2)}) collective-permute-start(bf16[32,2176]{1,0:T(8,128)(2,1)S(1)} %collective-permute-done.9.refs_6_), channel_id=1, source_target_pairs={{0,1},{1,0},{2,3},{3,2},{4,5},{5,4},{6,7},{7,6},{8,9},{9,8},{10,11... | collective-permute-start | bytes 417800 | tf_op jit(solution)/shard_map/ppermute | solution.py:309
  25.2 0.0 collective-permute-done.10.refs_1_
  25.2 0.0 collective-permute-done.13.refs_5_
  25.2 0.0 collective-permute-done.12.refs_3_
  25.2 1.0 %collective-permute-done.14.refs_7_ = bf16[32,2176]{1,0:T(8,128)(2,1)S(1)} collective-permute-done((bf16[32,2176]{1,0:T(8,128)(2,1)S(1)}, bf16[32,2176]{1,0:T(8,128)(2,1)S(1)}, u32[]{:S(2)}, u32[]{:S(2)}) %collective-permute-start.14) | collective-permute-done | bytes 139296 | tf_op jit(solution)/shard_map/ppermute | solution.py:309
  26.1 0.7 %combine_kernel.1 = (bf16[192,2048]{1,0:T(8,128)(2,1)S(1)}, f32[16,128]{1,0:T(8,128)S(1)}) custom-call(bf16[32,2176]{1,0:T(8,128)(2,1)S(1)} %collective-permute-done.7.refs_0_, bf16[32,2176]{1,0:T(8,128)(2,1)S(1)} %collective-permute-done.10.refs_1_, bf16[32,2176]{1,0:T(8,128)(2,1)S(1)} %collective-permute-done.11.refs_2_, ...), custom_call_target="tpu_custom_call" | custom-call | tf_op jit(solution)/shard_map/combine_kernel/pallas_call | solution.py:312
  26.9 1.2 %collective-permute-start.15 = (f32[16,128]{1,0:T(8,128)S(1)}, f32[16,128]{1,0:T(8,128)S(1)}, u32[]{:S(2)}, u32[]{:S(2)}) collective-permute-start(f32[16,128]{1,0:T(8,128)S(1)} %get-tuple-element.59), channel_id=1, source_target_pairs={{0,8},{1,9},{2,10},{3,11},{4,12},{5,13},{6,14},{7,15},{8,0},{9,1},... | collective-permute-start | bytes 24584 | tf_op jit(solution)/shard_map/ppermute | solution.py:309
  28.1 1.7 %collective-permute-start.16 = (f32[16,128]{1,0:T(8,128)S(1)}, f32[16,128]{1,0:T(8,128)S(1)}, u32[]{:S(2)}, u32[]{:S(2)}) collective-permute-start(f32[16,128]{1,0:T(8,128)S(1)} %get-tuple-element.59), channel_id=1, source_target_pairs={{0,12},{1,13},{2,14},{3,15},{4,8},{5,9},{6,10},{7,11},{8,4},{9,5},... | collective-permute-start | bytes 24584 | tf_op jit(solution)/shard_map/ppermute | solution.py:309
  29.7 0.7 %collective-permute-start.17 = (f32[16,128]{1,0:T(8,128)S(1)}, f32[16,128]{1,0:T(8,128)S(1)}, u32[]{:S(2)}, u32[]{:S(2)}) collective-permute-start(f32[16,128]{1,0:T(8,128)S(1)} %get-tuple-element.59), channel_id=1, source_target_pairs={{0,4},{1,5},{2,6},{3,7},{4,0},{5,1},{6,2},{7,3},{8,12},{9,13},{10,... | collective-permute-start | bytes 24584 | tf_op jit(solution)/shard_map/ppermute | solution.py:309
  30.4 2.0 %late_kernel.1 = (bf16[192,768]{1,0:T(8,128)(2,1)S(1)}, f32[32,768]{1,0:T(8,128)}, f32[32,2048]{1,0:T(8,128)}) custom-call(bf16[192,2048]{1,0:T(8,128)(2,1)S(1)} %get-tuple-element.60.scaled_ref, bf16[192,32]{1,0:T(8,128)(2,1)S(1)} %get-tuple-element.61.low_ref, bf16[384,768]{1,0:T(8,128)(2,1)S(1)} %get-tuple-element.44.hidden.refs_10_.hidden_ref, ...), custom_call_target="tpu_custom_call" | custom-call | tf_op jit(solution)/shard_map/late_kernel/pallas_call | solution.py:312
  32.4 0.0 collective-permute-done.15
  32.4 1.1 %collective-permute-done.16 = f32[16,128]{1,0:T(8,128)S(1)} collective-permute-done((f32[16,128]{1,0:T(8,128)S(1)}, f32[16,128]{1,0:T(8,128)S(1)}, u32[]{:S(2)}, u32[]{:S(2)}) %collective-permute-start.16) | collective-permute-done | bytes 8224 | tf_op jit(solution)/shard_map/ppermute | solution.py:309
  33.5 0.0 collective-permute-done.17
  33.5 0.1 select_select_fusion
  33.6 0.0 collective-permute-start.18
  33.6 1.6 %collective-permute-start.19 = (f32[16,128]{1,0:T(8,128)S(1)}, f32[16,128]{1,0:T(8,128)S(1)}, u32[]{:S(2)}, u32[]{:S(2)}) collective-permute-start(f32[16,128]{1,0:T(8,128)S(1)} %select_select_fusion), channel_id=1, source_target_pairs={{0,2},{1,3},{2,0},{3,1},{4,6},{5,7},{6,4},{7,5},{8,10},{9,11},{10,... | collective-permute-start | bytes 24584 | tf_op jit(solution)/shard_map/ppermute | solution.py:309
  35.2 0.3 collective-permute-start.20
  35.5 1.9 %cotangent_kernel.1 = bf16[384,768]{1,0:T(8,128)(2,1)} custom-call(bf16[192,2048]{1,0:T(8,128)(2,1)S(1)} %get-tuple-element.50.scaled_ref, bf16[192,32]{1,0:T(8,128)(2,1)S(1)} %get-tuple-element.55.lowered_ref, bf16[768,2048]{1,0:T(8,128)(2,1)S(1)} %get-tuple-element.45.down.down_ref, bf16[32,768]{1,0:T(8,128)(2,1)S(1)} %get-tuple-element.46.first.first_ref, ...), custom_call_target="tpu_custom_call" | custom-call | tf_op jit(solution)/shard_map/cotangent_kernel/pallas_call | solution.py:312
  37.4 0.0 collective-permute-done.18
  37.4 0.0 collective-permute-done.19
  37.4 0.0 collective-permute-done.20
  37.4 0.1 slice_select_fusion
  37.5 0.6 %select_reduce_fusion = f32[8,32]{1,0:T(8,128)} fusion(f32[16,32]{1,0:T(8,128)S(1)} %slice_select_fusion, s32[8,32]{1,0:T(8,128)S(1)} %get-tuple-element.70), kind=kLoop, calls=%fused_computation | loop fusion | flops 12032 | bytes 4096 | tf_op jit(solution)/shard_map/reduce_sum | solution.py:451
  (4 shorter events, 0.0 us)
Async XLA Ops:
  1.6 9.3 %collective-permute-start.3 = (bf16[32,2176]{1,0:T(8,128)(2,1)S(1)}, bf16[32,2176]{1,0:T(8,128)(2,1)S(1)}, u32[]{:S(2)}, u32[]{:S(2)}) collective-permute-start(bf16[32,2176]{1,0:T(8,128)(2,1)S(1)} %get-tuple-element.38.refs_0_), channel_id=1, source_target_pairs={{0,4},{1,5},{2,6},{3,7},{4,0},{5,1},{6,2},{7,3},{8,12},{9,13},{10,... | collective-permute-start | bytes 417800 | tf_op jit(solution)/shard_map/ppermute | solution.py:309
  4.7 9.1 %collective-permute-start.7 = (bf16[32,2176]{1,0:T(8,128)(2,1)S(1)}, bf16[32,2176]{1,0:T(8,128)(2,1)S(1)}, u32[]{:S(2)}, u32[]{:S(2)}) collective-permute-start(bf16[32,2176]{1,0:T(8,128)(2,1)S(1)} %get-tuple-element.38.refs_0_), channel_id=1, source_target_pairs={{0,8},{1,9},{2,10},{3,11},{4,12},{5,13},{6,14},{7,15},{8,0},{9,1},... | collective-permute-start | bytes 417800 | tf_op jit(solution)/shard_map/ppermute | solution.py:309
  7.3 6.9 %collective-permute-start.1 = (bf16[32,2176]{1,0:T(8,128)(2,1)S(1)}, bf16[32,2176]{1,0:T(8,128)(2,1)S(1)}, u32[]{:S(2)}, u32[]{:S(2)}) collective-permute-start(bf16[32,2176]{1,0:T(8,128)(2,1)S(1)} %get-tuple-element.38.refs_0_), channel_id=1, source_target_pairs={{0,2},{1,3},{2,0},{3,1},{4,6},{5,7},{6,4},{7,5},{8,10},{9,11},{10,... | collective-permute-start | bytes 417800 | tf_op jit(solution)/shard_map/ppermute | solution.py:309
  8.8 6.0 %collective-permute-start = (bf16[32,2176]{1,0:T(8,128)(2,1)S(1)}, bf16[32,2176]{1,0:T(8,128)(2,1)S(1)}, u32[]{:S(2)}, u32[]{:S(2)}) collective-permute-start(bf16[32,2176]{1,0:T(8,128)(2,1)S(1)} %get-tuple-element.38.refs_0_), channel_id=1, source_target_pairs={{0,1},{1,0},{2,3},{3,2},{4,5},{5,4},{6,7},{7,6},{8,9},{9,8},{10,11... | collective-permute-start | bytes 417800 | tf_op jit(solution)/shard_map/ppermute | solution.py:309
  10.9 6.2 %collective-permute-start.5 = (bf16[32,2176]{1,0:T(8,128)(2,1)S(1)}, bf16[32,2176]{1,0:T(8,128)(2,1)S(1)}, u32[]{:S(2)}, u32[]{:S(2)}) collective-permute-start(bf16[32,2176]{1,0:T(8,128)(2,1)S(1)} %collective-permute-done.3.refs_4_), channel_id=1, source_target_pairs={{0,2},{1,3},{2,0},{3,1},{4,6},{5,7},{6,4},{7,5},{8,10},{9,11},{10,... | collective-permute-start | bytes 417800 | tf_op jit(solution)/shard_map/ppermute | solution.py:309
  13.8 5.1 %collective-permute-start.8 = (bf16[32,2176]{1,0:T(8,128)(2,1)S(1)}, bf16[32,2176]{1,0:T(8,128)(2,1)S(1)}, u32[]{:S(2)}, u32[]{:S(2)}) collective-permute-start(bf16[32,2176]{1,0:T(8,128)(2,1)S(1)} %collective-permute-done.7.refs_0_), channel_id=1, source_target_pairs={{0,4},{1,5},{2,6},{3,7},{4,0},{5,1},{6,2},{7,3},{8,12},{9,13},{10,... | collective-permute-start | bytes 417800 | tf_op jit(solution)/shard_map/ppermute | solution.py:309
  14.2 8.4 %collective-permute-start.4 = (bf16[32,2176]{1,0:T(8,128)(2,1)S(1)}, bf16[32,2176]{1,0:T(8,128)(2,1)S(1)}, u32[]{:S(2)}, u32[]{:S(2)}) collective-permute-start(bf16[32,2176]{1,0:T(8,128)(2,1)S(1)} %collective-permute-done.3.refs_4_), channel_id=1, source_target_pairs={{0,1},{1,0},{2,3},{3,2},{4,5},{5,4},{6,7},{7,6},{8,9},{9,8},{10,11... | collective-permute-start | bytes 417800 | tf_op jit(solution)/shard_map/ppermute | solution.py:309
  14.2 8.5 %collective-permute-start.2 = (bf16[32,2176]{1,0:T(8,128)(2,1)S(1)}, bf16[32,2176]{1,0:T(8,128)(2,1)S(1)}, u32[]{:S(2)}, u32[]{:S(2)}) collective-permute-start(bf16[32,2176]{1,0:T(8,128)(2,1)S(1)} %collective-permute-done.1.refs_2_), channel_id=1, source_target_pairs={{0,1},{1,0},{2,3},{3,2},{4,5},{5,4},{6,7},{7,6},{8,9},{9,8},{10,11... | collective-permute-start | bytes 417800 | tf_op jit(solution)/shard_map/ppermute | solution.py:309
  14.7 8.5 %collective-permute-start.11 = (bf16[32,2176]{1,0:T(8,128)(2,1)S(1)}, bf16[32,2176]{1,0:T(8,128)(2,1)S(1)}, u32[]{:S(2)}, u32[]{:S(2)}) collective-permute-start(bf16[32,2176]{1,0:T(8,128)(2,1)S(1)} %collective-permute-done.7.refs_0_), channel_id=1, source_target_pairs={{0,2},{1,3},{2,0},{3,1},{4,6},{5,7},{6,4},{7,5},{8,10},{9,11},{10,... | collective-permute-start | bytes 417800 | tf_op jit(solution)/shard_map/ppermute | solution.py:309
  17.0 6.2 %collective-permute-start.6 = (bf16[32,2176]{1,0:T(8,128)(2,1)S(1)}, bf16[32,2176]{1,0:T(8,128)(2,1)S(1)}, u32[]{:S(2)}, u32[]{:S(2)}) collective-permute-start(bf16[32,2176]{1,0:T(8,128)(2,1)S(1)} %collective-permute-done.5.refs_6_), channel_id=1, source_target_pairs={{0,1},{1,0},{2,3},{3,2},{4,5},{5,4},{6,7},{7,6},{8,9},{9,8},{10,11... | collective-permute-start | bytes 417800 | tf_op jit(solution)/shard_map/ppermute | solution.py:309
  18.8 5.8 %collective-permute-start.9 = (bf16[32,2176]{1,0:T(8,128)(2,1)S(1)}, bf16[32,2176]{1,0:T(8,128)(2,1)S(1)}, u32[]{:S(2)}, u32[]{:S(2)}) collective-permute-start(bf16[32,2176]{1,0:T(8,128)(2,1)S(1)} %collective-permute-done.8.refs_4_), channel_id=1, source_target_pairs={{0,2},{1,3},{2,0},{3,1},{4,6},{5,7},{6,4},{7,5},{8,10},{9,11},{10,... | collective-permute-start | bytes 417800 | tf_op jit(solution)/shard_map/ppermute | solution.py:309
  22.6 2.6 %collective-permute-start.10 = (bf16[32,2176]{1,0:T(8,128)(2,1)S(1)}, bf16[32,2176]{1,0:T(8,128)(2,1)S(1)}, u32[]{:S(2)}, u32[]{:S(2)}) collective-permute-start(bf16[32,2176]{1,0:T(8,128)(2,1)S(1)} %collective-permute-done.7.refs_0_), channel_id=1, source_target_pairs={{0,1},{1,0},{2,3},{3,2},{4,5},{5,4},{6,7},{7,6},{8,9},{9,8},{10,11... | collective-permute-start | bytes 417800 | tf_op jit(solution)/shard_map/ppermute | solution.py:309
  22.7 2.5 %collective-permute-start.13 = (bf16[32,2176]{1,0:T(8,128)(2,1)S(1)}, bf16[32,2176]{1,0:T(8,128)(2,1)S(1)}, u32[]{:S(2)}, u32[]{:S(2)}) collective-permute-start(bf16[32,2176]{1,0:T(8,128)(2,1)S(1)} %collective-permute-done.8.refs_4_), channel_id=1, source_target_pairs={{0,1},{1,0},{2,3},{3,2},{4,5},{5,4},{6,7},{7,6},{8,9},{9,8},{10,11... | collective-permute-start | bytes 417800 | tf_op jit(solution)/shard_map/ppermute | solution.py:309
  23.2 2.0 %collective-permute-start.12 = (bf16[32,2176]{1,0:T(8,128)(2,1)S(1)}, bf16[32,2176]{1,0:T(8,128)(2,1)S(1)}, u32[]{:S(2)}, u32[]{:S(2)}) collective-permute-start(bf16[32,2176]{1,0:T(8,128)(2,1)S(1)} %collective-permute-done.11.refs_2_), channel_id=1, source_target_pairs={{0,1},{1,0},{2,3},{3,2},{4,5},{5,4},{6,7},{7,6},{8,9},{9,8},{10,11... | collective-permute-start | bytes 417800 | tf_op jit(solution)/shard_map/ppermute | solution.py:309
  24.7 1.5 %collective-permute-start.14 = (bf16[32,2176]{1,0:T(8,128)(2,1)S(1)}, bf16[32,2176]{1,0:T(8,128)(2,1)S(1)}, u32[]{:S(2)}, u32[]{:S(2)}) collective-permute-start(bf16[32,2176]{1,0:T(8,128)(2,1)S(1)} %collective-permute-done.9.refs_6_), channel_id=1, source_target_pairs={{0,1},{1,0},{2,3},{3,2},{4,5},{5,4},{6,7},{7,6},{8,9},{9,8},{10,11... | collective-permute-start | bytes 417800 | tf_op jit(solution)/shard_map/ppermute | solution.py:309
  26.9 5.5 %collective-permute-start.15 = (f32[16,128]{1,0:T(8,128)S(1)}, f32[16,128]{1,0:T(8,128)S(1)}, u32[]{:S(2)}, u32[]{:S(2)}) collective-permute-start(f32[16,128]{1,0:T(8,128)S(1)} %get-tuple-element.59), channel_id=1, source_target_pairs={{0,8},{1,9},{2,10},{3,11},{4,12},{5,13},{6,14},{7,15},{8,0},{9,1},... | collective-permute-start | bytes 24584 | tf_op jit(solution)/shard_map/ppermute | solution.py:309
  28.1 5.4 %collective-permute-start.16 = (f32[16,128]{1,0:T(8,128)S(1)}, f32[16,128]{1,0:T(8,128)S(1)}, u32[]{:S(2)}, u32[]{:S(2)}) collective-permute-start(f32[16,128]{1,0:T(8,128)S(1)} %get-tuple-element.59), channel_id=1, source_target_pairs={{0,12},{1,13},{2,14},{3,15},{4,8},{5,9},{6,10},{7,11},{8,4},{9,5},... | collective-permute-start | bytes 24584 | tf_op jit(solution)/shard_map/ppermute | solution.py:309
  29.7 3.8 %collective-permute-start.17 = (f32[16,128]{1,0:T(8,128)S(1)}, f32[16,128]{1,0:T(8,128)S(1)}, u32[]{:S(2)}, u32[]{:S(2)}) collective-permute-start(f32[16,128]{1,0:T(8,128)S(1)} %get-tuple-element.59), channel_id=1, source_target_pairs={{0,4},{1,5},{2,6},{3,7},{4,0},{5,1},{6,2},{7,3},{8,12},{9,13},{10,... | collective-permute-start | bytes 24584 | tf_op jit(solution)/shard_map/ppermute | solution.py:309
  33.6 3.8 %collective-permute-start.18 = (f32[16,128]{1,0:T(8,128)S(1)}, f32[16,128]{1,0:T(8,128)S(1)}, u32[]{:S(2)}, u32[]{:S(2)}) collective-permute-start(f32[16,128]{1,0:T(8,128)S(1)} %select_select_fusion), channel_id=1, source_target_pairs={{0,3},{1,2},{2,1},{3,0},{4,7},{5,6},{6,5},{7,4},{8,11},{9,10},{10,... | collective-permute-start | bytes 24584 | tf_op jit(solution)/shard_map/ppermute | solution.py:309
  33.6 3.8 %collective-permute-start.19 = (f32[16,128]{1,0:T(8,128)S(1)}, f32[16,128]{1,0:T(8,128)S(1)}, u32[]{:S(2)}, u32[]{:S(2)}) collective-permute-start(f32[16,128]{1,0:T(8,128)S(1)} %select_select_fusion), channel_id=1, source_target_pairs={{0,2},{1,3},{2,0},{3,1},{4,6},{5,7},{6,4},{7,5},{8,10},{9,11},{10,... | collective-permute-start | bytes 24584 | tf_op jit(solution)/shard_map/ppermute | solution.py:309
  35.2 2.2 %collective-permute-start.20 = (f32[16,128]{1,0:T(8,128)S(1)}, f32[16,128]{1,0:T(8,128)S(1)}, u32[]{:S(2)}, u32[]{:S(2)}) collective-permute-start(f32[16,128]{1,0:T(8,128)S(1)} %select_select_fusion), channel_id=1, source_target_pairs={{0,1},{1,0},{2,3},{3,2},{4,5},{5,4},{6,7},{7,6},{8,9},{9,8},{10,11... | collective-permute-start | bytes 24584 | tf_op jit(solution)/shard_map/ppermute | solution.py:309

commit v7 on v5

--- a/solution.py
+++ b/solution.py
@@ -235,10 +235,13 @@
 
 
 def first_kernel(count, capacity, *refs):
-    blocks, refs = refs[:count], refs[count:]
-    out_ref, low_ref, hidden_ref, second_ref = refs[:4]
-    scaled_ref, lowered_ref, dfirst_ref, dsecond_ref, pair_ref = refs[4:]
+    blocks, (out_ref, scaled_ref, pair_ref) = refs[:count], refs[count:]
     combine(lax.axis_index("expert"), capacity, blocks, out_ref, scaled_ref, pair_ref, 0)
+
+
+def early_kernel(
+    scaled_ref, low_ref, hidden_ref, second_ref, lowered_ref, dfirst_ref, dsecond_ref
+):
     lowered_ref[...], dfirst_ref[...], dsecond_ref[...] = factor_sums(
         0, scaled_ref, low_ref, hidden_ref, second_ref
     )
@@ -380,23 +383,32 @@
     hidden_held, down, first, second = held
     grads = [((rank, hidden_width), f32), ((rank, width), f32)]
     lowered = ((slots // 2, rank), bf16)
-    scaled, *partial, pair = call(
+    scaled, pair = call(
         24,
         functools.partial(first_kernel, half, capacity),
-        [((slots // 2, width), bf16), lowered, *grads, ((half, lanes), f32)],
-        [pltpu.VMEM] * (half + 4),
+        [((slots // 2, width), bf16), ((half, lanes), f32)],
+        [pltpu.VMEM] * (half + 1),
         [],
         *[blocks[s] for s in range(half)],
         out,
+    )
+    d = late[-1] + 2
+    blocks[d], scaled, pair = lax.optimization_barrier((blocks[d], scaled, pair))
+    for d in late:
+        blocks[d + 1] = swap(blocks[d], 1)
+        blocks[d + 3] = swap(blocks[d + 2], 1)
+    lowered_early, dfirst, dsecond = call(
+        24,
+        early_kernel,
+        [lowered, *grads],
+        [pltpu.VMEM] * 4,
+        [],
+        scaled,
         low,
         hidden_held,
         second,
     )
-    for d in late:
-        blocks[d + 2], partial, pair = lax.optimization_barrier((blocks[d + 2], partial, pair))
-        blocks[d + 1] = swap(blocks[d], 1)
-        blocks[d + 3] = swap(blocks[d + 2], 1)
-    lowered_early, dfirst, dsecond = partial
+    out_late, dsecond = lax.optimization_barrier((out_late, dsecond))
     scaled_late, pair = call(
         24,
         functools.partial(combine_kernel, half, capacity),
@@ -423,7 +435,7 @@
     )
 
     distance = lax.broadcasted_iota(jnp.int32, pair.shape, 0)
-    order = near + late[::-1]
+    order = far
     moved = [swap(pair, d) for d in order]
     for d, values in zip(order, moved):
         pair = jnp.where(distance - jnp.bitwise_and(distance, 3) == d, values, pair)

time: 39 us -> 38 us (0.974)
  waiting for transfers between devices: 6.89 us -> 4.69 us
  starting transfers between devices: 19 us -> 20 us
    ppermute x21, waiting for transfers between devices: 6.89 us -> 4.69 us  [swap(): lax.ppermute(array, 'expert', [(i, i ^ distance) for i in range(count)])]
    ppermute x21, starting transfers between devices: 19 us -> 20 us  [swap(): lax.ppermute(array, 'expert', [(i, i ^ distance) for i in range(count)])]
    pallas_call x7 -> x8, Pallas kernels: 11.4 us -> 11.6 us  [call(): pl.pallas_call(kernel, out_shape=tuple((jax.ShapeDtypeStruct(*out) if i i...]
  transfers between devices with their start and end apart: 21 -> 21, of which waited for: 7 -> 4; matrix products, arithmetic and copies ran while one was open for 0% -> 0% of each run, Pallas kernels for 25% -> 26%
where the time goes in v7:
time: 38 us; the launch traced here: 37.8 us
  starting transfers between devices  20 us (53%)
  Pallas kernels  11.6 us (31%)
  waiting for transfers between devices  4.69 us (12%)
  other arithmetic  0.8 us (2%)
  between operations  0.75 us (2%)
    ppermute x21, starting transfers between devices, swap(): lax.ppermute(array, 'expert', [(i, i ^ distance) for i in range(count)])  20 us
    pallas_call x8, Pallas kernels, call(): pl.pallas_call(kernel, out_shape=tuple((jax.ShapeDtypeStruct(*out) if i i...  11.6 us
    ppermute x21, waiting for transfers between devices, swap(): lax.ppermute(array, 'expert', [(i, i ^ distance) for i in range(count)])  4.69 us
  transfers between devices with their start and end apart: 21, of which 4 were waited for; matrix products, arithmetic and copies ran while one was open for 0% of the time, Pallas kernels for 26%

profile of v7, /device:TPU:0, one launch (start us, length us, event | category | flops | bytes accessed | tf_op | source)
XLA Modules:
  0.0 37.8 jit_solution(17224556954709803045)
XLA Ops:
  0.6 1.0 %pack_kernel.1 = (bf16[32,2176]{1,0:T(8,128)(2,1)S(1)}, s32[8,32]{1,0:T(8,128)S(1)}) custom-call(bf16[32,2048]{1,0:T(8,128)(2,1)} %cotangent_hbm.1, s32[8,32]{1,0:T(8,128)} %bitcast.19, bf16[8,32]{1,0:T(8,128)(2,1)} %bitcast.21), custom_call_target="tpu_custom_call" | custom-call | tf_op jit(solution)/shard_map/pack_kernel/pallas_call | solution.py:315
  1.6 3.1 %collective-permute-start.6 = (bf16[32,2176]{1,0:T(8,128)(2,1)S(1)}, bf16[32,2176]{1,0:T(8,128)(2,1)S(1)}, u32[]{:S(2)}, u32[]{:S(2)}) collective-permute-start(bf16[32,2176]{1,0:T(8,128)(2,1)S(1)} %get-tuple-element.38.refs_0_), channel_id=1, source_target_pairs={{0,4},{1,5},{2,6},{3,7},{4,0},{5,1},{6,2},{7,3},{8,12},{9,13},{10,... | collective-permute-start | bytes 417800 | tf_op jit(solution)/shard_map/ppermute | solution.py:312
  4.7 2.6 %collective-permute-start = (bf16[32,2176]{1,0:T(8,128)(2,1)S(1)}, bf16[32,2176]{1,0:T(8,128)(2,1)S(1)}, u32[]{:S(2)}, u32[]{:S(2)}) collective-permute-start(bf16[32,2176]{1,0:T(8,128)(2,1)S(1)} %get-tuple-element.38.refs_0_), channel_id=1, source_target_pairs={{0,8},{1,9},{2,10},{3,11},{4,12},{5,13},{6,14},{7,15},{8,0},{9,1},... | collective-permute-start | bytes 417800 | tf_op jit(solution)/shard_map/ppermute | solution.py:312
  7.3 1.5 %collective-permute-start.4 = (bf16[32,2176]{1,0:T(8,128)(2,1)S(1)}, bf16[32,2176]{1,0:T(8,128)(2,1)S(1)}, u32[]{:S(2)}, u32[]{:S(2)}) collective-permute-start(bf16[32,2176]{1,0:T(8,128)(2,1)S(1)} %get-tuple-element.38.refs_0_), channel_id=1, source_target_pairs={{0,2},{1,3},{2,0},{3,1},{4,6},{5,7},{6,4},{7,5},{8,10},{9,11},{10,... | collective-permute-start | bytes 417800 | tf_op jit(solution)/shard_map/ppermute | solution.py:312
  8.8 0.0 collective-permute-start.3
  8.8 2.1 %load_kernel.1 = (bf16[384,768]{1,0:T(8,128)(2,1)S(1)}, bf16[768,2048]{1,0:T(8,128)(2,1)S(1)}, bf16[32,768]{1,0:T(8,128)(2,1)S(1)}, bf16[32,2048]{1,0:T(8,128)(2,1)S(1)}) custom-call(bf16[384,768]{1,0:T(8,128)(2,1)} %bitcast.16, bf16[768,2048]{1,0:T(8,128)(2,1)} %bitcast.14, bf16[32,768]{1,0:T(8,128)(2,1)} %bitcast.18, bf16[32,2048]{1,0:T(8,128)(2,1)} %bitcast.17), custom_call_target="tpu_custom_call" | custom-call | tf_op jit(solution)/shard_map/load_kernel/pallas_call | solution.py:315
  10.9 0.0 collective-permute-done.6.refs_4_
  10.9 1.5 %collective-permute-start.8 = (bf16[32,2176]{1,0:T(8,128)(2,1)S(1)}, bf16[32,2176]{1,0:T(8,128)(2,1)S(1)}, u32[]{:S(2)}, u32[]{:S(2)}) collective-permute-start(bf16[32,2176]{1,0:T(8,128)(2,1)S(1)} %collective-permute-done.6.refs_4_), channel_id=1, source_target_pairs={{0,2},{1,3},{2,0},{3,1},{4,6},{5,7},{6,4},{7,5},{8,10},{9,11},{10,... | collective-permute-start | bytes 417800 | tf_op jit(solution)/shard_map/ppermute | solution.py:312
  12.4 1.4 %collective-permute-done.refs_0_ = bf16[32,2176]{1,0:T(8,128)(2,1)S(1)} collective-permute-done((bf16[32,2176]{1,0:T(8,128)(2,1)S(1)}, bf16[32,2176]{1,0:T(8,128)(2,1)S(1)}, u32[]{:S(2)}, u32[]{:S(2)}) %collective-permute-start) | collective-permute-done | bytes 139296 | tf_op jit(solution)/shard_map/ppermute | solution.py:312
  13.8 0.4 %collective-permute-start.1 = (bf16[32,2176]{1,0:T(8,128)(2,1)S(1)}, bf16[32,2176]{1,0:T(8,128)(2,1)S(1)}, u32[]{:S(2)}, u32[]{:S(2)}) collective-permute-start(bf16[32,2176]{1,0:T(8,128)(2,1)S(1)} %collective-permute-done.refs_0_), channel_id=1, source_target_pairs={{0,4},{1,5},{2,6},{3,7},{4,0},{5,1},{6,2},{7,3},{8,12},{9,13},{10,... | collective-permute-start | bytes 417800 | tf_op jit(solution)/shard_map/ppermute | solution.py:312
  14.2 0.0 collective-permute-start.7
  14.2 0.0 collective-permute-done.4.refs_2_
  14.2 0.5 %collective-permute-start.5 = (bf16[32,2176]{1,0:T(8,128)(2,1)S(1)}, bf16[32,2176]{1,0:T(8,128)(2,1)S(1)}, u32[]{:S(2)}, u32[]{:S(2)}) collective-permute-start(bf16[32,2176]{1,0:T(8,128)(2,1)S(1)} %collective-permute-done.4.refs_2_), channel_id=1, source_target_pairs={{0,1},{1,0},{2,3},{3,2},{4,5},{5,4},{6,7},{7,6},{8,9},{9,8},{10,11... | collective-permute-start | bytes 417800 | tf_op jit(solution)/shard_map/ppermute | solution.py:312
  14.7 0.0 collective-permute-done.3.refs_1_
  14.7 1.5 %collective-permute-start.11 = (bf16[32,2176]{1,0:T(8,128)(2,1)S(1)}, bf16[32,2176]{1,0:T(8,128)(2,1)S(1)}, u32[]{:S(2)}, u32[]{:S(2)}) collective-permute-start(bf16[32,2176]{1,0:T(8,128)(2,1)S(1)} %collective-permute-done.refs_0_), channel_id=1, source_target_pairs={{0,2},{1,3},{2,0},{3,1},{4,6},{5,7},{6,4},{7,5},{8,10},{9,11},{10,... | collective-permute-start | bytes 417800 | tf_op jit(solution)/shard_map/ppermute | solution.py:312
  16.2 0.8 %collective-permute-done.8.refs_6_ = bf16[32,2176]{1,0:T(8,128)(2,1)S(1)} collective-permute-done((bf16[32,2176]{1,0:T(8,128)(2,1)S(1)}, bf16[32,2176]{1,0:T(8,128)(2,1)S(1)}, u32[]{:S(2)}, u32[]{:S(2)}) %collective-permute-start.8) | collective-permute-done | bytes 139296 | tf_op jit(solution)/shard_map/ppermute | solution.py:312
  17.0 0.0 collective-permute-start.9
  17.0 1.8 %collective-permute-done.1.refs_4_ = bf16[32,2176]{1,0:T(8,128)(2,1)S(1)} collective-permute-done((bf16[32,2176]{1,0:T(8,128)(2,1)S(1)}, bf16[32,2176]{1,0:T(8,128)(2,1)S(1)}, u32[]{:S(2)}, u32[]{:S(2)}) %collective-permute-start.1) | collective-permute-done | bytes 139296 | tf_op jit(solution)/shard_map/ppermute | solution.py:312
  18.8 1.5 %collective-permute-start.2 = (bf16[32,2176]{1,0:T(8,128)(2,1)S(1)}, bf16[32,2176]{1,0:T(8,128)(2,1)S(1)}, u32[]{:S(2)}, u32[]{:S(2)}) collective-permute-start(bf16[32,2176]{1,0:T(8,128)(2,1)S(1)} %collective-permute-done.1.refs_4_), channel_id=1, source_target_pairs={{0,2},{1,3},{2,0},{3,1},{4,6},{5,7},{6,4},{7,5},{8,10},{9,11},{10,... | collective-permute-start | bytes 417800 | tf_op jit(solution)/shard_map/ppermute | solution.py:312
  20.3 2.3 %forward_kernel.1 = (bf16[192,32]{1,0:T(8,128)(2,1)S(1)}, bf16[192,32]{1,0:T(8,128)(2,1)S(1)}, f32[192,2048]{1,0:T(8,128)S(1)}, f32[192,2048]{1,0:T(8,128)S(1)}) custom-call(bf16[384,768]{1,0:T(8,128)(2,1)S(1)} %get-tuple-element.44.hidden.hidden_ref, bf16[768,2048]{1,0:T(8,128)(2,1)S(1)} %get-tuple-element.45.down.down_ref, ...), custom_call_target="tpu_custom_call" | custom-call | tf_op jit(solution)/shard_map/forward_kernel/pallas_call | solution.py:315
  22.6 0.0 collective-permute-done.7.refs_5_
  22.6 0.1 collective-permute-start.10
  22.7 0.0 collective-permute-done.5.refs_3_
  22.7 0.5 %collective-permute-start.13 = (bf16[32,2176]{1,0:T(8,128)(2,1)S(1)}, bf16[32,2176]{1,0:T(8,128)(2,1)S(1)}, u32[]{:S(2)}, u32[]{:S(2)}) collective-permute-start(bf16[32,2176]{1,0:T(8,128)(2,1)S(1)} %collective-permute-done.1.refs_4_), channel_id=1, source_target_pairs={{0,1},{1,0},{2,3},{3,2},{4,5},{5,4},{6,7},{7,6},{8,9},{9,8},{10,11... | collective-permute-start | bytes 417800 | tf_op jit(solution)/shard_map/ppermute | solution.py:312
  23.2 0.0 collective-permute-done.11.refs_2_
  23.2 0.1 collective-permute-start.12
  23.3 0.0 collective-permute-done.9.refs_7_
  23.3 0.7 %first_kernel.1 = (bf16[192,2048]{1,0:T(8,128)(2,1)S(1)}, f32[8,128]{1,0:T(8,128)S(1)}) custom-call(bf16[32,2176]{1,0:T(8,128)(2,1)S(1)} %get-tuple-element.38.refs_0_, bf16[32,2176]{1,0:T(8,128)(2,1)S(1)} %collective-permute-done.3.refs_1_, bf16[32,2176]{1,0:T(8,128)(2,1)S(1)} %collective-permute-done.4.refs_2_, ...), custom_call_target="tpu_custom_call" | custom-call | tf_op jit(solution)/shard_map/first_kernel/pallas_call | solution.py:315
  24.0 0.0 collective-permute-done.2.refs_6_
  24.0 0.4 %collective-permute-start.14 = (bf16[32,2176]{1,0:T(8,128)(2,1)S(1)}, bf16[32,2176]{1,0:T(8,128)(2,1)S(1)}, u32[]{:S(2)}, u32[]{:S(2)}) collective-permute-start(bf16[32,2176]{1,0:T(8,128)(2,1)S(1)} %collective-permute-done.2.refs_6_), channel_id=1, source_target_pairs={{0,1},{1,0},{2,3},{3,2},{4,5},{5,4},{6,7},{7,6},{8,9},{9,8},{10,11... | collective-permute-start | bytes 417800 | tf_op jit(solution)/shard_map/ppermute | solution.py:312
  24.5 0.9 %early_kernel.1 = (bf16[192,32]{1,0:T(8,128)(2,1)S(1)}, f32[32,768]{1,0:T(8,128)S(1)}, f32[32,2048]{1,0:T(8,128)S(1)}) custom-call(bf16[192,2048]{1,0:T(8,128)(2,1)S(1)} %get-tuple-element.51.scaled_ref, bf16[192,32]{1,0:T(8,128)(2,1)S(1)} %get-tuple-element.52.low_ref, bf16[384,768]{1,0:T(8,128)(2,1)S(1)} %get-tuple-element.44.hidden.hidden_ref, ...), custom_call_target="tpu_custom_call" | custom-call | tf_op jit(solution)/shard_map/early_kernel/pallas_call | solution.py:315
  25.4 0.0 collective-permute-done.10.refs_1_
  25.4 0.0 collective-permute-done.13.refs_5_
  25.4 0.0 collective-permute-done.12.refs_3_
  25.4 0.0 collective-permute-done.14.refs_7_
  25.5 0.7 %combine_kernel.1 = (bf16[192,2048]{1,0:T(8,128)(2,1)S(1)}, f32[16,128]{1,0:T(8,128)S(1)}) custom-call(bf16[32,2176]{1,0:T(8,128)(2,1)S(1)} %collective-permute-done.refs_0_, bf16[32,2176]{1,0:T(8,128)(2,1)S(1)} %collective-permute-done.10.refs_1_, bf16[32,2176]{1,0:T(8,128)(2,1)S(1)} %collective-permute-done.11.refs_2_, ...), custom_call_target="tpu_custom_call" | custom-call | tf_op jit(solution)/shard_map/combine_kernel/pallas_call | solution.py:315
  26.2 2.5 %collective-permute-start.15 = (f32[16,128]{1,0:T(8,128)S(1)}, f32[16,128]{1,0:T(8,128)S(1)}, u32[]{:S(2)}, u32[]{:S(2)}) collective-permute-start(f32[16,128]{1,0:T(8,128)S(1)} %get-tuple-element.59), channel_id=1, source_target_pairs={{0,12},{1,13},{2,14},{3,15},{4,8},{5,9},{6,10},{7,11},{8,4},{9,5},... | collective-permute-start | bytes 24584 | tf_op jit(solution)/shard_map/ppermute | solution.py:312
  28.7 0.0 collective-permute-start.16
  28.7 1.9 %collective-permute-start.17 = (f32[16,128]{1,0:T(8,128)S(1)}, f32[16,128]{1,0:T(8,128)S(1)}, u32[]{:S(2)}, u32[]{:S(2)}) collective-permute-start(f32[16,128]{1,0:T(8,128)S(1)} %get-tuple-element.59), channel_id=1, source_target_pairs={{0,4},{1,5},{2,6},{3,7},{4,0},{5,1},{6,2},{7,3},{8,12},{9,13},{10,... | collective-permute-start | bytes 24584 | tf_op jit(solution)/shard_map/ppermute | solution.py:312
  30.6 2.0 %late_kernel.1 = (bf16[192,768]{1,0:T(8,128)(2,1)S(1)}, f32[32,768]{1,0:T(8,128)}, f32[32,2048]{1,0:T(8,128)}) custom-call(bf16[192,2048]{1,0:T(8,128)(2,1)S(1)} %get-tuple-element.60.scaled_ref, bf16[192,32]{1,0:T(8,128)(2,1)S(1)} %get-tuple-element.61.low_ref, bf16[384,768]{1,0:T(8,128)(2,1)S(1)} %get-tuple-element.44.hidden.hidden_ref, ...), custom_call_target="tpu_custom_call" | custom-call | tf_op jit(solution)/shard_map/late_kernel/pallas_call | solution.py:315
  32.6 0.0 collective-permute-done.15
  32.6 0.6 %collective-permute-done.16 = f32[16,128]{1,0:T(8,128)S(1)} collective-permute-done((f32[16,128]{1,0:T(8,128)S(1)}, f32[16,128]{1,0:T(8,128)S(1)}, u32[]{:S(2)}, u32[]{:S(2)}) %collective-permute-start.16) | collective-permute-done | bytes 8224 | tf_op jit(solution)/shard_map/ppermute | solution.py:312
  33.2 0.0 collective-permute-done.17
  33.2 0.1 select_select_fusion
  33.3 0.0 collective-permute-start.18
  33.3 1.3 %collective-permute-start.19 = (f32[16,128]{1,0:T(8,128)S(1)}, f32[16,128]{1,0:T(8,128)S(1)}, u32[]{:S(2)}, u32[]{:S(2)}) collective-permute-start(f32[16,128]{1,0:T(8,128)S(1)} %select_select_fusion), channel_id=1, source_target_pairs={{0,2},{1,3},{2,0},{3,1},{4,6},{5,7},{6,4},{7,5},{8,10},{9,11},{10,... | collective-permute-start | bytes 24584 | tf_op jit(solution)/shard_map/ppermute | solution.py:312
  34.7 0.5 %collective-permute-start.20 = (f32[16,128]{1,0:T(8,128)S(1)}, f32[16,128]{1,0:T(8,128)S(1)}, u32[]{:S(2)}, u32[]{:S(2)}) collective-permute-start(f32[16,128]{1,0:T(8,128)S(1)} %select_select_fusion), channel_id=1, source_target_pairs={{0,1},{1,0},{2,3},{3,2},{4,5},{5,4},{6,7},{7,6},{8,9},{9,8},{10,11... | collective-permute-start | bytes 24584 | tf_op jit(solution)/shard_map/ppermute | solution.py:312
  35.2 1.9 %cotangent_kernel.1 = bf16[384,768]{1,0:T(8,128)(2,1)} custom-call(bf16[192,2048]{1,0:T(8,128)(2,1)S(1)} %get-tuple-element.51.scaled_ref, bf16[192,32]{1,0:T(8,128)(2,1)S(1)} %get-tuple-element.53.lowered_ref, bf16[768,2048]{1,0:T(8,128)(2,1)S(1)} %get-tuple-element.45.down.down_ref, bf16[32,768]{1,0:T(8,128)(2,1)S(1)} %get-tuple-element.46.first.first_ref, ...), custom_call_target="tpu_custom_call" | custom-call | tf_op jit(solution)/shard_map/cotangent_kernel/pallas_call | solution.py:315
  37.1 0.0 collective-permute-done.18
  37.1 0.0 collective-permute-done.19
  37.1 0.0 collective-permute-done.20
  37.1 0.1 slice_select_fusion
  37.2 0.6 %select_reduce_fusion = f32[8,32]{1,0:T(8,128)} fusion(f32[16,32]{1,0:T(8,128)S(1)} %slice_select_fusion, s32[8,32]{1,0:T(8,128)S(1)} %get-tuple-element.70), kind=kLoop, calls=%fused_computation | loop fusion | flops 12032 | bytes 4096 | tf_op jit(solution)/shard_map/reduce_sum | solution.py:462
  (4 shorter events, 0.0 us)
Async XLA Ops:
  1.6 9.3 %collective-permute-start.6 = (bf16[32,2176]{1,0:T(8,128)(2,1)S(1)}, bf16[32,2176]{1,0:T(8,128)(2,1)S(1)}, u32[]{:S(2)}, u32[]{:S(2)}) collective-permute-start(bf16[32,2176]{1,0:T(8,128)(2,1)S(1)} %get-tuple-element.38.refs_0_), channel_id=1, source_target_pairs={{0,4},{1,5},{2,6},{3,7},{4,0},{5,1},{6,2},{7,3},{8,12},{9,13},{10,... | collective-permute-start | bytes 417800 | tf_op jit(solution)/shard_map/ppermute | solution.py:312
  4.7 9.1 %collective-permute-start = (bf16[32,2176]{1,0:T(8,128)(2,1)S(1)}, bf16[32,2176]{1,0:T(8,128)(2,1)S(1)}, u32[]{:S(2)}, u32[]{:S(2)}) collective-permute-start(bf16[32,2176]{1,0:T(8,128)(2,1)S(1)} %get-tuple-element.38.refs_0_), channel_id=1, source_target_pairs={{0,8},{1,9},{2,10},{3,11},{4,12},{5,13},{6,14},{7,15},{8,0},{9,1},... | collective-permute-start | bytes 417800 | tf_op jit(solution)/shard_map/ppermute | solution.py:312
  7.3 6.9 %collective-permute-start.4 = (bf16[32,2176]{1,0:T(8,128)(2,1)S(1)}, bf16[32,2176]{1,0:T(8,128)(2,1)S(1)}, u32[]{:S(2)}, u32[]{:S(2)}) collective-permute-start(bf16[32,2176]{1,0:T(8,128)(2,1)S(1)} %get-tuple-element.38.refs_0_), channel_id=1, source_target_pairs={{0,2},{1,3},{2,0},{3,1},{4,6},{5,7},{6,4},{7,5},{8,10},{9,11},{10,... | collective-permute-start | bytes 417800 | tf_op jit(solution)/shard_map/ppermute | solution.py:312
  8.8 6.0 %collective-permute-start.3 = (bf16[32,2176]{1,0:T(8,128)(2,1)S(1)}, bf16[32,2176]{1,0:T(8,128)(2,1)S(1)}, u32[]{:S(2)}, u32[]{:S(2)}) collective-permute-start(bf16[32,2176]{1,0:T(8,128)(2,1)S(1)} %get-tuple-element.38.refs_0_), channel_id=1, source_target_pairs={{0,1},{1,0},{2,3},{3,2},{4,5},{5,4},{6,7},{7,6},{8,9},{9,8},{10,11... | collective-permute-start | bytes 417800 | tf_op jit(solution)/shard_map/ppermute | solution.py:312
  10.9 6.2 %collective-permute-start.8 = (bf16[32,2176]{1,0:T(8,128)(2,1)S(1)}, bf16[32,2176]{1,0:T(8,128)(2,1)S(1)}, u32[]{:S(2)}, u32[]{:S(2)}) collective-permute-start(bf16[32,2176]{1,0:T(8,128)(2,1)S(1)} %collective-permute-done.6.refs_4_), channel_id=1, source_target_pairs={{0,2},{1,3},{2,0},{3,1},{4,6},{5,7},{6,4},{7,5},{8,10},{9,11},{10,... | collective-permute-start | bytes 417800 | tf_op jit(solution)/shard_map/ppermute | solution.py:312
  13.8 5.1 %collective-permute-start.1 = (bf16[32,2176]{1,0:T(8,128)(2,1)S(1)}, bf16[32,2176]{1,0:T(8,128)(2,1)S(1)}, u32[]{:S(2)}, u32[]{:S(2)}) collective-permute-start(bf16[32,2176]{1,0:T(8,128)(2,1)S(1)} %collective-permute-done.refs_0_), channel_id=1, source_target_pairs={{0,4},{1,5},{2,6},{3,7},{4,0},{5,1},{6,2},{7,3},{8,12},{9,13},{10,... | collective-permute-start | bytes 417800 | tf_op jit(solution)/shard_map/ppermute | solution.py:312
  14.2 8.4 %collective-permute-start.7 = (bf16[32,2176]{1,0:T(8,128)(2,1)S(1)}, bf16[32,2176]{1,0:T(8,128)(2,1)S(1)}, u32[]{:S(2)}, u32[]{:S(2)}) collective-permute-start(bf16[32,2176]{1,0:T(8,128)(2,1)S(1)} %collective-permute-done.6.refs_4_), channel_id=1, source_target_pairs={{0,1},{1,0},{2,3},{3,2},{4,5},{5,4},{6,7},{7,6},{8,9},{9,8},{10,11... | collective-permute-start | bytes 417800 | tf_op jit(solution)/shard_map/ppermute | solution.py:312
  14.2 8.5 %collective-permute-start.5 = (bf16[32,2176]{1,0:T(8,128)(2,1)S(1)}, bf16[32,2176]{1,0:T(8,128)(2,1)S(1)}, u32[]{:S(2)}, u32[]{:S(2)}) collective-permute-start(bf16[32,2176]{1,0:T(8,128)(2,1)S(1)} %collective-permute-done.4.refs_2_), channel_id=1, source_target_pairs={{0,1},{1,0},{2,3},{3,2},{4,5},{5,4},{6,7},{7,6},{8,9},{9,8},{10,11... | collective-permute-start | bytes 417800 | tf_op jit(solution)/shard_map/ppermute | solution.py:312
  14.7 8.5 %collective-permute-start.11 = (bf16[32,2176]{1,0:T(8,128)(2,1)S(1)}, bf16[32,2176]{1,0:T(8,128)(2,1)S(1)}, u32[]{:S(2)}, u32[]{:S(2)}) collective-permute-start(bf16[32,2176]{1,0:T(8,128)(2,1)S(1)} %collective-permute-done.refs_0_), channel_id=1, source_target_pairs={{0,2},{1,3},{2,0},{3,1},{4,6},{5,7},{6,4},{7,5},{8,10},{9,11},{10,... | collective-permute-start | bytes 417800 | tf_op jit(solution)/shard_map/ppermute | solution.py:312
  17.0 6.2 %collective-permute-start.9 = (bf16[32,2176]{1,0:T(8,128)(2,1)S(1)}, bf16[32,2176]{1,0:T(8,128)(2,1)S(1)}, u32[]{:S(2)}, u32[]{:S(2)}) collective-permute-start(bf16[32,2176]{1,0:T(8,128)(2,1)S(1)} %collective-permute-done.8.refs_6_), channel_id=1, source_target_pairs={{0,1},{1,0},{2,3},{3,2},{4,5},{5,4},{6,7},{7,6},{8,9},{9,8},{10,11... | collective-permute-start | bytes 417800 | tf_op jit(solution)/shard_map/ppermute | solution.py:312
  18.8 5.2 %collective-permute-start.2 = (bf16[32,2176]{1,0:T(8,128)(2,1)S(1)}, bf16[32,2176]{1,0:T(8,128)(2,1)S(1)}, u32[]{:S(2)}, u32[]{:S(2)}) collective-permute-start(bf16[32,2176]{1,0:T(8,128)(2,1)S(1)} %collective-permute-done.1.refs_4_), channel_id=1, source_target_pairs={{0,2},{1,3},{2,0},{3,1},{4,6},{5,7},{6,4},{7,5},{8,10},{9,11},{10,... | collective-permute-start | bytes 417800 | tf_op jit(solution)/shard_map/ppermute | solution.py:312
  22.6 2.8 %collective-permute-start.10 = (bf16[32,2176]{1,0:T(8,128)(2,1)S(1)}, bf16[32,2176]{1,0:T(8,128)(2,1)S(1)}, u32[]{:S(2)}, u32[]{:S(2)}) collective-permute-start(bf16[32,2176]{1,0:T(8,128)(2,1)S(1)} %collective-permute-done.refs_0_), channel_id=1, source_target_pairs={{0,1},{1,0},{2,3},{3,2},{4,5},{5,4},{6,7},{7,6},{8,9},{9,8},{10,11... | collective-permute-start | bytes 417800 | tf_op jit(solution)/shard_map/ppermute | solution.py:312
  22.7 2.7 %collective-permute-start.13 = (bf16[32,2176]{1,0:T(8,128)(2,1)S(1)}, bf16[32,2176]{1,0:T(8,128)(2,1)S(1)}, u32[]{:S(2)}, u32[]{:S(2)}) collective-permute-start(bf16[32,2176]{1,0:T(8,128)(2,1)S(1)} %collective-permute-done.1.refs_4_), channel_id=1, source_target_pairs={{0,1},{1,0},{2,3},{3,2},{4,5},{5,4},{6,7},{7,6},{8,9},{9,8},{10,11... | collective-permute-start | bytes 417800 | tf_op jit(solution)/shard_map/ppermute | solution.py:312
  23.2 2.2 %collective-permute-start.12 = (bf16[32,2176]{1,0:T(8,128)(2,1)S(1)}, bf16[32,2176]{1,0:T(8,128)(2,1)S(1)}, u32[]{:S(2)}, u32[]{:S(2)}) collective-permute-start(bf16[32,2176]{1,0:T(8,128)(2,1)S(1)} %collective-permute-done.11.refs_2_), channel_id=1, source_target_pairs={{0,1},{1,0},{2,3},{3,2},{4,5},{5,4},{6,7},{7,6},{8,9},{9,8},{10,11... | collective-permute-start | bytes 417800 | tf_op jit(solution)/shard_map/ppermute | solution.py:312
  24.0 1.4 %collective-permute-start.14 = (bf16[32,2176]{1,0:T(8,128)(2,1)S(1)}, bf16[32,2176]{1,0:T(8,128)(2,1)S(1)}, u32[]{:S(2)}, u32[]{:S(2)}) collective-permute-start(bf16[32,2176]{1,0:T(8,128)(2,1)S(1)} %collective-permute-done.2.refs_6_), channel_id=1, source_target_pairs={{0,1},{1,0},{2,3},{3,2},{4,5},{5,4},{6,7},{7,6},{8,9},{9,8},{10,11... | collective-permute-start | bytes 417800 | tf_op jit(solution)/shard_map/ppermute | solution.py:312
  26.2 6.4 %collective-permute-start.15 = (f32[16,128]{1,0:T(8,128)S(1)}, f32[16,128]{1,0:T(8,128)S(1)}, u32[]{:S(2)}, u32[]{:S(2)}) collective-permute-start(f32[16,128]{1,0:T(8,128)S(1)} %get-tuple-element.59), channel_id=1, source_target_pairs={{0,12},{1,13},{2,14},{3,15},{4,8},{5,9},{6,10},{7,11},{8,4},{9,5},... | collective-permute-start | bytes 24584 | tf_op jit(solution)/shard_map/ppermute | solution.py:312
  28.7 4.5 %collective-permute-start.16 = (f32[16,128]{1,0:T(8,128)S(1)}, f32[16,128]{1,0:T(8,128)S(1)}, u32[]{:S(2)}, u32[]{:S(2)}) collective-permute-start(f32[16,128]{1,0:T(8,128)S(1)} %get-tuple-element.59), channel_id=1, source_target_pairs={{0,8},{1,9},{2,10},{3,11},{4,12},{5,13},{6,14},{7,15},{8,0},{9,1},... | collective-permute-start | bytes 24584 | tf_op jit(solution)/shard_map/ppermute | solution.py:312
  28.7 4.5 %collective-permute-start.17 = (f32[16,128]{1,0:T(8,128)S(1)}, f32[16,128]{1,0:T(8,128)S(1)}, u32[]{:S(2)}, u32[]{:S(2)}) collective-permute-start(f32[16,128]{1,0:T(8,128)S(1)} %get-tuple-element.59), channel_id=1, source_target_pairs={{0,4},{1,5},{2,6},{3,7},{4,0},{5,1},{6,2},{7,3},{8,12},{9,13},{10,... | collective-permute-start | bytes 24584 | tf_op jit(solution)/shard_map/ppermute | solution.py:312
  33.3 3.8 %collective-permute-start.18 = (f32[16,128]{1,0:T(8,128)S(1)}, f32[16,128]{1,0:T(8,128)S(1)}, u32[]{:S(2)}, u32[]{:S(2)}) collective-permute-start(f32[16,128]{1,0:T(8,128)S(1)} %select_select_fusion), channel_id=1, source_target_pairs={{0,3},{1,2},{2,1},{3,0},{4,7},{5,6},{6,5},{7,4},{8,11},{9,10},{10,... | collective-permute-start | bytes 24584 | tf_op jit(solution)/shard_map/ppermute | solution.py:312
  33.3 3.8 %collective-permute-start.19 = (f32[16,128]{1,0:T(8,128)S(1)}, f32[16,128]{1,0:T(8,128)S(1)}, u32[]{:S(2)}, u32[]{:S(2)}) collective-permute-start(f32[16,128]{1,0:T(8,128)S(1)} %select_select_fusion), channel_id=1, source_target_pairs={{0,2},{1,3},{2,0},{3,1},{4,6},{5,7},{6,4},{7,5},{8,10},{9,11},{10,... | collective-permute-start | bytes 24584 | tf_op jit(solution)/shard_map/ppermute | solution.py:312
  34.7 2.4 %collective-permute-start.20 = (f32[16,128]{1,0:T(8,128)S(1)}, f32[16,128]{1,0:T(8,128)S(1)}, u32[]{:S(2)}, u32[]{:S(2)}) collective-permute-start(f32[16,128]{1,0:T(8,128)S(1)} %select_select_fusion), channel_id=1, source_target_pairs={{0,1},{1,0},{2,3},{3,2},{4,5},{5,4},{6,7},{7,6},{8,9},{9,8},{10,11... | collective-permute-start | bytes 24584 | tf_op jit(solution)/shard_map/ppermute | solution.py:312

commit v8 on v7

--- a/solution.py
+++ b/solution.py
@@ -345,7 +345,7 @@
     near = [d for d in far if d < half]
     late = [d for d in far if d >= half]
     direct = [d for d in far if d & (d - 1) == 0]
-    for d in direct[::-1]:
+    for d in direct:
         blocks[d] = swap(payload, d)
     blocks[2] = swap(payload, 2)
     parameters = (
@@ -375,7 +375,7 @@
     for d in far:
         if d not in direct:
             blocks[d] = swap(blocks[half], d - half)
-    for d in far:
+    for d in far[::-1]:
         blocks[d + 2] = swap(blocks[d], 2)
     for d in [0] + near:
         blocks[d + 1] = swap(blocks[d], 1)

time: 38 us -> 38 us (level)
  no operation moved by 1% of the time
where the time goes in v8:
time: 38 us; the launch traced here: 37.8 us
  starting transfers between devices  20 us (53%)
  Pallas kernels  11.6 us (31%)
  waiting for transfers between devices  4.69 us (12%)
  other arithmetic  0.8 us (2%)
  between operations  0.75 us (2%)
    ppermute x21, starting transfers between devices, swap(): lax.ppermute(array, 'expert', [(i, i ^ distance) for i in range(count)])  20 us
    pallas_call x8, Pallas kernels, call(): pl.pallas_call(kernel, out_shape=tuple((jax.ShapeDtypeStruct(*out) if i i...  11.6 us
    ppermute x21, waiting for transfers between devices, swap(): lax.ppermute(array, 'expert', [(i, i ^ distance) for i in range(count)])  4.69 us
  transfers between devices with their start and end apart: 21, of which 4 were waited for; matrix products, arithmetic and copies ran while one was open for 0% of the time, Pallas kernels for 26%

profile of v8, /device:TPU:0, one launch (start us, length us, event | category | flops | bytes accessed | tf_op | source)
XLA Modules:
  0.0 37.8 jit_solution(17224556954709803045)
XLA Ops:
  0.6 1.0 %pack_kernel.1 = (bf16[32,2176]{1,0:T(8,128)(2,1)S(1)}, s32[8,32]{1,0:T(8,128)S(1)}) custom-call(bf16[32,2048]{1,0:T(8,128)(2,1)} %cotangent_hbm.1, s32[8,32]{1,0:T(8,128)} %bitcast.19, bf16[8,32]{1,0:T(8,128)(2,1)} %bitcast.21), custom_call_target="tpu_custom_call" | custom-call | tf_op jit(solution)/shard_map/pack_kernel/pallas_call | solution.py:315
  1.6 3.1 %collective-permute-start.6 = (bf16[32,2176]{1,0:T(8,128)(2,1)S(1)}, bf16[32,2176]{1,0:T(8,128)(2,1)S(1)}, u32[]{:S(2)}, u32[]{:S(2)}) collective-permute-start(bf16[32,2176]{1,0:T(8,128)(2,1)S(1)} %get-tuple-element.38.refs_0_), channel_id=1, source_target_pairs={{0,4},{1,5},{2,6},{3,7},{4,0},{5,1},{6,2},{7,3},{8,12},{9,13},{10,... | collective-permute-start | bytes 417800 | tf_op jit(solution)/shard_map/ppermute | solution.py:312
  4.7 2.6 %collective-permute-start = (bf16[32,2176]{1,0:T(8,128)(2,1)S(1)}, bf16[32,2176]{1,0:T(8,128)(2,1)S(1)}, u32[]{:S(2)}, u32[]{:S(2)}) collective-permute-start(bf16[32,2176]{1,0:T(8,128)(2,1)S(1)} %get-tuple-element.38.refs_0_), channel_id=1, source_target_pairs={{0,8},{1,9},{2,10},{3,11},{4,12},{5,13},{6,14},{7,15},{8,0},{9,1},... | collective-permute-start | bytes 417800 | tf_op jit(solution)/shard_map/ppermute | solution.py:312
  7.3 1.5 %collective-permute-start.4 = (bf16[32,2176]{1,0:T(8,128)(2,1)S(1)}, bf16[32,2176]{1,0:T(8,128)(2,1)S(1)}, u32[]{:S(2)}, u32[]{:S(2)}) collective-permute-start(bf16[32,2176]{1,0:T(8,128)(2,1)S(1)} %get-tuple-element.38.refs_0_), channel_id=1, source_target_pairs={{0,2},{1,3},{2,0},{3,1},{4,6},{5,7},{6,4},{7,5},{8,10},{9,11},{10,... | collective-permute-start | bytes 417800 | tf_op jit(solution)/shard_map/ppermute | solution.py:312
  8.8 0.0 collective-permute-start.3
  8.8 2.1 %load_kernel.1 = (bf16[384,768]{1,0:T(8,128)(2,1)S(1)}, bf16[768,2048]{1,0:T(8,128)(2,1)S(1)}, bf16[32,768]{1,0:T(8,128)(2,1)S(1)}, bf16[32,2048]{1,0:T(8,128)(2,1)S(1)}) custom-call(bf16[384,768]{1,0:T(8,128)(2,1)} %bitcast.16, bf16[768,2048]{1,0:T(8,128)(2,1)} %bitcast.14, bf16[32,768]{1,0:T(8,128)(2,1)} %bitcast.18, bf16[32,2048]{1,0:T(8,128)(2,1)} %bitcast.17), custom_call_target="tpu_custom_call" | custom-call | tf_op jit(solution)/shard_map/load_kernel/pallas_call | solution.py:315
  10.9 0.0 collective-permute-done.6.refs_4_
  10.9 1.5 %collective-permute-start.8 = (bf16[32,2176]{1,0:T(8,128)(2,1)S(1)}, bf16[32,2176]{1,0:T(8,128)(2,1)S(1)}, u32[]{:S(2)}, u32[]{:S(2)}) collective-permute-start(bf16[32,2176]{1,0:T(8,128)(2,1)S(1)} %collective-permute-done.6.refs_4_), channel_id=1, source_target_pairs={{0,2},{1,3},{2,0},{3,1},{4,6},{5,7},{6,4},{7,5},{8,10},{9,11},{10,... | collective-permute-start | bytes 417800 | tf_op jit(solution)/shard_map/ppermute | solution.py:312
  12.4 1.4 %collective-permute-done.refs_0_ = bf16[32,2176]{1,0:T(8,128)(2,1)S(1)} collective-permute-done((bf16[32,2176]{1,0:T(8,128)(2,1)S(1)}, bf16[32,2176]{1,0:T(8,128)(2,1)S(1)}, u32[]{:S(2)}, u32[]{:S(2)}) %collective-permute-start) | collective-permute-done | bytes 139296 | tf_op jit(solution)/shard_map/ppermute | solution.py:312
  13.8 0.4 %collective-permute-start.1 = (bf16[32,2176]{1,0:T(8,128)(2,1)S(1)}, bf16[32,2176]{1,0:T(8,128)(2,1)S(1)}, u32[]{:S(2)}, u32[]{:S(2)}) collective-permute-start(bf16[32,2176]{1,0:T(8,128)(2,1)S(1)} %collective-permute-done.refs_0_), channel_id=1, source_target_pairs={{0,4},{1,5},{2,6},{3,7},{4,0},{5,1},{6,2},{7,3},{8,12},{9,13},{10,... | collective-permute-start | bytes 417800 | tf_op jit(solution)/shard_map/ppermute | solution.py:312
  14.2 0.0 collective-permute-start.7
  14.2 0.0 collective-permute-done.4.refs_2_
  14.2 0.5 %collective-permute-start.5 = (bf16[32,2176]{1,0:T(8,128)(2,1)S(1)}, bf16[32,2176]{1,0:T(8,128)(2,1)S(1)}, u32[]{:S(2)}, u32[]{:S(2)}) collective-permute-start(bf16[32,2176]{1,0:T(8,128)(2,1)S(1)} %collective-permute-done.4.refs_2_), channel_id=1, source_target_pairs={{0,1},{1,0},{2,3},{3,2},{4,5},{5,4},{6,7},{7,6},{8,9},{9,8},{10,11... | collective-permute-start | bytes 417800 | tf_op jit(solution)/shard_map/ppermute | solution.py:312
  14.7 0.0 collective-permute-done.3.refs_1_
  14.7 1.5 %collective-permute-start.11 = (bf16[32,2176]{1,0:T(8,128)(2,1)S(1)}, bf16[32,2176]{1,0:T(8,128)(2,1)S(1)}, u32[]{:S(2)}, u32[]{:S(2)}) collective-permute-start(bf16[32,2176]{1,0:T(8,128)(2,1)S(1)} %collective-permute-done.refs_0_), channel_id=1, source_target_pairs={{0,2},{1,3},{2,0},{3,1},{4,6},{5,7},{6,4},{7,5},{8,10},{9,11},{10,... | collective-permute-start | bytes 417800 | tf_op jit(solution)/shard_map/ppermute | solution.py:312
  16.2 0.8 %collective-permute-done.8.refs_6_ = bf16[32,2176]{1,0:T(8,128)(2,1)S(1)} collective-permute-done((bf16[32,2176]{1,0:T(8,128)(2,1)S(1)}, bf16[32,2176]{1,0:T(8,128)(2,1)S(1)}, u32[]{:S(2)}, u32[]{:S(2)}) %collective-permute-start.8) | collective-permute-done | bytes 139296 | tf_op jit(solution)/shard_map/ppermute | solution.py:312
  17.0 0.0 collective-permute-start.9
  17.0 1.8 %collective-permute-done.1.refs_4_ = bf16[32,2176]{1,0:T(8,128)(2,1)S(1)} collective-permute-done((bf16[32,2176]{1,0:T(8,128)(2,1)S(1)}, bf16[32,2176]{1,0:T(8,128)(2,1)S(1)}, u32[]{:S(2)}, u32[]{:S(2)}) %collective-permute-start.1) | collective-permute-done | bytes 139296 | tf_op jit(solution)/shard_map/ppermute | solution.py:312
  18.8 1.5 %collective-permute-start.2 = (bf16[32,2176]{1,0:T(8,128)(2,1)S(1)}, bf16[32,2176]{1,0:T(8,128)(2,1)S(1)}, u32[]{:S(2)}, u32[]{:S(2)}) collective-permute-start(bf16[32,2176]{1,0:T(8,128)(2,1)S(1)} %collective-permute-done.1.refs_4_), channel_id=1, source_target_pairs={{0,2},{1,3},{2,0},{3,1},{4,6},{5,7},{6,4},{7,5},{8,10},{9,11},{10,... | collective-permute-start | bytes 417800 | tf_op jit(solution)/shard_map/ppermute | solution.py:312
  20.3 2.3 %forward_kernel.1 = (bf16[192,32]{1,0:T(8,128)(2,1)S(1)}, bf16[192,32]{1,0:T(8,128)(2,1)S(1)}, f32[192,2048]{1,0:T(8,128)S(1)}, f32[192,2048]{1,0:T(8,128)S(1)}) custom-call(bf16[384,768]{1,0:T(8,128)(2,1)S(1)} %get-tuple-element.44.hidden.hidden_ref, bf16[768,2048]{1,0:T(8,128)(2,1)S(1)} %get-tuple-element.45.down.down_ref, ...), custom_call_target="tpu_custom_call" | custom-call | tf_op jit(solution)/shard_map/forward_kernel/pallas_call | solution.py:315
  22.6 0.0 collective-permute-done.7.refs_5_
  22.6 0.1 collective-permute-start.10
  22.7 0.0 collective-permute-done.5.refs_3_
  22.7 0.5 %collective-permute-start.13 = (bf16[32,2176]{1,0:T(8,128)(2,1)S(1)}, bf16[32,2176]{1,0:T(8,128)(2,1)S(1)}, u32[]{:S(2)}, u32[]{:S(2)}) collective-permute-start(bf16[32,2176]{1,0:T(8,128)(2,1)S(1)} %collective-permute-done.1.refs_4_), channel_id=1, source_target_pairs={{0,1},{1,0},{2,3},{3,2},{4,5},{5,4},{6,7},{7,6},{8,9},{9,8},{10,11... | collective-permute-start | bytes 417800 | tf_op jit(solution)/shard_map/ppermute | solution.py:312
  23.2 0.0 collective-permute-done.11.refs_2_
  23.2 0.1 collective-permute-start.12
  23.3 0.0 collective-permute-done.9.refs_7_
  23.3 0.7 %first_kernel.1 = (bf16[192,2048]{1,0:T(8,128)(2,1)S(1)}, f32[8,128]{1,0:T(8,128)S(1)}) custom-call(bf16[32,2176]{1,0:T(8,128)(2,1)S(1)} %get-tuple-element.38.refs_0_, bf16[32,2176]{1,0:T(8,128)(2,1)S(1)} %collective-permute-done.3.refs_1_, bf16[32,2176]{1,0:T(8,128)(2,1)S(1)} %collective-permute-done.4.refs_2_, ...), custom_call_target="tpu_custom_call" | custom-call | tf_op jit(solution)/shard_map/first_kernel/pallas_call | solution.py:315
  24.0 0.0 collective-permute-done.2.refs_6_
  24.0 0.4 %collective-permute-start.14 = (bf16[32,2176]{1,0:T(8,128)(2,1)S(1)}, bf16[32,2176]{1,0:T(8,128)(2,1)S(1)}, u32[]{:S(2)}, u32[]{:S(2)}) collective-permute-start(bf16[32,2176]{1,0:T(8,128)(2,1)S(1)} %collective-permute-done.2.refs_6_), channel_id=1, source_target_pairs={{0,1},{1,0},{2,3},{3,2},{4,5},{5,4},{6,7},{7,6},{8,9},{9,8},{10,11... | collective-permute-start | bytes 417800 | tf_op jit(solution)/shard_map/ppermute | solution.py:312
  24.5 0.9 %early_kernel.1 = (bf16[192,32]{1,0:T(8,128)(2,1)S(1)}, f32[32,768]{1,0:T(8,128)S(1)}, f32[32,2048]{1,0:T(8,128)S(1)}) custom-call(bf16[192,2048]{1,0:T(8,128)(2,1)S(1)} %get-tuple-element.51.scaled_ref, bf16[192,32]{1,0:T(8,128)(2,1)S(1)} %get-tuple-element.52.low_ref, bf16[384,768]{1,0:T(8,128)(2,1)S(1)} %get-tuple-element.44.hidden.hidden_ref, ...), custom_call_target="tpu_custom_call" | custom-call | tf_op jit(solution)/shard_map/early_kernel/pallas_call | solution.py:315
  25.4 0.0 collective-permute-done.10.refs_1_
  25.4 0.0 collective-permute-done.13.refs_5_
  25.4 0.0 collective-permute-done.12.refs_3_
  25.4 0.0 collective-permute-done.14.refs_7_
  25.5 0.7 %combine_kernel.1 = (bf16[192,2048]{1,0:T(8,128)(2,1)S(1)}, f32[16,128]{1,0:T(8,128)S(1)}) custom-call(bf16[32,2176]{1,0:T(8,128)(2,1)S(1)} %collective-permute-done.refs_0_, bf16[32,2176]{1,0:T(8,128)(2,1)S(1)} %collective-permute-done.10.refs_1_, bf16[32,2176]{1,0:T(8,128)(2,1)S(1)} %collective-permute-done.11.refs_2_, ...), custom_call_target="tpu_custom_call" | custom-call | tf_op jit(solution)/shard_map/combine_kernel/pallas_call | solution.py:315
  26.2 2.5 %collective-permute-start.15 = (f32[16,128]{1,0:T(8,128)S(1)}, f32[16,128]{1,0:T(8,128)S(1)}, u32[]{:S(2)}, u32[]{:S(2)}) collective-permute-start(f32[16,128]{1,0:T(8,128)S(1)} %get-tuple-element.59), channel_id=1, source_target_pairs={{0,12},{1,13},{2,14},{3,15},{4,8},{5,9},{6,10},{7,11},{8,4},{9,5},... | collective-permute-start | bytes 24584 | tf_op jit(solution)/shard_map/ppermute | solution.py:312
  28.7 0.0 collective-permute-start.16
  28.7 1.9 %collective-permute-start.17 = (f32[16,128]{1,0:T(8,128)S(1)}, f32[16,128]{1,0:T(8,128)S(1)}, u32[]{:S(2)}, u32[]{:S(2)}) collective-permute-start(f32[16,128]{1,0:T(8,128)S(1)} %get-tuple-element.59), channel_id=1, source_target_pairs={{0,4},{1,5},{2,6},{3,7},{4,0},{5,1},{6,2},{7,3},{8,12},{9,13},{10,... | collective-permute-start | bytes 24584 | tf_op jit(solution)/shard_map/ppermute | solution.py:312
  30.6 2.0 %late_kernel.1 = (bf16[192,768]{1,0:T(8,128)(2,1)S(1)}, f32[32,768]{1,0:T(8,128)}, f32[32,2048]{1,0:T(8,128)}) custom-call(bf16[192,2048]{1,0:T(8,128)(2,1)S(1)} %get-tuple-element.60.scaled_ref, bf16[192,32]{1,0:T(8,128)(2,1)S(1)} %get-tuple-element.61.low_ref, bf16[384,768]{1,0:T(8,128)(2,1)S(1)} %get-tuple-element.44.hidden.hidden_ref, ...), custom_call_target="tpu_custom_call" | custom-call | tf_op jit(solution)/shard_map/late_kernel/pallas_call | solution.py:315
  32.6 0.0 collective-permute-done.15
  32.6 0.6 %collective-permute-done.16 = f32[16,128]{1,0:T(8,128)S(1)} collective-permute-done((f32[16,128]{1,0:T(8,128)S(1)}, f32[16,128]{1,0:T(8,128)S(1)}, u32[]{:S(2)}, u32[]{:S(2)}) %collective-permute-start.16) | collective-permute-done | bytes 8224 | tf_op jit(solution)/shard_map/ppermute | solution.py:312
  33.2 0.0 collective-permute-done.17
  33.2 0.1 select_select_fusion
  33.3 0.0 collective-permute-start.18
  33.3 1.3 %collective-permute-start.19 = (f32[16,128]{1,0:T(8,128)S(1)}, f32[16,128]{1,0:T(8,128)S(1)}, u32[]{:S(2)}, u32[]{:S(2)}) collective-permute-start(f32[16,128]{1,0:T(8,128)S(1)} %select_select_fusion), channel_id=1, source_target_pairs={{0,2},{1,3},{2,0},{3,1},{4,6},{5,7},{6,4},{7,5},{8,10},{9,11},{10,... | collective-permute-start | bytes 24584 | tf_op jit(solution)/shard_map/ppermute | solution.py:312
  34.7 0.5 %collective-permute-start.20 = (f32[16,128]{1,0:T(8,128)S(1)}, f32[16,128]{1,0:T(8,128)S(1)}, u32[]{:S(2)}, u32[]{:S(2)}) collective-permute-start(f32[16,128]{1,0:T(8,128)S(1)} %select_select_fusion), channel_id=1, source_target_pairs={{0,1},{1,0},{2,3},{3,2},{4,5},{5,4},{6,7},{7,6},{8,9},{9,8},{10,11... | collective-permute-start | bytes 24584 | tf_op jit(solution)/shard_map/ppermute | solution.py:312
  35.2 1.9 %cotangent_kernel.1 = bf16[384,768]{1,0:T(8,128)(2,1)} custom-call(bf16[192,2048]{1,0:T(8,128)(2,1)S(1)} %get-tuple-element.51.scaled_ref, bf16[192,32]{1,0:T(8,128)(2,1)S(1)} %get-tuple-element.53.lowered_ref, bf16[768,2048]{1,0:T(8,128)(2,1)S(1)} %get-tuple-element.45.down.down_ref, bf16[32,768]{1,0:T(8,128)(2,1)S(1)} %get-tuple-element.46.first.first_ref, ...), custom_call_target="tpu_custom_call" | custom-call | tf_op jit(solution)/shard_map/cotangent_kernel/pallas_call | solution.py:315
  37.1 0.0 collective-permute-done.18
  37.1 0.0 collective-permute-done.19
  37.1 0.0 collective-permute-done.20
  37.1 0.1 slice_select_fusion
  37.2 0.6 %select_reduce_fusion = f32[8,32]{1,0:T(8,128)} fusion(f32[16,32]{1,0:T(8,128)S(1)} %slice_select_fusion, s32[8,32]{1,0:T(8,128)S(1)} %get-tuple-element.70), kind=kLoop, calls=%fused_computation | loop fusion | flops 12032 | bytes 4096 | tf_op jit(solution)/shard_map/reduce_sum | solution.py:462
  (4 shorter events, 0.0 us)
Async XLA Ops:
  1.6 9.3 %collective-permute-start.6 = (bf16[32,2176]{1,0:T(8,128)(2,1)S(1)}, bf16[32,2176]{1,0:T(8,128)(2,1)S(1)}, u32[]{:S(2)}, u32[]{:S(2)}) collective-permute-start(bf16[32,2176]{1,0:T(8,128)(2,1)S(1)} %get-tuple-element.38.refs_0_), channel_id=1, source_target_pairs={{0,4},{1,5},{2,6},{3,7},{4,0},{5,1},{6,2},{7,3},{8,12},{9,13},{10,... | collective-permute-start | bytes 417800 | tf_op jit(solution)/shard_map/ppermute | solution.py:312
  4.7 9.1 %collective-permute-start = (bf16[32,2176]{1,0:T(8,128)(2,1)S(1)}, bf16[32,2176]{1,0:T(8,128)(2,1)S(1)}, u32[]{:S(2)}, u32[]{:S(2)}) collective-permute-start(bf16[32,2176]{1,0:T(8,128)(2,1)S(1)} %get-tuple-element.38.refs_0_), channel_id=1, source_target_pairs={{0,8},{1,9},{2,10},{3,11},{4,12},{5,13},{6,14},{7,15},{8,0},{9,1},... | collective-permute-start | bytes 417800 | tf_op jit(solution)/shard_map/ppermute | solution.py:312
  7.3 6.9 %collective-permute-start.4 = (bf16[32,2176]{1,0:T(8,128)(2,1)S(1)}, bf16[32,2176]{1,0:T(8,128)(2,1)S(1)}, u32[]{:S(2)}, u32[]{:S(2)}) collective-permute-start(bf16[32,2176]{1,0:T(8,128)(2,1)S(1)} %get-tuple-element.38.refs_0_), channel_id=1, source_target_pairs={{0,2},{1,3},{2,0},{3,1},{4,6},{5,7},{6,4},{7,5},{8,10},{9,11},{10,... | collective-permute-start | bytes 417800 | tf_op jit(solution)/shard_map/ppermute | solution.py:312
  8.8 6.0 %collective-permute-start.3 = (bf16[32,2176]{1,0:T(8,128)(2,1)S(1)}, bf16[32,2176]{1,0:T(8,128)(2,1)S(1)}, u32[]{:S(2)}, u32[]{:S(2)}) collective-permute-start(bf16[32,2176]{1,0:T(8,128)(2,1)S(1)} %get-tuple-element.38.refs_0_), channel_id=1, source_target_pairs={{0,1},{1,0},{2,3},{3,2},{4,5},{5,4},{6,7},{7,6},{8,9},{9,8},{10,11... | collective-permute-start | bytes 417800 | tf_op jit(solution)/shard_map/ppermute | solution.py:312
  10.9 6.2 %collective-permute-start.8 = (bf16[32,2176]{1,0:T(8,128)(2,1)S(1)}, bf16[32,2176]{1,0:T(8,128)(2,1)S(1)}, u32[]{:S(2)}, u32[]{:S(2)}) collective-permute-start(bf16[32,2176]{1,0:T(8,128)(2,1)S(1)} %collective-permute-done.6.refs_4_), channel_id=1, source_target_pairs={{0,2},{1,3},{2,0},{3,1},{4,6},{5,7},{6,4},{7,5},{8,10},{9,11},{10,... | collective-permute-start | bytes 417800 | tf_op jit(solution)/shard_map/ppermute | solution.py:312
  13.8 5.1 %collective-permute-start.1 = (bf16[32,2176]{1,0:T(8,128)(2,1)S(1)}, bf16[32,2176]{1,0:T(8,128)(2,1)S(1)}, u32[]{:S(2)}, u32[]{:S(2)}) collective-permute-start(bf16[32,2176]{1,0:T(8,128)(2,1)S(1)} %collective-permute-done.refs_0_), channel_id=1, source_target_pairs={{0,4},{1,5},{2,6},{3,7},{4,0},{5,1},{6,2},{7,3},{8,12},{9,13},{10,... | collective-permute-start | bytes 417800 | tf_op jit(solution)/shard_map/ppermute | solution.py:312
  14.2 8.4 %collective-permute-start.7 = (bf16[32,2176]{1,0:T(8,128)(2,1)S(1)}, bf16[32,2176]{1,0:T(8,128)(2,1)S(1)}, u32[]{:S(2)}, u32[]{:S(2)}) collective-permute-start(bf16[32,2176]{1,0:T(8,128)(2,1)S(1)} %collective-permute-done.6.refs_4_), channel_id=1, source_target_pairs={{0,1},{1,0},{2,3},{3,2},{4,5},{5,4},{6,7},{7,6},{8,9},{9,8},{10,11... | collective-permute-start | bytes 417800 | tf_op jit(solution)/shard_map/ppermute | solution.py:312
  14.2 8.5 %collective-permute-start.5 = (bf16[32,2176]{1,0:T(8,128)(2,1)S(1)}, bf16[32,2176]{1,0:T(8,128)(2,1)S(1)}, u32[]{:S(2)}, u32[]{:S(2)}) collective-permute-start(bf16[32,2176]{1,0:T(8,128)(2,1)S(1)} %collective-permute-done.4.refs_2_), channel_id=1, source_target_pairs={{0,1},{1,0},{2,3},{3,2},{4,5},{5,4},{6,7},{7,6},{8,9},{9,8},{10,11... | collective-permute-start | bytes 417800 | tf_op jit(solution)/shard_map/ppermute | solution.py:312
  14.7 8.5 %collective-permute-start.11 = (bf16[32,2176]{1,0:T(8,128)(2,1)S(1)}, bf16[32,2176]{1,0:T(8,128)(2,1)S(1)}, u32[]{:S(2)}, u32[]{:S(2)}) collective-permute-start(bf16[32,2176]{1,0:T(8,128)(2,1)S(1)} %collective-permute-done.refs_0_), channel_id=1, source_target_pairs={{0,2},{1,3},{2,0},{3,1},{4,6},{5,7},{6,4},{7,5},{8,10},{9,11},{10,... | collective-permute-start | bytes 417800 | tf_op jit(solution)/shard_map/ppermute | solution.py:312
  17.0 6.2 %collective-permute-start.9 = (bf16[32,2176]{1,0:T(8,128)(2,1)S(1)}, bf16[32,2176]{1,0:T(8,128)(2,1)S(1)}, u32[]{:S(2)}, u32[]{:S(2)}) collective-permute-start(bf16[32,2176]{1,0:T(8,128)(2,1)S(1)} %collective-permute-done.8.refs_6_), channel_id=1, source_target_pairs={{0,1},{1,0},{2,3},{3,2},{4,5},{5,4},{6,7},{7,6},{8,9},{9,8},{10,11... | collective-permute-start | bytes 417800 | tf_op jit(solution)/shard_map/ppermute | solution.py:312
  18.8 5.2 %collective-permute-start.2 = (bf16[32,2176]{1,0:T(8,128)(2,1)S(1)}, bf16[32,2176]{1,0:T(8,128)(2,1)S(1)}, u32[]{:S(2)}, u32[]{:S(2)}) collective-permute-start(bf16[32,2176]{1,0:T(8,128)(2,1)S(1)} %collective-permute-done.1.refs_4_), channel_id=1, source_target_pairs={{0,2},{1,3},{2,0},{3,1},{4,6},{5,7},{6,4},{7,5},{8,10},{9,11},{10,... | collective-permute-start | bytes 417800 | tf_op jit(solution)/shard_map/ppermute | solution.py:312
  22.6 2.8 %collective-permute-start.10 = (bf16[32,2176]{1,0:T(8,128)(2,1)S(1)}, bf16[32,2176]{1,0:T(8,128)(2,1)S(1)}, u32[]{:S(2)}, u32[]{:S(2)}) collective-permute-start(bf16[32,2176]{1,0:T(8,128)(2,1)S(1)} %collective-permute-done.refs_0_), channel_id=1, source_target_pairs={{0,1},{1,0},{2,3},{3,2},{4,5},{5,4},{6,7},{7,6},{8,9},{9,8},{10,11... | collective-permute-start | bytes 417800 | tf_op jit(solution)/shard_map/ppermute | solution.py:312
  22.7 2.7 %collective-permute-start.13 = (bf16[32,2176]{1,0:T(8,128)(2,1)S(1)}, bf16[32,2176]{1,0:T(8,128)(2,1)S(1)}, u32[]{:S(2)}, u32[]{:S(2)}) collective-permute-start(bf16[32,2176]{1,0:T(8,128)(2,1)S(1)} %collective-permute-done.1.refs_4_), channel_id=1, source_target_pairs={{0,1},{1,0},{2,3},{3,2},{4,5},{5,4},{6,7},{7,6},{8,9},{9,8},{10,11... | collective-permute-start | bytes 417800 | tf_op jit(solution)/shard_map/ppermute | solution.py:312
  23.2 2.2 %collective-permute-start.12 = (bf16[32,2176]{1,0:T(8,128)(2,1)S(1)}, bf16[32,2176]{1,0:T(8,128)(2,1)S(1)}, u32[]{:S(2)}, u32[]{:S(2)}) collective-permute-start(bf16[32,2176]{1,0:T(8,128)(2,1)S(1)} %collective-permute-done.11.refs_2_), channel_id=1, source_target_pairs={{0,1},{1,0},{2,3},{3,2},{4,5},{5,4},{6,7},{7,6},{8,9},{9,8},{10,11... | collective-permute-start | bytes 417800 | tf_op jit(solution)/shard_map/ppermute | solution.py:312
  24.0 1.4 %collective-permute-start.14 = (bf16[32,2176]{1,0:T(8,128)(2,1)S(1)}, bf16[32,2176]{1,0:T(8,128)(2,1)S(1)}, u32[]{:S(2)}, u32[]{:S(2)}) collective-permute-start(bf16[32,2176]{1,0:T(8,128)(2,1)S(1)} %collective-permute-done.2.refs_6_), channel_id=1, source_target_pairs={{0,1},{1,0},{2,3},{3,2},{4,5},{5,4},{6,7},{7,6},{8,9},{9,8},{10,11... | collective-permute-start | bytes 417800 | tf_op jit(solution)/shard_map/ppermute | solution.py:312
  26.2 6.4 %collective-permute-start.15 = (f32[16,128]{1,0:T(8,128)S(1)}, f32[16,128]{1,0:T(8,128)S(1)}, u32[]{:S(2)}, u32[]{:S(2)}) collective-permute-start(f32[16,128]{1,0:T(8,128)S(1)} %get-tuple-element.59), channel_id=1, source_target_pairs={{0,12},{1,13},{2,14},{3,15},{4,8},{5,9},{6,10},{7,11},{8,4},{9,5},... | collective-permute-start | bytes 24584 | tf_op jit(solution)/shard_map/ppermute | solution.py:312
  28.7 4.5 %collective-permute-start.16 = (f32[16,128]{1,0:T(8,128)S(1)}, f32[16,128]{1,0:T(8,128)S(1)}, u32[]{:S(2)}, u32[]{:S(2)}) collective-permute-start(f32[16,128]{1,0:T(8,128)S(1)} %get-tuple-element.59), channel_id=1, source_target_pairs={{0,8},{1,9},{2,10},{3,11},{4,12},{5,13},{6,14},{7,15},{8,0},{9,1},... | collective-permute-start | bytes 24584 | tf_op jit(solution)/shard_map/ppermute | solution.py:312
  28.7 4.5 %collective-permute-start.17 = (f32[16,128]{1,0:T(8,128)S(1)}, f32[16,128]{1,0:T(8,128)S(1)}, u32[]{:S(2)}, u32[]{:S(2)}) collective-permute-start(f32[16,128]{1,0:T(8,128)S(1)} %get-tuple-element.59), channel_id=1, source_target_pairs={{0,4},{1,5},{2,6},{3,7},{4,0},{5,1},{6,2},{7,3},{8,12},{9,13},{10,... | collective-permute-start | bytes 24584 | tf_op jit(solution)/shard_map/ppermute | solution.py:312
  33.3 3.8 %collective-permute-start.18 = (f32[16,128]{1,0:T(8,128)S(1)}, f32[16,128]{1,0:T(8,128)S(1)}, u32[]{:S(2)}, u32[]{:S(2)}) collective-permute-start(f32[16,128]{1,0:T(8,128)S(1)} %select_select_fusion), channel_id=1, source_target_pairs={{0,3},{1,2},{2,1},{3,0},{4,7},{5,6},{6,5},{7,4},{8,11},{9,10},{10,... | collective-permute-start | bytes 24584 | tf_op jit(solution)/shard_map/ppermute | solution.py:312
  33.3 3.8 %collective-permute-start.19 = (f32[16,128]{1,0:T(8,128)S(1)}, f32[16,128]{1,0:T(8,128)S(1)}, u32[]{:S(2)}, u32[]{:S(2)}) collective-permute-start(f32[16,128]{1,0:T(8,128)S(1)} %select_select_fusion), channel_id=1, source_target_pairs={{0,2},{1,3},{2,0},{3,1},{4,6},{5,7},{6,4},{7,5},{8,10},{9,11},{10,... | collective-permute-start | bytes 24584 | tf_op jit(solution)/shard_map/ppermute | solution.py:312
  34.7 2.4 %collective-permute-start.20 = (f32[16,128]{1,0:T(8,128)S(1)}, f32[16,128]{1,0:T(8,128)S(1)}, u32[]{:S(2)}, u32[]{:S(2)}) collective-permute-start(f32[16,128]{1,0:T(8,128)S(1)} %select_select_fusion), channel_id=1, source_target_pairs={{0,1},{1,0},{2,3},{3,2},{4,5},{5,4},{6,7},{7,6},{8,9},{9,8},{10,11... | collective-permute-start | bytes 24584 | tf_op jit(solution)/shard_map/ppermute | solution.py:312

commit v9 on v7

--- a/solution.py
+++ b/solution.py
@@ -208,7 +208,7 @@
         picks.append(pick)
     picker = jnp.concatenate([pick.astype(jnp.bfloat16) for pick in picks], axis=1)
     grads = jnp.zeros((slots, 1), jnp.float32)
-    for cut in pieces(width, 512):
+    for cut in pieces(width, 256):
         gathered_rows = jnp.concatenate([block[:, cut] for block in blocks], axis=0)
         rows = jnp.dot(picker, gathered_rows, preferred_element_type=jnp.float32)
         grads = grads + jnp.sum(rows * out_ref[:, cut], axis=1, keepdims=True)

time: 38 us -> 38 us (level)
  no operation moved by 1% of the time
where the time goes in v9:
time: 38 us; the launch traced here: 37.8 us
  starting transfers between devices  20 us (53%)
  Pallas kernels  11.6 us (31%)
  waiting for transfers between devices  4.68 us (12%)
  other arithmetic  0.8 us (2%)
  between operations  0.75 us (2%)
    ppermute x21, starting transfers between devices, swap(): lax.ppermute(array, 'expert', [(i, i ^ distance) for i in range(count)])  20 us
    pallas_call x8, Pallas kernels, call(): pl.pallas_call(kernel, out_shape=tuple((jax.ShapeDtypeStruct(*out) if i i...  11.6 us
    ppermute x21, waiting for transfers between devices, swap(): lax.ppermute(array, 'expert', [(i, i ^ distance) for i in range(count)])  4.68 us
  transfers between devices with their start and end apart: 21, of which 4 were waited for; matrix products, arithmetic and copies ran while one was open for 0% of the time, Pallas kernels for 26%

profile of v9, /device:TPU:0, one launch (start us, length us, event | category | flops | bytes accessed | tf_op | source)
XLA Modules:
  0.0 37.8 jit_solution(10678925420216654290)
XLA Ops:
  0.6 1.0 %pack_kernel.1 = (bf16[32,2176]{1,0:T(8,128)(2,1)S(1)}, s32[8,32]{1,0:T(8,128)S(1)}) custom-call(bf16[32,2048]{1,0:T(8,128)(2,1)} %cotangent_hbm.1, s32[8,32]{1,0:T(8,128)} %bitcast.19, bf16[8,32]{1,0:T(8,128)(2,1)} %bitcast.21), custom_call_target="tpu_custom_call" | custom-call | tf_op jit(solution)/shard_map/pack_kernel/pallas_call | solution.py:315
  1.6 3.1 %collective-permute-start.6 = (bf16[32,2176]{1,0:T(8,128)(2,1)S(1)}, bf16[32,2176]{1,0:T(8,128)(2,1)S(1)}, u32[]{:S(2)}, u32[]{:S(2)}) collective-permute-start(bf16[32,2176]{1,0:T(8,128)(2,1)S(1)} %get-tuple-element.38.refs_0_), channel_id=1, source_target_pairs={{0,4},{1,5},{2,6},{3,7},{4,0},{5,1},{6,2},{7,3},{8,12},{9,13},{10,... | collective-permute-start | bytes 417800 | tf_op jit(solution)/shard_map/ppermute | solution.py:312
  4.7 2.6 %collective-permute-start = (bf16[32,2176]{1,0:T(8,128)(2,1)S(1)}, bf16[32,2176]{1,0:T(8,128)(2,1)S(1)}, u32[]{:S(2)}, u32[]{:S(2)}) collective-permute-start(bf16[32,2176]{1,0:T(8,128)(2,1)S(1)} %get-tuple-element.38.refs_0_), channel_id=1, source_target_pairs={{0,8},{1,9},{2,10},{3,11},{4,12},{5,13},{6,14},{7,15},{8,0},{9,1},... | collective-permute-start | bytes 417800 | tf_op jit(solution)/shard_map/ppermute | solution.py:312
  7.3 1.5 %collective-permute-start.4 = (bf16[32,2176]{1,0:T(8,128)(2,1)S(1)}, bf16[32,2176]{1,0:T(8,128)(2,1)S(1)}, u32[]{:S(2)}, u32[]{:S(2)}) collective-permute-start(bf16[32,2176]{1,0:T(8,128)(2,1)S(1)} %get-tuple-element.38.refs_0_), channel_id=1, source_target_pairs={{0,2},{1,3},{2,0},{3,1},{4,6},{5,7},{6,4},{7,5},{8,10},{9,11},{10,... | collective-permute-start | bytes 417800 | tf_op jit(solution)/shard_map/ppermute | solution.py:312
  8.8 0.0 collective-permute-start.3
  8.8 2.1 %load_kernel.1 = (bf16[384,768]{1,0:T(8,128)(2,1)S(1)}, bf16[768,2048]{1,0:T(8,128)(2,1)S(1)}, bf16[32,768]{1,0:T(8,128)(2,1)S(1)}, bf16[32,2048]{1,0:T(8,128)(2,1)S(1)}) custom-call(bf16[384,768]{1,0:T(8,128)(2,1)} %bitcast.16, bf16[768,2048]{1,0:T(8,128)(2,1)} %bitcast.14, bf16[32,768]{1,0:T(8,128)(2,1)} %bitcast.18, bf16[32,2048]{1,0:T(8,128)(2,1)} %bitcast.17), custom_call_target="tpu_custom_call" | custom-call | tf_op jit(solution)/shard_map/load_kernel/pallas_call | solution.py:315
  10.9 0.0 collective-permute-done.6.refs_4_
  10.9 1.5 %collective-permute-start.8 = (bf16[32,2176]{1,0:T(8,128)(2,1)S(1)}, bf16[32,2176]{1,0:T(8,128)(2,1)S(1)}, u32[]{:S(2)}, u32[]{:S(2)}) collective-permute-start(bf16[32,2176]{1,0:T(8,128)(2,1)S(1)} %collective-permute-done.6.refs_4_), channel_id=1, source_target_pairs={{0,2},{1,3},{2,0},{3,1},{4,6},{5,7},{6,4},{7,5},{8,10},{9,11},{10,... | collective-permute-start | bytes 417800 | tf_op jit(solution)/shard_map/ppermute | solution.py:312
  12.4 1.4 %collective-permute-done.refs_0_ = bf16[32,2176]{1,0:T(8,128)(2,1)S(1)} collective-permute-done((bf16[32,2176]{1,0:T(8,128)(2,1)S(1)}, bf16[32,2176]{1,0:T(8,128)(2,1)S(1)}, u32[]{:S(2)}, u32[]{:S(2)}) %collective-permute-start) | collective-permute-done | bytes 139296 | tf_op jit(solution)/shard_map/ppermute | solution.py:312
  13.8 0.4 %collective-permute-start.1 = (bf16[32,2176]{1,0:T(8,128)(2,1)S(1)}, bf16[32,2176]{1,0:T(8,128)(2,1)S(1)}, u32[]{:S(2)}, u32[]{:S(2)}) collective-permute-start(bf16[32,2176]{1,0:T(8,128)(2,1)S(1)} %collective-permute-done.refs_0_), channel_id=1, source_target_pairs={{0,4},{1,5},{2,6},{3,7},{4,0},{5,1},{6,2},{7,3},{8,12},{9,13},{10,... | collective-permute-start | bytes 417800 | tf_op jit(solution)/shard_map/ppermute | solution.py:312
  14.2 0.0 collective-permute-start.7
  14.2 0.0 collective-permute-done.4.refs_2_
  14.2 0.5 %collective-permute-start.5 = (bf16[32,2176]{1,0:T(8,128)(2,1)S(1)}, bf16[32,2176]{1,0:T(8,128)(2,1)S(1)}, u32[]{:S(2)}, u32[]{:S(2)}) collective-permute-start(bf16[32,2176]{1,0:T(8,128)(2,1)S(1)} %collective-permute-done.4.refs_2_), channel_id=1, source_target_pairs={{0,1},{1,0},{2,3},{3,2},{4,5},{5,4},{6,7},{7,6},{8,9},{9,8},{10,11... | collective-permute-start | bytes 417800 | tf_op jit(solution)/shard_map/ppermute | solution.py:312
  14.7 0.0 collective-permute-done.3.refs_1_
  14.7 1.5 %collective-permute-start.11 = (bf16[32,2176]{1,0:T(8,128)(2,1)S(1)}, bf16[32,2176]{1,0:T(8,128)(2,1)S(1)}, u32[]{:S(2)}, u32[]{:S(2)}) collective-permute-start(bf16[32,2176]{1,0:T(8,128)(2,1)S(1)} %collective-permute-done.refs_0_), channel_id=1, source_target_pairs={{0,2},{1,3},{2,0},{3,1},{4,6},{5,7},{6,4},{7,5},{8,10},{9,11},{10,... | collective-permute-start | bytes 417800 | tf_op jit(solution)/shard_map/ppermute | solution.py:312
  16.2 0.8 %collective-permute-done.8.refs_6_ = bf16[32,2176]{1,0:T(8,128)(2,1)S(1)} collective-permute-done((bf16[32,2176]{1,0:T(8,128)(2,1)S(1)}, bf16[32,2176]{1,0:T(8,128)(2,1)S(1)}, u32[]{:S(2)}, u32[]{:S(2)}) %collective-permute-start.8) | collective-permute-done | bytes 139296 | tf_op jit(solution)/shard_map/ppermute | solution.py:312
  17.0 0.0 collective-permute-start.9
  17.0 1.8 %collective-permute-done.1.refs_4_ = bf16[32,2176]{1,0:T(8,128)(2,1)S(1)} collective-permute-done((bf16[32,2176]{1,0:T(8,128)(2,1)S(1)}, bf16[32,2176]{1,0:T(8,128)(2,1)S(1)}, u32[]{:S(2)}, u32[]{:S(2)}) %collective-permute-start.1) | collective-permute-done | bytes 139296 | tf_op jit(solution)/shard_map/ppermute | solution.py:312
  18.8 1.5 %collective-permute-start.2 = (bf16[32,2176]{1,0:T(8,128)(2,1)S(1)}, bf16[32,2176]{1,0:T(8,128)(2,1)S(1)}, u32[]{:S(2)}, u32[]{:S(2)}) collective-permute-start(bf16[32,2176]{1,0:T(8,128)(2,1)S(1)} %collective-permute-done.1.refs_4_), channel_id=1, source_target_pairs={{0,2},{1,3},{2,0},{3,1},{4,6},{5,7},{6,4},{7,5},{8,10},{9,11},{10,... | collective-permute-start | bytes 417800 | tf_op jit(solution)/shard_map/ppermute | solution.py:312
  20.3 2.3 %forward_kernel.1 = (bf16[192,32]{1,0:T(8,128)(2,1)S(1)}, bf16[192,32]{1,0:T(8,128)(2,1)S(1)}, f32[192,2048]{1,0:T(8,128)S(1)}, f32[192,2048]{1,0:T(8,128)S(1)}) custom-call(bf16[384,768]{1,0:T(8,128)(2,1)S(1)} %get-tuple-element.44.hidden.hidden_ref, bf16[768,2048]{1,0:T(8,128)(2,1)S(1)} %get-tuple-element.45.down.down_ref, ...), custom_call_target="tpu_custom_call" | custom-call | tf_op jit(solution)/shard_map/forward_kernel/pallas_call | solution.py:315
  22.6 0.0 collective-permute-done.7.refs_5_
  22.6 0.1 collective-permute-start.10
  22.7 0.0 collective-permute-done.5.refs_3_
  22.7 0.5 %collective-permute-start.13 = (bf16[32,2176]{1,0:T(8,128)(2,1)S(1)}, bf16[32,2176]{1,0:T(8,128)(2,1)S(1)}, u32[]{:S(2)}, u32[]{:S(2)}) collective-permute-start(bf16[32,2176]{1,0:T(8,128)(2,1)S(1)} %collective-permute-done.1.refs_4_), channel_id=1, source_target_pairs={{0,1},{1,0},{2,3},{3,2},{4,5},{5,4},{6,7},{7,6},{8,9},{9,8},{10,11... | collective-permute-start | bytes 417800 | tf_op jit(solution)/shard_map/ppermute | solution.py:312
  23.2 0.0 collective-permute-done.11.refs_2_
  23.2 0.1 collective-permute-start.12
  23.3 0.0 collective-permute-done.9.refs_7_
  23.3 0.8 %first_kernel.1 = (bf16[192,2048]{1,0:T(8,128)(2,1)S(1)}, f32[8,128]{1,0:T(8,128)S(1)}) custom-call(bf16[32,2176]{1,0:T(8,128)(2,1)S(1)} %get-tuple-element.38.refs_0_, bf16[32,2176]{1,0:T(8,128)(2,1)S(1)} %collective-permute-done.3.refs_1_, bf16[32,2176]{1,0:T(8,128)(2,1)S(1)} %collective-permute-done.4.refs_2_, ...), custom_call_target="tpu_custom_call" | custom-call | tf_op jit(solution)/shard_map/first_kernel/pallas_call | solution.py:315
  24.0 0.0 collective-permute-done.2.refs_6_
  24.0 0.4 %collective-permute-start.14 = (bf16[32,2176]{1,0:T(8,128)(2,1)S(1)}, bf16[32,2176]{1,0:T(8,128)(2,1)S(1)}, u32[]{:S(2)}, u32[]{:S(2)}) collective-permute-start(bf16[32,2176]{1,0:T(8,128)(2,1)S(1)} %collective-permute-done.2.refs_6_), channel_id=1, source_target_pairs={{0,1},{1,0},{2,3},{3,2},{4,5},{5,4},{6,7},{7,6},{8,9},{9,8},{10,11... | collective-permute-start | bytes 417800 | tf_op jit(solution)/shard_map/ppermute | solution.py:312
  24.5 0.9 %early_kernel.1 = (bf16[192,32]{1,0:T(8,128)(2,1)S(1)}, f32[32,768]{1,0:T(8,128)S(1)}, f32[32,2048]{1,0:T(8,128)S(1)}) custom-call(bf16[192,2048]{1,0:T(8,128)(2,1)S(1)} %get-tuple-element.51.scaled_ref, bf16[192,32]{1,0:T(8,128)(2,1)S(1)} %get-tuple-element.52.low_ref, bf16[384,768]{1,0:T(8,128)(2,1)S(1)} %get-tuple-element.44.hidden.hidden_ref, ...), custom_call_target="tpu_custom_call" | custom-call | tf_op jit(solution)/shard_map/early_kernel/pallas_call | solution.py:315
  25.4 0.0 collective-permute-done.10.refs_1_
  25.4 0.0 collective-permute-done.13.refs_5_
  25.4 0.0 collective-permute-done.12.refs_3_
  25.4 0.0 collective-permute-done.14.refs_7_
  25.5 0.7 %combine_kernel.1 = (bf16[192,2048]{1,0:T(8,128)(2,1)S(1)}, f32[16,128]{1,0:T(8,128)S(1)}) custom-call(bf16[32,2176]{1,0:T(8,128)(2,1)S(1)} %collective-permute-done.refs_0_, bf16[32,2176]{1,0:T(8,128)(2,1)S(1)} %collective-permute-done.10.refs_1_, bf16[32,2176]{1,0:T(8,128)(2,1)S(1)} %collective-permute-done.11.refs_2_, ...), custom_call_target="tpu_custom_call" | custom-call | tf_op jit(solution)/shard_map/combine_kernel/pallas_call | solution.py:315
  26.2 2.5 %collective-permute-start.15 = (f32[16,128]{1,0:T(8,128)S(1)}, f32[16,128]{1,0:T(8,128)S(1)}, u32[]{:S(2)}, u32[]{:S(2)}) collective-permute-start(f32[16,128]{1,0:T(8,128)S(1)} %get-tuple-element.59), channel_id=1, source_target_pairs={{0,12},{1,13},{2,14},{3,15},{4,8},{5,9},{6,10},{7,11},{8,4},{9,5},... | collective-permute-start | bytes 24584 | tf_op jit(solution)/shard_map/ppermute | solution.py:312
  28.7 0.0 collective-permute-start.16
  28.7 1.9 %collective-permute-start.17 = (f32[16,128]{1,0:T(8,128)S(1)}, f32[16,128]{1,0:T(8,128)S(1)}, u32[]{:S(2)}, u32[]{:S(2)}) collective-permute-start(f32[16,128]{1,0:T(8,128)S(1)} %get-tuple-element.59), channel_id=1, source_target_pairs={{0,4},{1,5},{2,6},{3,7},{4,0},{5,1},{6,2},{7,3},{8,12},{9,13},{10,... | collective-permute-start | bytes 24584 | tf_op jit(solution)/shard_map/ppermute | solution.py:312
  30.6 2.0 %late_kernel.1 = (bf16[192,768]{1,0:T(8,128)(2,1)S(1)}, f32[32,768]{1,0:T(8,128)}, f32[32,2048]{1,0:T(8,128)}) custom-call(bf16[192,2048]{1,0:T(8,128)(2,1)S(1)} %get-tuple-element.60.scaled_ref, bf16[192,32]{1,0:T(8,128)(2,1)S(1)} %get-tuple-element.61.low_ref, bf16[384,768]{1,0:T(8,128)(2,1)S(1)} %get-tuple-element.44.hidden.hidden_ref, ...), custom_call_target="tpu_custom_call" | custom-call | tf_op jit(solution)/shard_map/late_kernel/pallas_call | solution.py:315
  32.6 0.0 collective-permute-done.15
  32.6 0.6 %collective-permute-done.16 = f32[16,128]{1,0:T(8,128)S(1)} collective-permute-done((f32[16,128]{1,0:T(8,128)S(1)}, f32[16,128]{1,0:T(8,128)S(1)}, u32[]{:S(2)}, u32[]{:S(2)}) %collective-permute-start.16) | collective-permute-done | bytes 8224 | tf_op jit(solution)/shard_map/ppermute | solution.py:312
  33.3 0.0 collective-permute-done.17
  33.3 0.1 select_select_fusion
  33.3 0.0 collective-permute-start.18
  33.4 1.3 %collective-permute-start.19 = (f32[16,128]{1,0:T(8,128)S(1)}, f32[16,128]{1,0:T(8,128)S(1)}, u32[]{:S(2)}, u32[]{:S(2)}) collective-permute-start(f32[16,128]{1,0:T(8,128)S(1)} %select_select_fusion), channel_id=1, source_target_pairs={{0,2},{1,3},{2,0},{3,1},{4,6},{5,7},{6,4},{7,5},{8,10},{9,11},{10,... | collective-permute-start | bytes 24584 | tf_op jit(solution)/shard_map/ppermute | solution.py:312
  34.7 0.5 %collective-permute-start.20 = (f32[16,128]{1,0:T(8,128)S(1)}, f32[16,128]{1,0:T(8,128)S(1)}, u32[]{:S(2)}, u32[]{:S(2)}) collective-permute-start(f32[16,128]{1,0:T(8,128)S(1)} %select_select_fusion), channel_id=1, source_target_pairs={{0,1},{1,0},{2,3},{3,2},{4,5},{5,4},{6,7},{7,6},{8,9},{9,8},{10,11... | collective-permute-start | bytes 24584 | tf_op jit(solution)/shard_map/ppermute | solution.py:312
  35.2 1.9 %cotangent_kernel.1 = bf16[384,768]{1,0:T(8,128)(2,1)} custom-call(bf16[192,2048]{1,0:T(8,128)(2,1)S(1)} %get-tuple-element.51.scaled_ref, bf16[192,32]{1,0:T(8,128)(2,1)S(1)} %get-tuple-element.53.lowered_ref, bf16[768,2048]{1,0:T(8,128)(2,1)S(1)} %get-tuple-element.45.down.down_ref, bf16[32,768]{1,0:T(8,128)(2,1)S(1)} %get-tuple-element.46.first.first_ref, ...), custom_call_target="tpu_custom_call" | custom-call | tf_op jit(solution)/shard_map/cotangent_kernel/pallas_call | solution.py:315
  37.1 0.0 collective-permute-done.18
  37.1 0.0 collective-permute-done.19
  37.1 0.0 collective-permute-done.20
  37.1 0.1 slice_select_fusion
  37.2 0.6 %select_reduce_fusion = f32[8,32]{1,0:T(8,128)} fusion(f32[16,32]{1,0:T(8,128)S(1)} %slice_select_fusion, s32[8,32]{1,0:T(8,128)S(1)} %get-tuple-element.70), kind=kLoop, calls=%fused_computation | loop fusion | flops 12032 | bytes 4096 | tf_op jit(solution)/shard_map/reduce_sum | solution.py:462
  (4 shorter events, 0.0 us)
Async XLA Ops:
  1.6 9.3 %collective-permute-start.6 = (bf16[32,2176]{1,0:T(8,128)(2,1)S(1)}, bf16[32,2176]{1,0:T(8,128)(2,1)S(1)}, u32[]{:S(2)}, u32[]{:S(2)}) collective-permute-start(bf16[32,2176]{1,0:T(8,128)(2,1)S(1)} %get-tuple-element.38.refs_0_), channel_id=1, source_target_pairs={{0,4},{1,5},{2,6},{3,7},{4,0},{5,1},{6,2},{7,3},{8,12},{9,13},{10,... | collective-permute-start | bytes 417800 | tf_op jit(solution)/shard_map/ppermute | solution.py:312
  4.7 9.1 %collective-permute-start = (bf16[32,2176]{1,0:T(8,128)(2,1)S(1)}, bf16[32,2176]{1,0:T(8,128)(2,1)S(1)}, u32[]{:S(2)}, u32[]{:S(2)}) collective-permute-start(bf16[32,2176]{1,0:T(8,128)(2,1)S(1)} %get-tuple-element.38.refs_0_), channel_id=1, source_target_pairs={{0,8},{1,9},{2,10},{3,11},{4,12},{5,13},{6,14},{7,15},{8,0},{9,1},... | collective-permute-start | bytes 417800 | tf_op jit(solution)/shard_map/ppermute | solution.py:312
  7.3 6.9 %collective-permute-start.4 = (bf16[32,2176]{1,0:T(8,128)(2,1)S(1)}, bf16[32,2176]{1,0:T(8,128)(2,1)S(1)}, u32[]{:S(2)}, u32[]{:S(2)}) collective-permute-start(bf16[32,2176]{1,0:T(8,128)(2,1)S(1)} %get-tuple-element.38.refs_0_), channel_id=1, source_target_pairs={{0,2},{1,3},{2,0},{3,1},{4,6},{5,7},{6,4},{7,5},{8,10},{9,11},{10,... | collective-permute-start | bytes 417800 | tf_op jit(solution)/shard_map/ppermute | solution.py:312
  8.8 6.0 %collective-permute-start.3 = (bf16[32,2176]{1,0:T(8,128)(2,1)S(1)}, bf16[32,2176]{1,0:T(8,128)(2,1)S(1)}, u32[]{:S(2)}, u32[]{:S(2)}) collective-permute-start(bf16[32,2176]{1,0:T(8,128)(2,1)S(1)} %get-tuple-element.38.refs_0_), channel_id=1, source_target_pairs={{0,1},{1,0},{2,3},{3,2},{4,5},{5,4},{6,7},{7,6},{8,9},{9,8},{10,11... | collective-permute-start | bytes 417800 | tf_op jit(solution)/shard_map/ppermute | solution.py:312
  10.9 6.2 %collective-permute-start.8 = (bf16[32,2176]{1,0:T(8,128)(2,1)S(1)}, bf16[32,2176]{1,0:T(8,128)(2,1)S(1)}, u32[]{:S(2)}, u32[]{:S(2)}) collective-permute-start(bf16[32,2176]{1,0:T(8,128)(2,1)S(1)} %collective-permute-done.6.refs_4_), channel_id=1, source_target_pairs={{0,2},{1,3},{2,0},{3,1},{4,6},{5,7},{6,4},{7,5},{8,10},{9,11},{10,... | collective-permute-start | bytes 417800 | tf_op jit(solution)/shard_map/ppermute | solution.py:312
  13.8 5.1 %collective-permute-start.1 = (bf16[32,2176]{1,0:T(8,128)(2,1)S(1)}, bf16[32,2176]{1,0:T(8,128)(2,1)S(1)}, u32[]{:S(2)}, u32[]{:S(2)}) collective-permute-start(bf16[32,2176]{1,0:T(8,128)(2,1)S(1)} %collective-permute-done.refs_0_), channel_id=1, source_target_pairs={{0,4},{1,5},{2,6},{3,7},{4,0},{5,1},{6,2},{7,3},{8,12},{9,13},{10,... | collective-permute-start | bytes 417800 | tf_op jit(solution)/shard_map/ppermute | solution.py:312
  14.2 8.4 %collective-permute-start.7 = (bf16[32,2176]{1,0:T(8,128)(2,1)S(1)}, bf16[32,2176]{1,0:T(8,128)(2,1)S(1)}, u32[]{:S(2)}, u32[]{:S(2)}) collective-permute-start(bf16[32,2176]{1,0:T(8,128)(2,1)S(1)} %collective-permute-done.6.refs_4_), channel_id=1, source_target_pairs={{0,1},{1,0},{2,3},{3,2},{4,5},{5,4},{6,7},{7,6},{8,9},{9,8},{10,11... | collective-permute-start | bytes 417800 | tf_op jit(solution)/shard_map/ppermute | solution.py:312
  14.2 8.5 %collective-permute-start.5 = (bf16[32,2176]{1,0:T(8,128)(2,1)S(1)}, bf16[32,2176]{1,0:T(8,128)(2,1)S(1)}, u32[]{:S(2)}, u32[]{:S(2)}) collective-permute-start(bf16[32,2176]{1,0:T(8,128)(2,1)S(1)} %collective-permute-done.4.refs_2_), channel_id=1, source_target_pairs={{0,1},{1,0},{2,3},{3,2},{4,5},{5,4},{6,7},{7,6},{8,9},{9,8},{10,11... | collective-permute-start | bytes 417800 | tf_op jit(solution)/shard_map/ppermute | solution.py:312
  14.7 8.5 %collective-permute-start.11 = (bf16[32,2176]{1,0:T(8,128)(2,1)S(1)}, bf16[32,2176]{1,0:T(8,128)(2,1)S(1)}, u32[]{:S(2)}, u32[]{:S(2)}) collective-permute-start(bf16[32,2176]{1,0:T(8,128)(2,1)S(1)} %collective-permute-done.refs_0_), channel_id=1, source_target_pairs={{0,2},{1,3},{2,0},{3,1},{4,6},{5,7},{6,4},{7,5},{8,10},{9,11},{10,... | collective-permute-start | bytes 417800 | tf_op jit(solution)/shard_map/ppermute | solution.py:312
  17.0 6.2 %collective-permute-start.9 = (bf16[32,2176]{1,0:T(8,128)(2,1)S(1)}, bf16[32,2176]{1,0:T(8,128)(2,1)S(1)}, u32[]{:S(2)}, u32[]{:S(2)}) collective-permute-start(bf16[32,2176]{1,0:T(8,128)(2,1)S(1)} %collective-permute-done.8.refs_6_), channel_id=1, source_target_pairs={{0,1},{1,0},{2,3},{3,2},{4,5},{5,4},{6,7},{7,6},{8,9},{9,8},{10,11... | collective-permute-start | bytes 417800 | tf_op jit(solution)/shard_map/ppermute | solution.py:312
  18.8 5.2 %collective-permute-start.2 = (bf16[32,2176]{1,0:T(8,128)(2,1)S(1)}, bf16[32,2176]{1,0:T(8,128)(2,1)S(1)}, u32[]{:S(2)}, u32[]{:S(2)}) collective-permute-start(bf16[32,2176]{1,0:T(8,128)(2,1)S(1)} %collective-permute-done.1.refs_4_), channel_id=1, source_target_pairs={{0,2},{1,3},{2,0},{3,1},{4,6},{5,7},{6,4},{7,5},{8,10},{9,11},{10,... | collective-permute-start | bytes 417800 | tf_op jit(solution)/shard_map/ppermute | solution.py:312
  22.6 2.8 %collective-permute-start.10 = (bf16[32,2176]{1,0:T(8,128)(2,1)S(1)}, bf16[32,2176]{1,0:T(8,128)(2,1)S(1)}, u32[]{:S(2)}, u32[]{:S(2)}) collective-permute-start(bf16[32,2176]{1,0:T(8,128)(2,1)S(1)} %collective-permute-done.refs_0_), channel_id=1, source_target_pairs={{0,1},{1,0},{2,3},{3,2},{4,5},{5,4},{6,7},{7,6},{8,9},{9,8},{10,11... | collective-permute-start | bytes 417800 | tf_op jit(solution)/shard_map/ppermute | solution.py:312
  22.7 2.7 %collective-permute-start.13 = (bf16[32,2176]{1,0:T(8,128)(2,1)S(1)}, bf16[32,2176]{1,0:T(8,128)(2,1)S(1)}, u32[]{:S(2)}, u32[]{:S(2)}) collective-permute-start(bf16[32,2176]{1,0:T(8,128)(2,1)S(1)} %collective-permute-done.1.refs_4_), channel_id=1, source_target_pairs={{0,1},{1,0},{2,3},{3,2},{4,5},{5,4},{6,7},{7,6},{8,9},{9,8},{10,11... | collective-permute-start | bytes 417800 | tf_op jit(solution)/shard_map/ppermute | solution.py:312
  23.2 2.2 %collective-permute-start.12 = (bf16[32,2176]{1,0:T(8,128)(2,1)S(1)}, bf16[32,2176]{1,0:T(8,128)(2,1)S(1)}, u32[]{:S(2)}, u32[]{:S(2)}) collective-permute-start(bf16[32,2176]{1,0:T(8,128)(2,1)S(1)} %collective-permute-done.11.refs_2_), channel_id=1, source_target_pairs={{0,1},{1,0},{2,3},{3,2},{4,5},{5,4},{6,7},{7,6},{8,9},{9,8},{10,11... | collective-permute-start | bytes 417800 | tf_op jit(solution)/shard_map/ppermute | solution.py:312
  24.0 1.4 %collective-permute-start.14 = (bf16[32,2176]{1,0:T(8,128)(2,1)S(1)}, bf16[32,2176]{1,0:T(8,128)(2,1)S(1)}, u32[]{:S(2)}, u32[]{:S(2)}) collective-permute-start(bf16[32,2176]{1,0:T(8,128)(2,1)S(1)} %collective-permute-done.2.refs_6_), channel_id=1, source_target_pairs={{0,1},{1,0},{2,3},{3,2},{4,5},{5,4},{6,7},{7,6},{8,9},{9,8},{10,11... | collective-permute-start | bytes 417800 | tf_op jit(solution)/shard_map/ppermute | solution.py:312
  26.2 6.4 %collective-permute-start.15 = (f32[16,128]{1,0:T(8,128)S(1)}, f32[16,128]{1,0:T(8,128)S(1)}, u32[]{:S(2)}, u32[]{:S(2)}) collective-permute-start(f32[16,128]{1,0:T(8,128)S(1)} %get-tuple-element.59), channel_id=1, source_target_pairs={{0,12},{1,13},{2,14},{3,15},{4,8},{5,9},{6,10},{7,11},{8,4},{9,5},... | collective-permute-start | bytes 24584 | tf_op jit(solution)/shard_map/ppermute | solution.py:312
  28.7 4.5 %collective-permute-start.16 = (f32[16,128]{1,0:T(8,128)S(1)}, f32[16,128]{1,0:T(8,128)S(1)}, u32[]{:S(2)}, u32[]{:S(2)}) collective-permute-start(f32[16,128]{1,0:T(8,128)S(1)} %get-tuple-element.59), channel_id=1, source_target_pairs={{0,8},{1,9},{2,10},{3,11},{4,12},{5,13},{6,14},{7,15},{8,0},{9,1},... | collective-permute-start | bytes 24584 | tf_op jit(solution)/shard_map/ppermute | solution.py:312
  28.7 4.5 %collective-permute-start.17 = (f32[16,128]{1,0:T(8,128)S(1)}, f32[16,128]{1,0:T(8,128)S(1)}, u32[]{:S(2)}, u32[]{:S(2)}) collective-permute-start(f32[16,128]{1,0:T(8,128)S(1)} %get-tuple-element.59), channel_id=1, source_target_pairs={{0,4},{1,5},{2,6},{3,7},{4,0},{5,1},{6,2},{7,3},{8,12},{9,13},{10,... | collective-permute-start | bytes 24584 | tf_op jit(solution)/shard_map/ppermute | solution.py:312
  33.3 3.8 %collective-permute-start.18 = (f32[16,128]{1,0:T(8,128)S(1)}, f32[16,128]{1,0:T(8,128)S(1)}, u32[]{:S(2)}, u32[]{:S(2)}) collective-permute-start(f32[16,128]{1,0:T(8,128)S(1)} %select_select_fusion), channel_id=1, source_target_pairs={{0,3},{1,2},{2,1},{3,0},{4,7},{5,6},{6,5},{7,4},{8,11},{9,10},{10,... | collective-permute-start | bytes 24584 | tf_op jit(solution)/shard_map/ppermute | solution.py:312
  33.4 3.8 %collective-permute-start.19 = (f32[16,128]{1,0:T(8,128)S(1)}, f32[16,128]{1,0:T(8,128)S(1)}, u32[]{:S(2)}, u32[]{:S(2)}) collective-permute-start(f32[16,128]{1,0:T(8,128)S(1)} %select_select_fusion), channel_id=1, source_target_pairs={{0,2},{1,3},{2,0},{3,1},{4,6},{5,7},{6,4},{7,5},{8,10},{9,11},{10,... | collective-permute-start | bytes 24584 | tf_op jit(solution)/shard_map/ppermute | solution.py:312
  34.7 2.5 %collective-permute-start.20 = (f32[16,128]{1,0:T(8,128)S(1)}, f32[16,128]{1,0:T(8,128)S(1)}, u32[]{:S(2)}, u32[]{:S(2)}) collective-permute-start(f32[16,128]{1,0:T(8,128)S(1)} %select_select_fusion), channel_id=1, source_target_pairs={{0,1},{1,0},{2,3},{3,2},{4,5},{5,4},{6,7},{7,6},{8,9},{9,8},{10,11... | collective-permute-start | bytes 24584 | tf_op jit(solution)/shard_map/ppermute | solution.py:312
